TPU v7x, 32 devices: a whole 2x2x4 slice. The times are simulated.
32 devices in a mesh: dp: 8 (over y, x, core), ctx: 4 (over z).
Axes of the slice: x: 2, y: 2, z: 4, core: 2. Of those that a mesh axis runs over, the one named last changes fastest.
Arguments:
- input_gate: bfloat16 [512, 131072], P('dp', 'ctx'), may hold values from -6 to 6
- output_gate: bfloat16 [512, 131072], P('dp', 'ctx'), may hold values from -6 to 6
- values: bfloat16 [512, 131072], P('dp', 'ctx'), may hold values from -6 to 6
- cotangent: bfloat16 [512, 131072], P('dp', 'ctx'), may hold values from -6 to 6
- filter_raw: bfloat16 [16, 131072], P(None, 'ctx'), may hold values from -6 to 6
- filter_decay: float32 [16], replicated, may hold values from 0.25 to 2
- skip_gain: float32 [512], P('dp'), may hold values from -4 to 4
Outputs:
- outputs: bfloat16 [512, 131072], P('dp', 'ctx')
- grad_input_gate: bfloat16 [512, 131072], P('dp', 'ctx')
- grad_output_gate: bfloat16 [512, 131072], P('dp', 'ctx')
- grad_values: bfloat16 [512, 131072], P('dp', 'ctx')
- grad_filter: float32 [16, 131072], P(None, 'ctx')
All inputs are finite; a program needn't handle non-finite values.
Results may differ from a plain program's by a relative error of at most 0.018.
Values may be sent and summed in bfloat16 or wider, within the bound.
No kernel may reach another device: no remote copies, remote signals or barrier semaphores. Data moves between devices by JAX's collectives and lax.ppermute only.
A program may use at most 256 MiB of HBM per device.

v0:
```python
import math

import jax
import jax.numpy as jnp
import ml_dtypes
import numpy as np
from jax import lax
from jax.experimental import pallas as pl
from jax.experimental.pallas import tpu as pltpu
from jax.sharding import PartitionSpec as P

N1 = 512
N2 = 512
FFT_LEN = 262144


two_pi = 2.0 * math.pi


def first_tables(row_total):
    first_index = jnp.arange(N1, dtype=jnp.int32)
    source_rows = jnp.arange(row_total, dtype=jnp.int32)
    angles = (first_index[:, None] * source_rows[None, :] % N1).astype(jnp.float32) * (two_pi / N1)
    cosine = jnp.cos(angles).astype(jnp.bfloat16)
    minus_sine = (-jnp.sin(angles)).astype(jnp.bfloat16)
    forward_table = jnp.concatenate([cosine, minus_sine], axis=0)
    inverse_table = jnp.stack([cosine.T, minus_sine.T], axis=2)
    return (forward_table, inverse_table)


def second_tables():
    second_index = jnp.arange(N2, dtype=jnp.int32)
    angles = (second_index[:, None] * second_index[None, :] % N2).astype(jnp.float32) * (
        two_pi / N2
    )
    cosine = jnp.cos(angles).astype(jnp.bfloat16)
    minus_sine = (-jnp.sin(angles)).astype(jnp.bfloat16)
    forward_table = jnp.stack(
        [
            jnp.concatenate([cosine, minus_sine], axis=1),
            jnp.concatenate([-minus_sine, cosine], axis=1),
        ],
        axis=0,
    )
    inverse_table = jnp.concatenate(
        [
            jnp.concatenate([cosine, -minus_sine], axis=1),
            jnp.concatenate([minus_sine, cosine], axis=1),
        ],
        axis=0,
    )
    return (forward_table, inverse_table)


def twiddle_table(spectrum_rows, columns):
    angles = (spectrum_rows[:, None] * columns[None, :] % FFT_LEN).astype(jnp.float32) * (
        two_pi / FFT_LEN
    )
    return (jnp.cos(angles), -jnp.sin(angles))


def halves(array):
    return (array[..., :N2], array[..., N2:])


def joined(real_part, imaginary_part):
    return jnp.concatenate([real_part, imaginary_part], axis=-1).astype(jnp.bfloat16)


def spectral_products(mix_spec, weight_spec, filter_spec, which):
    lead = mix_spec.shape[:-2]
    filters = filter_spec.shape[-2]
    filter_real, filter_imaginary = halves(filter_spec.astype(jnp.float32))
    filter_real = jnp.expand_dims(filter_real, -3)
    filter_imaginary = jnp.expand_dims(filter_imaginary, -3)
    outcome = []
    mix_real, mix_imaginary = halves(mix_spec.reshape(lead + (-1, filters, 2 * N2)))
    weight_real, weight_imaginary = halves(weight_spec.reshape(lead + (-1, filters, 2 * N2)))
    for name in which:
        if name == "convolve":
            made = joined(
                mix_real * filter_real - mix_imaginary * filter_imaginary,
                mix_real * filter_imaginary + mix_imaginary * filter_real,
            )
        elif name == "correlate":
            made = joined(
                filter_real * weight_real + filter_imaginary * weight_imaginary,
                filter_real * weight_imaginary - filter_imaginary * weight_real,
            )
        else:
            made = joined(
                mix_real * weight_real + mix_imaginary * weight_imaginary,
                mix_real * weight_imaginary - mix_imaginary * weight_real,
            )
        outcome.append(made.reshape(lead + (-1, 2 * N2)))
    return outcome


def shards(input_gate, output_gate, values, cotangent, filter_raw, filter_decay, skip_gain):
    context_size = lax.axis_size("ctx")
    context_index = lax.axis_index("ctx")
    channels, local_len = input_gate.shape
    filters = filter_raw.shape[0]
    groups = channels // filters
    row_local = local_len // N2
    row_total = row_local * context_size
    seq_len = local_len * context_size
    first_forward, first_inverse = first_tables(row_total)
    second_forward, second_inverse = second_tables()
    inverse_scale = 1.0 / FFT_LEN
    mixed_input = (input_gate.astype(jnp.float32) * values.astype(jnp.float32)).astype(jnp.bfloat16)
    weighted = (cotangent.astype(jnp.float32) * output_gate.astype(jnp.float32)).astype(
        jnp.bfloat16
    )
    global_positions = (context_index * local_len + jnp.arange(local_len, dtype=jnp.int32)).astype(
        jnp.float32
    )
    envelope = jnp.exp(-filter_decay[:, None] * (global_positions[None, :] / seq_len))
    filter_scale = seq_len ** (-0.5)
    filter_taps = (filter_raw.astype(jnp.float32) * envelope * filter_scale).astype(jnp.bfloat16)
    spread_count = filters // context_size
    full_real, full_imaginary = twiddle_table(
        jnp.arange(N1, dtype=jnp.int32), jnp.arange(N2, dtype=jnp.int32)
    )
    pair = jnp.stack([mixed_input, weighted], axis=0).reshape(2, groups, filters, row_local, N2)
    taps_block = filter_taps.reshape(1, 1, filters, row_local, N2)
    pair_whole, taps_whole = (
        lax.all_to_all(pair, "ctx", split_axis=2, concat_axis=3, tiled=True),
        lax.all_to_all(taps_block, "ctx", split_axis=2, concat_axis=3, tiled=True),
    )
    signal_count = 2 * groups * spread_count
    every = jnp.concatenate(
        [
            pair_whole.reshape(signal_count, row_total, N2),
            taps_whole.reshape(spread_count, row_total, N2),
        ],
        axis=0,
    )
    first = jnp.einsum("km,imn->ikn", first_forward, every, preferred_element_type=jnp.float32)
    first_real = first[:, :N1]
    first_imaginary = first[:, N1:]
    turned = jnp.stack(
        [
            first_real * full_real - first_imaginary * full_imaginary,
            first_real * full_imaginary + first_imaginary * full_real,
        ],
        axis=1,
    ).astype(jnp.bfloat16)
    spectra = jnp.einsum(
        "ipkn,pnl->ikl", turned, second_forward, preferred_element_type=jnp.float32
    )
    signal_spec = spectra[:signal_count].reshape(2, groups * spread_count, N1, 2 * N2)
    filter_spec = spectra[signal_count:].astype(jnp.bfloat16)
    filter_spec = jnp.transpose(filter_spec, (1, 0, 2))
    mix_spec = jnp.transpose(signal_spec[0], (1, 0, 2))
    weight_spec = jnp.transpose(signal_spec[1], (1, 0, 2))
    made = spectral_products(mix_spec, weight_spec, filter_spec, ["convolve", "correlate", "lag"])
    stacked = jnp.transpose(jnp.concatenate(made, axis=1), (1, 0, 2))
    back = jnp.einsum("ikl,lm->ikm", stacked, second_inverse, preferred_element_type=jnp.float32)
    back_real, back_imaginary = halves(back)
    rotated = jnp.stack(
        [
            (back_real * full_real + back_imaginary * full_imaginary) * inverse_scale,
            (back_imaginary * full_real - back_real * full_imaginary) * inverse_scale,
        ],
        axis=1,
    ).astype(jnp.bfloat16)
    inverted = jnp.einsum(
        "mkp,ipkn->imn", first_inverse, rotated, preferred_element_type=jnp.float32
    )
    inverted = inverted.astype(jnp.bfloat16).reshape(3, groups, spread_count, row_total, N2)
    back_rows = lax.all_to_all(inverted[:2], "ctx", split_axis=3, concat_axis=2, tiled=True)
    convolved = back_rows[0].reshape(channels, local_len)
    correlated = back_rows[1].reshape(channels, local_len)
    lag_whole = jnp.sum(inverted[2].astype(jnp.float32), axis=0)
    lag_part = (
        lax.all_to_all(
            lag_whole.astype(jnp.bfloat16), "ctx", split_axis=1, concat_axis=0, tiled=True
        )
        .astype(lag_whole.dtype)
        .reshape(filters, local_len)
    )
    summed = convolved.astype(jnp.float32) + skip_gain[:, None] * mixed_input.astype(jnp.float32)
    outputs = (output_gate.astype(jnp.float32) * summed).astype(jnp.bfloat16)
    grad_output_gate = (cotangent.astype(jnp.float32) * summed).astype(jnp.bfloat16)
    back_total = correlated.astype(jnp.float32) + skip_gain[:, None] * weighted.astype(jnp.float32)
    grad_input_gate = (back_total * values.astype(jnp.float32)).astype(jnp.bfloat16)
    grad_values = (back_total * input_gate.astype(jnp.float32)).astype(jnp.bfloat16)
    lag_total = lax.psum(lag_part.astype(jnp.bfloat16), "dp").astype(jnp.float32)
    grad_filter = lag_total * envelope * filter_scale
    return (outputs, grad_input_gate, grad_output_gate, grad_values, grad_filter)


LANES = 128
SHARES = (6, 5, 3, 2)
STRIP = 16
EDGE_ROWS = 16


def block_tables(rows):
    length = 2 * rows * LANES
    k = np.arange(rows)
    m = np.arange(rows)
    n = np.arange(LANES)
    first = np.exp(-1j * np.pi * (np.outer(2 * k + 1, m) % (4 * rows)) / (2 * rows))
    turn = np.exp(-1j * np.pi * (np.outer(2 * k + 1, n) % (2 * length)) / length)
    second = np.exp(-2j * np.pi * (np.outer(n, n) % LANES) / LANES)
    first_forward = np.concatenate([first.real, first.imag], axis=0)
    first_inverse = np.concatenate([first.real.T, first.imag.T], axis=1)
    second_forward = np.block([[second.real, second.imag], [-second.imag, second.real]])
    second_inverse = np.block([[second.real, -second.imag], [second.imag, second.real]])
    half = ml_dtypes.bfloat16
    turns = np.stack([turn.real, turn.imag]).astype(np.float32)
    return tuple(
        jnp.asarray(table)
        for table in (
            first_forward.astype(half),
            second_forward.astype(half),
            second_inverse.astype(half),
            first_inverse.astype(half),
            turns,
            (turns * np.float32(2.0 / length)),
        )
    )


def block_kernel(
    side_ref,
    own_ref,
    far_ref,
    other_own_ref,
    other_next_ref,
    other_far_ref,
    taps_ref,
    first_forward_ref,
    second_forward_ref,
    second_inverse_ref,
    first_inverse_ref,
    turn_ref,
    back_turn_ref,
    near_out_ref,
    other_out_ref,
    passed_out_ref,
    lag_out_ref,
    spectra,
    products,
):
    groups, _, rows, lanes = own_ref.shape
    side = side_ref[0]
    signals = (own_ref, far_ref, other_own_ref, other_next_ref, other_far_ref, taps_ref)
    for number, signal in enumerate(signals):
        for pair in range(signal.shape[0] // 2):
            both = jnp.concatenate([signal[2 * pair, 0], signal[2 * pair + 1, 0]], axis=1)
            first = jnp.dot(first_forward_ref[...], both, preferred_element_type=jnp.float32)
            for which in range(2):
                real = first[:rows, which * lanes : (which + 1) * lanes]
                imaginary = first[rows:, which * lanes : (which + 1) * lanes]
                turned = jnp.concatenate(
                    [
                        real * turn_ref[0] - imaginary * turn_ref[1],
                        real * turn_ref[1] + imaginary * turn_ref[0],
                    ],
                    axis=1,
                ).astype(jnp.bfloat16)
                spectra[number, 2 * pair + which] = jnp.dot(
                    turned, second_forward_ref[...], preferred_element_type=jnp.float32
                )

    row_index = lax.broadcasted_iota(jnp.int32, (STRIP, lanes), 0)
    parity = 1.0 - 2.0 * (row_index % 2).astype(jnp.float32)

    def strip(step, carry):
        at = pl.ds(pl.multiple_of(step * STRIP, STRIP), STRIP)

        def load(number, which):
            return spectra[number, which, at, :lanes], spectra[number, which, at, lanes:]

        def store(number, real, imaginary):
            products[number, at, :lanes] = real.astype(jnp.bfloat16)
            products[number, at, lanes:] = imaginary.astype(jnp.bfloat16)

        filters = [load(5, delay) for delay in range(4)]
        gains = []
        for delay in range(4):
            real, imaginary = filters[delay]
            if delay:
                before_real, before_imaginary = filters[delay - 1]
                real = real - parity * before_imaginary
                imaginary = imaginary + parity * before_real
            gains.append((real, side * imaginary))
        lag = [(jnp.zeros((STRIP, lanes), jnp.float32),) * 2 for _ in range(4)]

        def times(total, left, right):
            real = left[0] * right[0] - left[1] * right[1]
            imaginary = left[0] * right[1] + left[1] * right[0]
            return (real, imaginary) if total is None else (total[0] + real, total[1] + imaginary)

        def conjugate_times(total, left, right):
            real = left[0] * right[0] + left[1] * right[1]
            imaginary = left[0] * right[1] - left[1] * right[0]
            return (real, imaginary) if total is None else (total[0] + real, total[1] + imaginary)

        for group in range(groups):
            own, far = load(0, group), load(1, group)
            near = times(times(None, gains[0], own), gains[1], far)
            store(group, *near)
            other_own, other_next, other_far = load(2, group), load(3, group), load(4, group)
            other = conjugate_times(None, gains[0], other_own)
            other = conjugate_times(other, gains[1], other_next)
            other = conjugate_times(other, gains[2], other_far)
            store(groups + group, *other)
            passed = conjugate_times(None, gains[1], other_own)
            passed = conjugate_times(passed, gains[2], other_next)
            passed = conjugate_times(passed, gains[3], other_far)
            store(2 * groups + group, *passed)
            half_own = (0.5 * own[0], 0.5 * own[1])
            lag[0] = conjugate_times(lag[0], own, other_own)
            lag[1] = conjugate_times(lag[1], far, other_own)
            lag[1] = conjugate_times(lag[1], half_own, other_next)
            lag[2] = conjugate_times(lag[2], far, other_next)
            lag[3] = conjugate_times(lag[3], far, other_far)
        lag[3] = (0.5 * lag[3][0], 0.5 * lag[3][1])
        for delay in range(4):
            real, imaginary = lag[delay][0], side * lag[delay][1]
            if delay < 3:
                real = real + parity * (side * lag[delay + 1][1])
                imaginary = imaginary - parity * lag[delay + 1][0]
            store(3 * groups + delay, real, imaginary)
        return carry

    lax.fori_loop(0, rows // STRIP, strip, 0)

    shares = lag_out_ref.shape[0]
    for kind, out_ref in enumerate((near_out_ref, other_out_ref, passed_out_ref, None)):
        for pair in range((groups if kind < 3 else 4) // 2):
            real_parts, imaginary_parts = [], []
            for which in range(2):
                back = jnp.dot(
                    products[kind * groups + 2 * pair + which],
                    second_inverse_ref[...],
                    preferred_element_type=jnp.float32,
                )
                real, imaginary = back[:, :lanes], back[:, lanes:]
                real_parts.append(
                    (real * back_turn_ref[0] + imaginary * back_turn_ref[1]).astype(jnp.bfloat16)
                )
                imaginary_parts.append(
                    (imaginary * back_turn_ref[0] - real * back_turn_ref[1]).astype(jnp.bfloat16)
                )
            rotated = jnp.concatenate(
                [jnp.concatenate(real_parts, axis=1), jnp.concatenate(imaginary_parts, axis=1)],
                axis=0,
            )
            result = jnp.dot(first_inverse_ref[...], rotated, preferred_element_type=jnp.float32)
            result = result.astype(jnp.bfloat16)
            for which in range(2):
                column = result[:, which * lanes : (which + 1) * lanes]
                if kind < 3:
                    out_ref[2 * pair + which, 0] = column
                else:
                    column = column.reshape(shares, rows // shares, lanes)
                    lag_out_ref[:, 2 * pair + which, 0] = column


def block_products(side, signals, other, taps, tables, start, shares):
    groups, filters, rows, lanes = signals[0].shape
    block = pl.BlockSpec((groups, 1, rows, lanes), lambda f: (0, f, 0, 0))
    other_block = pl.BlockSpec((groups, 1, rows, lanes), lambda f: (0, f + start, 0, 0))
    taps_block = pl.BlockSpec((4, 1, rows, lanes), lambda f: (0, f + start, 0, 0))
    lag_block = pl.BlockSpec((shares, 4, 1, rows // shares, lanes), lambda f: (0, 0, f, 0, 0))

    def whole(table):
        return pl.BlockSpec(table.shape, lambda f: (0,) * table.ndim)

    made = jax.ShapeDtypeStruct(signals[0].shape, jnp.bfloat16)
    lag = jax.ShapeDtypeStruct((shares, 4, filters, rows // shares, lanes), jnp.bfloat16)
    transforms = filters * (9 * groups + 8)
    own, far, other_next, other_far = signals
    return pl.pallas_call(
        block_kernel,
        grid=(filters,),
        in_specs=[pl.BlockSpec(memory_space=pltpu.SMEM)]
        + [block, block, other_block, block, block, taps_block]
        + [whole(table) for table in tables],
        out_specs=[block, block, block, lag_block],
        out_shape=[made, made, made, lag],
        scratch_shapes=[
            pltpu.VMEM((6, groups, rows, 2 * lanes), jnp.float32),
            pltpu.VMEM((3 * groups + 4, rows, 2 * lanes), jnp.bfloat16),
        ],
        compiler_params=pltpu.CompilerParams(vmem_limit_bytes=48 * 2**20),
        cost_estimate=pl.CostEstimate(
            flops=transforms * 2 * (2 * rows * rows * lanes + rows * 4 * lanes * lanes),
            bytes_accessed=filters * (8 * groups + 8) * rows * lanes * 2,
            transcendentals=0,
        ),
    )(side, own, far, other, other_next, other_far, taps, *tables)


def product(left, right):
    return (left.astype(jnp.float32) * right.astype(jnp.float32)).astype(jnp.bfloat16)


def enter_kernel(side_ref, gate_ref, values_ref, cotangent_ref, out_gate_ref, *out_refs):
    channels, width = gate_ref.shape
    *own_refs, other_ref = out_refs
    groups, filters, rows, lanes = other_ref.shape
    near_start = side_ref[0] > 0
    mixed = product(gate_ref[...], values_ref[...]).astype(jnp.float32)
    weighted = product(cotangent_ref[...], out_gate_ref[...]).astype(jnp.float32)

    def blocks(array):
        array = array.reshape(channels, rows, lanes).astype(jnp.bfloat16)
        return array.reshape(groups, filters, rows, lanes)

    own = blocks(jnp.where(near_start, mixed, weighted))
    start = 0
    for own_ref in own_refs:
        own_ref[...] = own[:, start : start + own_ref.shape[1]]
        start += own_ref.shape[1]
    other_ref[...] = blocks(jnp.where(near_start, weighted, mixed))


def enter(side, flat, filters):
    channels, local_len = flat[0].shape
    groups, rows = channels // filters, local_len // LANES
    counts = SHARES + (filters,)
    return pl.pallas_call(
        enter_kernel,
        grid=(rows // EDGE_ROWS,),
        in_specs=[pl.BlockSpec(memory_space=pltpu.SMEM)]
        + [pl.BlockSpec((channels, EDGE_ROWS * LANES), lambda i: (0, i))] * 4,
        out_specs=[
            pl.BlockSpec((groups, count, EDGE_ROWS, LANES), lambda i: (0, 0, i, 0))
            for count in counts
        ],
        out_shape=[
            jax.ShapeDtypeStruct((groups, count, rows, LANES), jnp.bfloat16) for count in counts
        ],
        compiler_params=pltpu.CompilerParams(vmem_limit_bytes=40 * 2**20),
        cost_estimate=pl.CostEstimate(
            flops=4 * channels * local_len,
            bytes_accessed=12 * channels * local_len,
            transcendentals=0,
        ),
    )(side, *flat)


def leave_kernel(side_ref, skip_ref, gate_ref, values_ref, cotangent_ref, out_gate_ref, *refs):
    channels, width = gate_ref.shape
    parts = len(SHARES)
    near_refs, other_refs = refs[:parts], refs[parts : 2 * parts]
    received_refs = refs[2 * parts : 3 * parts]
    outputs_ref, grad_gate_ref, grad_out_gate_ref, grad_values_ref = refs[3 * parts :]
    near_start = side_ref[0] > 0

    def flat(part_refs):
        whole = jnp.concatenate([ref[...] for ref in part_refs], axis=1).astype(jnp.float32)
        return whole.reshape(channels, width // LANES, LANES).reshape(channels, width)

    near = flat(near_refs)
    other = flat(other_refs) + flat(received_refs)
    skip = skip_ref[...]
    gate, values = gate_ref[...].astype(jnp.float32), values_ref[...].astype(jnp.float32)
    cotangent = cotangent_ref[...].astype(jnp.float32)
    out_gate = out_gate_ref[...].astype(jnp.float32)
    mixed = (gate * values).astype(jnp.bfloat16).astype(jnp.float32)
    weighted = (cotangent * out_gate).astype(jnp.bfloat16).astype(jnp.float32)
    summed = jnp.where(near_start, near, other) + skip * mixed
    outputs_ref[...] = (out_gate * summed).astype(jnp.bfloat16)
    grad_out_gate_ref[...] = (cotangent * summed).astype(jnp.bfloat16)
    back_total = jnp.where(near_start, other, near) + skip * weighted
    grad_gate_ref[...] = (back_total * values).astype(jnp.bfloat16)
    grad_values_ref[...] = (back_total * gate).astype(jnp.bfloat16)


def leave(side, skip_gain, flat, near_parts, other_parts, received_parts):
    channels, local_len = flat[0].shape
    parts = (*near_parts, *other_parts, *received_parts)
    flat_block = pl.BlockSpec((channels, EDGE_ROWS * LANES), lambda i: (0, i))
    return pl.pallas_call(
        leave_kernel,
        grid=(local_len // (EDGE_ROWS * LANES),),
        in_specs=[
            pl.BlockSpec(memory_space=pltpu.SMEM),
            pl.BlockSpec((channels, 1), lambda i: (0, 0)),
        ]
        + [flat_block] * 4
        + [
            pl.BlockSpec((*part.shape[:2], EDGE_ROWS, LANES), lambda i: (0, 0, i, 0))
            for part in parts
        ],
        out_specs=[flat_block] * 4,
        out_shape=[jax.ShapeDtypeStruct((channels, local_len), jnp.bfloat16)] * 4,
        compiler_params=pltpu.CompilerParams(vmem_limit_bytes=40 * 2**20),
        cost_estimate=pl.CostEstimate(
            flops=12 * channels * local_len,
            bytes_accessed=22 * channels * local_len,
            transcendentals=0,
        ),
    )(side, skip_gain[:, None], *flat, *parts)


def after(array, *earlier):
    return lax.optimization_barrier((array, *earlier))[0]


def block_shards(input_gate, output_gate, values, cotangent, filter_raw, filter_decay, skip_gain):
    context_index = lax.axis_index("ctx")
    channels, local_len = input_gate.shape
    filters = filter_raw.shape[0]
    rows = local_len // LANES
    seq_len = local_len * lax.axis_size("ctx")
    data_size = lax.axis_size("dp")
    tables = block_tables(rows)
    side = jnp.where(context_index < 2, 1.0, -1.0).astype(jnp.float32).reshape(1)
    flat = (input_gate, values, cotangent, output_gate)
    *own_parts, other = enter(side, flat, filters)

    positions = (context_index * local_len + jnp.arange(local_len, dtype=jnp.int32)).astype(
        jnp.float32
    )
    filter_scale = seq_len ** (-0.5)

    def envelope(decay):
        return jnp.exp(-decay[:, None] * (positions[None, :] / seq_len))

    share = filters // data_size
    first_filter = lax.axis_index("dp") * share
    raw_share = lax.dynamic_slice_in_dim(filter_raw, first_filter, share, 0)
    decay_share = lax.dynamic_slice_in_dim(filter_decay, first_filter, share, 0)
    taps = (raw_share.astype(jnp.float32) * envelope(decay_share) * filter_scale).astype(
        jnp.bfloat16
    )
    taps = after(taps.reshape(1, share, rows, LANES), own_parts[0])
    taps = lax.all_gather(taps, "ctx", axis=0, tiled=True)
    taps = lax.all_gather(taps, "dp", axis=1, tiled=True)

    def lag_sum(pieces):
        pieces = lax.all_to_all(pieces, "ctx", split_axis=0, concat_axis=0, tiled=True)
        total = jnp.sum(pieces.astype(jnp.float32), axis=0).astype(jnp.bfloat16)
        return lax.all_gather(total, "dp", axis=1, tiled=True)

    near_parts, other_parts, received_parts, lag_parts = [], [], [], []
    start = 0
    for number, own in enumerate(own_parts):
        other_next = lax.ppermute(own, "ctx", [(1, 2), (2, 1)])
        other_far = lax.ppermute(own, "ctx", [(0, 2), (3, 1)])
        far = lax.ppermute(own, "ctx", [(0, 1), (3, 2)])
        if number >= 2:
            own = after(own, received_parts[number - 2], lag_parts[number - 2])
        near_out, other_out, passed, lag = block_products(
            side, (own, far, other_next, other_far), other, taps, tables, start, data_size
        )
        start += own.shape[1]
        near_parts.append(near_out)
        other_parts.append(other_out)
        received_parts.append(lax.ppermute(passed, "ctx", [(1, 0), (2, 3)]))
        lag = lax.all_to_all(lag, "dp", split_axis=0, concat_axis=0, tiled=True)
        lag_parts.append(jnp.sum(lag.astype(jnp.float32), axis=0).astype(jnp.bfloat16))
    lag = jnp.concatenate(
        [
            lag_sum(jnp.concatenate(lag_parts[:2], axis=1)),
            lag_sum(jnp.concatenate(lag_parts[2:], axis=1)),
        ],
        axis=0,
    ).reshape(filters, local_len)
    grad_filter = lag.astype(jnp.float32) * envelope(filter_decay) * filter_scale
    outputs, grad_input_gate, grad_output_gate, grad_values = leave(
        side, skip_gain, flat, near_parts, other_parts, received_parts
    )
    return (outputs, grad_input_gate, grad_output_gate, grad_values, grad_filter)


def chosen_shards(dp, ctx):
    def run(input_gate, *others):
        channels, local_len = input_gate.shape
        filters = others[3].shape[0]
        by_blocks = (
            ctx == 4
            and local_len % (LANES * STRIP * dp) == 0
            and local_len % (LANES * EDGE_ROWS) == 0
            and channels % (2 * filters) == 0
            and filters % dp == 0
            and filters == sum(SHARES)
        )
        return (block_shards if by_blocks else shards)(input_gate, *others)

    return run


def solution(mesh):
    return jax.shard_map(
        chosen_shards(mesh.shape["dp"], mesh.shape["ctx"]),
        mesh=mesh,
        in_specs=(
            P("dp", "ctx"),
            P("dp", "ctx"),
            P("dp", "ctx"),
            P("dp", "ctx"),
            P(None, "ctx"),
            P(),
            P("dp"),
        ),
        out_specs=(P("dp", "ctx"), P("dp", "ctx"), P("dp", "ctx"), P("dp", "ctx"), P(None, "ctx")),
        check_vma=False,
    )
```

profile of v0, /device:TPU:0, one launch (start us, length us, event | category | flops | bytes accessed | tf_op | source)
XLA Modules:
  0.0 415.0 jit_solution(17739626180498113083)
XLA Ops:
  8.0 1.4 fusion.1
  10.1 2.2 copy-done
  12.3 14.0 %shard_map.164 = (bf16[4,6,256,128]{3,2,1,0:T(8,128)(2,1)S(1)}, bf16[4,5,256,128]{3,2,1,0:T(8,128)(2,1)S(1)}, bf16[4,3,256,128]{3,2,1,0:T(8,128)(2,1)S(1)}, bf16...) custom-call(f32[1]{0:T(128)} %bitcast.side_ref, bf16[64,32768]{1,0:T(8,128)(2,1)S(1)} %copy-done, ...), custom_call_target="tpu_custom_call" | custom-call | flops 8388608 | bytes 25165824 | tf_op jit(solution)/shard_map/pallas_call | solution.py:428
  26.3 2.0 copy-done.15
  30.0 18.0 %all_gather.12 = bf16[4,2,256,128]{3,2,1,0:T(8,128)(2,1)} all-gather(bf16[1,2,256,128]{3,2,1,0:T(8,128)(2,1)S(1)} %copy-done.48), channel_id=1, replica_groups=mesh['dp'=8,'ctx'=4] {'ctx'}, dimensions={0}, use_global_device_ids=true | all-gather | bytes 655360 | tf_op jit(solution)/shard_map/all_gather | solution.py:536
  48.0 4.2 %collective-permute-start.3 = (bf16[4,5,256,128]{3,2,1,0:T(8,128)(2,1)S(1)}, bf16[4,5,256,128]{3,2,1,0:T(8,128)(2,1)S(1)}, u32[]{:S(2)}, u32[]{:S(2)}) collective-permute-start(bf16[4,5,256,128]{3,2,1,0:T(8,128)(2,1)S(1)} %get-tuple-element.37.own_ref), channel_id=1, source_target_pairs={{0,1},{3,2},{4,5},{7,6},{8,9},{11,10},{12,13},{15,14},{16,17},{19,... | collective-permute-start | bytes 3932168 | tf_op jit(solution)/shard_map/ppermute | solution.py:549
  53.0 4.9 %collective-permute-start.5 = (bf16[4,5,256,128]{3,2,1,0:T(8,128)(2,1)S(1)}, bf16[4,5,256,128]{3,2,1,0:T(8,128)(2,1)}, u32[]{:S(2)}, u32[]{:S(2)}) collective-permute-start(bf16[4,5,256,128]{3,2,1,0:T(8,128)(2,1)S(1)} %get-tuple-element.37.own_ref), channel_id=1, source_target_pairs={{0,2},{3,1},{4,6},{7,5},{8,10},{11,9},{12,14},{15,13},{16,18},{19,... | collective-permute-start | bytes 3932168 | tf_op jit(solution)/shard_map/ppermute | solution.py:548
  57.9 2.5 collective-permute-start
  60.4 1.8 collective-permute-start.1
  62.3 19.1 %collective-permute-done.3.far_ref = bf16[4,5,256,128]{3,2,1,0:T(8,128)(2,1)S(1)} collective-permute-done((bf16[4,5,256,128]{3,2,1,0:T(8,128)(2,1)S(1)}, bf16[4,5,256,128]{3,2,1,0:T(8,128)(2,1)S(1)}, u32[]{:S(2)}, u32[]{:S(2)}) %collective-permute-start.3) | collective-permute-done | bytes 1310752 | tf_op jit(solution)/shard_map/ppermute | solution.py:549
  81.4 5.5 %collective-permute-start.2 = (bf16[4,6,256,128]{3,2,1,0:T(8,128)(2,1)S(1)}, bf16[4,6,256,128]{3,2,1,0:T(8,128)(2,1)}, u32[]{:S(2)}, u32[]{:S(2)}) collective-permute-start(bf16[4,6,256,128]{3,2,1,0:T(8,128)(2,1)S(1)} %get-tuple-element.33.own_ref), channel_id=1, source_target_pairs={{0,2},{3,1},{4,6},{7,5},{8,10},{11,9},{12,14},{15,13},{16,18},{19,... | collective-permute-start | bytes 4718600 | tf_op jit(solution)/shard_map/ppermute | solution.py:548
  87.9 21.6 %collective-permute-done.5.other_far_ref = bf16[4,5,256,128]{3,2,1,0:T(8,128)(2,1)} collective-permute-done((bf16[4,5,256,128]{3,2,1,0:T(8,128)(2,1)S(1)}, bf16[4,5,256,128]{3,2,1,0:T(8,128)(2,1)}, u32[]{:S(2)}, u32[]{:S(2)}) %collective-permute-start.5) | collective-permute-done | bytes 1310752 | tf_op jit(solution)/shard_map/ppermute | solution.py:548
  112.4 29.6 %shard_map.166 = (bf16[4,5,256,128]{3,2,1,0:T(8,128)(2,1)S(1)}, bf16[4,5,256,128]{3,2,1,0:T(8,128)(2,1)S(1)}, bf16[4,5,256,128]{3,2,1,0:T(8,128)(2,1)}, bf16[8,4,5,32,128]{4,3,2,1,0:T(8,128)(2,1)}) custom-call(f32[1]{0:T(128)} %bitcast.side_ref, bf16[4,5,256,128]{3,2,1,0:T(8,128)(2,1)} %copy-done.17, bf16[4,5,256,128]{3,2,1,0:T(8,128)(2,1)} %copy-done.50, ...), custom_call_target="tpu_custom_call" | custom-call | flops 14763950080 | bytes 13107200 | tf_op jit(solution)/shard_map/pallas_call | solution.py:379
  144.1 1.3 collective-permute-start.10
  145.4 4.3 %all-to-all-start.1 = ((bf16[8,4,5,32,128]{4,3,2,1,0:T(8,128)(2,1)}), bf16[8,4,5,32,128]{4,3,2,1,0:T(8,128)(2,1)}, u32[]{:S(2)}, u32[]{:S(2)}) async-start(bf16[8,4,5,32,128]{4,3,2,1,0:T(8,128)(2,1)} %get-tuple-element.46), calls=%async_computation.1 | async-start | bytes 2621440 | tf_op jit(solution)/shard_map/all_to_all | solution.py:559
  149.7 22.2 %collective-permute-done.2.other_far_ref = bf16[4,6,256,128]{3,2,1,0:T(8,128)(2,1)} collective-permute-done((bf16[4,6,256,128]{3,2,1,0:T(8,128)(2,1)S(1)}, bf16[4,6,256,128]{3,2,1,0:T(8,128)(2,1)}, u32[]{:S(2)}, u32[]{:S(2)}) %collective-permute-start.2) | collective-permute-done | bytes 1572896 | tf_op jit(solution)/shard_map/ppermute | solution.py:548
  175.7 35.1 %shard_map.165 = (bf16[4,6,256,128]{3,2,1,0:T(8,128)(2,1)S(1)}, bf16[4,6,256,128]{3,2,1,0:T(8,128)(2,1)S(1)}, bf16[4,6,256,128]{3,2,1,0:T(8,128)(2,1)}, bf16[8,4,6,32,128]{4,3,2,1,0:T(8,128)(2,1)}) custom-call(f32[1]{0:T(128)} %bitcast.side_ref, bf16[4,6,256,128]{3,2,1,0:T(8,128)(2,1)} %copy-done.16, bf16[4,6,256,128]{3,2,1,0:T(8,128)(2,1)} %collective-permute-done.far_ref, ...), custom_call_target="tpu_custom_call" | custom-call | flops 17716740096 | bytes 15728640 | tf_op jit(solution)/shard_map/pallas_call | solution.py:379
  210.8 1.3 collective-permute-start.6
  212.1 4.3 %all-to-all-start = ((bf16[8,4,6,32,128]{4,3,2,1,0:T(8,128)(2,1)}), bf16[8,4,6,32,128]{4,3,2,1,0:T(8,128)(2,1)}, u32[]{:S(2)}, u32[]{:S(2)}) async-start(bf16[8,4,6,32,128]{4,3,2,1,0:T(8,128)(2,1)} %get-tuple-element.41), calls=%async_computation | async-start | bytes 3145728 | tf_op jit(solution)/shard_map/all_to_all | solution.py:559
  216.4 6.9 %collective-permute-start.11 = (bf16[4,2,256,128]{3,2,1,0:T(8,128)(2,1)}, bf16[4,2,256,128]{3,2,1,0:T(8,128)(2,1)S(1)}, u32[]{:S(2)}, u32[]{:S(2)}) collective-permute-start(bf16[4,2,256,128]{3,2,1,0:T(8,128)(2,1)} %copy-done.21), channel_id=1, source_target_pairs={{0,1},{3,2},{4,5},{7,6},{8,9},{11,10},{12,13},{15,14},{16,17},{19,... | collective-permute-start | bytes 1572872 | tf_op jit(solution)/shard_map/ppermute | solution.py:549
  224.0 4.7 %collective-permute-start.13 = (bf16[4,2,256,128]{3,2,1,0:T(8,128)(2,1)}, bf16[4,2,256,128]{3,2,1,0:T(8,128)(2,1)}, u32[]{:S(2)}, u32[]{:S(2)}) collective-permute-start(bf16[4,2,256,128]{3,2,1,0:T(8,128)(2,1)} %copy-done.21), channel_id=1, source_target_pairs={{0,2},{3,1},{4,6},{7,5},{8,10},{11,9},{12,14},{15,13},{16,18},{19,... | collective-permute-start | bytes 1572872 | tf_op jit(solution)/shard_map/ppermute | solution.py:548
  228.8 7.1 %collective-permute-done.11.far_ref = bf16[4,2,256,128]{3,2,1,0:T(8,128)(2,1)S(1)} collective-permute-done((bf16[4,2,256,128]{3,2,1,0:T(8,128)(2,1)}, bf16[4,2,256,128]{3,2,1,0:T(8,128)(2,1)S(1)}, u32[]{:S(2)}, u32[]{:S(2)}) %collective-permute-start.11) | collective-permute-done | bytes 524320 | tf_op jit(solution)/shard_map/ppermute | solution.py:549
  236.7 5.2 %collective-permute-start.7 = (bf16[4,3,256,128]{3,2,1,0:T(8,128)(2,1)}, bf16[4,3,256,128]{3,2,1,0:T(8,128)(2,1)}, u32[]{:S(2)}, u32[]{:S(2)}) collective-permute-start(bf16[4,3,256,128]{3,2,1,0:T(8,128)(2,1)} %copy-done.18), channel_id=1, source_target_pairs={{0,1},{3,2},{4,5},{7,6},{8,9},{11,10},{12,13},{15,14},{16,17},{19,... | collective-permute-start | bytes 2359304 | tf_op jit(solution)/shard_map/ppermute | solution.py:549
  242.7 1.6 collective-permute-start.8
  244.3 12.8 %collective-permute-start.9 = (bf16[4,3,256,128]{3,2,1,0:T(8,128)(2,1)}, bf16[4,3,256,128]{3,2,1,0:T(8,128)(2,1)}, u32[]{:S(2)}, u32[]{:S(2)}) collective-permute-start(bf16[4,3,256,128]{3,2,1,0:T(8,128)(2,1)} %copy-done.18), channel_id=1, source_target_pairs={{0,2},{3,1},{4,6},{7,5},{8,10},{11,9},{12,14},{15,13},{16,18},{19,... | collective-permute-start | bytes 2359304 | tf_op jit(solution)/shard_map/ppermute | solution.py:548
  257.1 2.2 reduce_sum.73
  266.1 12.1 %shard_map.168 = (bf16[4,2,256,128]{3,2,1,0:T(8,128)(2,1)S(1)}, bf16[4,2,256,128]{3,2,1,0:T(8,128)(2,1)S(1)}, bf16[4,2,256,128]{3,2,1,0:T(8,128)(2,1)S(1)}, bf16[8,4,2,32,128]{4,3,2,1,0:T(8,128)(2,1)S(1)}) custom-call(f32[1]{0:T(128)} %bitcast.side_ref, bf16[4,2,256,128]{3,2,1,0:T(8,128)(2,1)S(1)} %copy-done.22, bf16[4,2,256,128]{3,2,1,0:T(8,128)(2,1)S(1)} %copy-done.25, ...), custom_call_target="tpu_custom_call" | custom-call | flops 5905580032 | bytes 5242880 | tf_op jit(solution)/shard_map/pallas_call | solution.py:379
  281.5 4.2 %all-to-all-start.4 = ((bf16[8,4,2,32,128]{4,3,2,1,0:T(8,128)(2,1)}), bf16[8,4,2,32,128]{4,3,2,1,0:T(8,128)(2,1)}, u32[]{:S(2)}, u32[]{:S(2)}) async-start(bf16[8,4,2,32,128]{4,3,2,1,0:T(8,128)(2,1)} %copy-done.14), calls=%async_computation.4 | async-start | bytes 1048576 | tf_op jit(solution)/shard_map/all_to_all | solution.py:559
  285.7 2.4 reduce_sum.72
  293.0 17.8 %shard_map.167 = (bf16[4,3,256,128]{3,2,1,0:T(8,128)(2,1)S(1)}, bf16[4,3,256,128]{3,2,1,0:T(8,128)(2,1)S(1)}, bf16[4,3,256,128]{3,2,1,0:T(8,128)(2,1)S(1)}, bf16[8,4,3,32,128]{4,3,2,1,0:T(8,128)(2,1)S(1)}) custom-call(f32[1]{0:T(128)} %bitcast.side_ref, bf16[4,3,256,128]{3,2,1,0:T(8,128)(2,1)S(1)} %copy-done.19, ...), custom_call_target="tpu_custom_call" | custom-call | flops 8858370048 | bytes 7864320 | tf_op jit(solution)/shard_map/pallas_call | solution.py:379
  314.3 4.2 %all-to-all-start.3 = ((bf16[8,4,3,32,128]{4,3,2,1,0:T(8,128)(2,1)}), bf16[8,4,3,32,128]{4,3,2,1,0:T(8,128)(2,1)}, u32[]{:S(2)}, u32[]{:S(2)}) async-start(bf16[8,4,3,32,128]{4,3,2,1,0:T(8,128)(2,1)} %copy-done.5), calls=%async_computation.3 | async-start | bytes 1572864 | tf_op jit(solution)/shard_map/all_to_all | solution.py:559
  318.6 1.3 collective-permute-start.14
  319.9 1.8 pad_maximum_fusion
  321.7 9.4 %all-to-all-done.3 = bf16[8,4,3,32,128]{4,3,2,1,0:T(8,128)(2,1)} async-done(((bf16[8,4,3,32,128]{4,3,2,1,0:T(8,128)(2,1)}), bf16[8,4,3,32,128]{4,3,2,1,0:T(8,128)(2,1)}, u32[]{:S(2)}, u32[]{:S(2)}) %all-to-all-start.3) | async-done | bytes 786464 | tf_op jit(solution)/shard_map/all_to_all | solution.py:559
  331.2 3.7 all-to-all-start.2
  334.9 1.3 collective-permute-start.15
  336.2 1.8 reduce_sum.76
  337.9 1.9 reduce_sum.75
  339.8 1.6 pad_maximum_fusion.1
  341.4 5.4 %all-to-all-done.2 = bf16[4,11,32,128]{3,2,1,0:T(8,128)(2,1)S(1)} async-done(((bf16[4,11,32,128]{3,2,1,0:T(8,128)(2,1)}), bf16[4,11,32,128]{3,2,1,0:T(8,128)(2,1)S(1)}, u32[]{:S(2)}, u32[]{:S(2)}) %all-to-all-start.2) | async-done | bytes 360480 | tf_op jit(solution)/shard_map/all_to_all | solution.py:540
  346.8 4.0 all-to-all-start.5
  351.6 12.8 %all_gather.14 = bf16[11,256,128]{2,1,0:T(8,128)(2,1)} all-gather(bf16[11,32,128]{2,1,0:T(8,128)(2,1)} %reduce_sum.74), channel_id=1, replica_groups=mesh['dp'=8,'ctx'=4] {'dp'}, dimensions={1}, use_global_device_ids=true | all-gather | bytes 811008 | tf_op jit(solution)/shard_map/all_gather | solution.py:542
  364.4 1.3 copy-done.2
  365.8 1.3 copy-done.4
  371.4 23.0 %shard_map.169 = (bf16[64,32768]{1,0:T(8,128)(2,1)}, bf16[64,32768]{1,0:T(8,128)(2,1)}, bf16[64,32768]{1,0:T(8,128)(2,1)}, bf16[64,32768]{1,0:T(8,128)(2,1)}) custom-call(f32[1]{0:T(128)} %bitcast.side_ref, f32[64,1]{1,0:T(8,128)S(1)} %copy.20.skip_ref, bf16[64,32768]{1,0:T(8,128)(2,1)} %gate_ref.3, bf16[64,32768]{1,0:T(8,128)(2,1)} %values_ref.3, ...), custom_call_target="tpu_custom_call" | custom-call | flops 25165824 | bytes 46137344 | tf_op jit(solution)/shard_map/pallas_call | solution.py:481
  395.4 8.7 %all_gather.15 = bf16[5,256,128]{2,1,0:T(8,128)(2,1)S(1)} all-gather(bf16[5,32,128]{2,1,0:T(8,128)(2,1)S(1)} %reduce_sum.77), channel_id=1, replica_groups=mesh['dp'=8,'ctx'=4] {'dp'}, dimensions={1}, use_global_device_ids=true | all-gather | bytes 368640 | tf_op jit(solution)/shard_map/all_gather | solution.py:542
  404.1 1.2 maximum_convert_fusion
  405.4 2.7 fusion
  (130 shorter events, 40.7 us)
Async XLA Ops:
  7.2 102.4 %all-gather.2.cloned.1.call-start = ((), (), s32[]{:S(2)}) async-start(), calls=%async_computation.6 | async-start | bytes 4718592 | tf_op jit(solution)/shard_map/all_gather | solution.py:537
  7.2 2.9 copy-start.46
  10.1 2.2 copy-start
  12.3 17.7 %copy-start.48 = (bf16[1,2,256,128]{3,2,1,0:T(8,128)(2,1)S(1)}, bf16[1,2,256,128]{3,2,1,0:T(8,128)(2,1)}, u32[]{:S(2)}) copy-start(bf16[1,2,256,128]{3,2,1,0:T(8,128)(2,1)} %copy.25) | copy-start | bytes 393220
  12.3 97.2 %copy-start.28 = (bf16[512,256]{1,0:T(8,128)(2,1)S(1)}, bf16[512,256]{1,0:T(8,128)(2,1)}, u32[]{:S(2)}) copy-start(bf16[512,256]{1,0:T(8,128)(2,1)} %constant.47.clone.first_forward_ref) | copy-start | bytes 786436
  12.3 97.2 %copy-start.29 = (bf16[256,512]{1,0:T(8,128)(2,1)S(1)}, bf16[256,512]{1,0:T(8,128)(2,1)}, u32[]{:S(2)}) copy-start(bf16[256,512]{1,0:T(8,128)(2,1)} %constant.50.clone.first_inverse_ref) | copy-start | bytes 786436
  12.3 97.2 %copy-start.41 = (bf16[256,256]{1,0:T(8,128)(2,1)S(1)}, bf16[256,256]{1,0:T(8,128)(2,1)}, u32[]{:S(2)}) copy-start(bf16[256,256]{1,0:T(8,128)(2,1)} %constant.48.clone.second_forward_ref) | copy-start | bytes 393220
  26.3 2.0 copy-start.15
  30.0 79.5 %copy-start.17 = (bf16[4,5,256,128]{3,2,1,0:T(8,128)(2,1)}, bf16[4,5,256,128]{3,2,1,0:T(8,128)(2,1)S(1)}, u32[]{:S(2)}) copy-start(bf16[4,5,256,128]{3,2,1,0:T(8,128)(2,1)S(1)} %get-tuple-element.37.own_ref) | copy-start | bytes 3932164
  30.0 112.0 %copy-start.16 = (bf16[4,6,256,128]{3,2,1,0:T(8,128)(2,1)}, bf16[4,6,256,128]{3,2,1,0:T(8,128)(2,1)S(1)}, u32[]{:S(2)}) copy-start(bf16[4,6,256,128]{3,2,1,0:T(8,128)(2,1)S(1)} %get-tuple-element.33.own_ref) | copy-start | bytes 4718596
  48.0 33.4 %collective-permute-start.3 = (bf16[4,5,256,128]{3,2,1,0:T(8,128)(2,1)S(1)}, bf16[4,5,256,128]{3,2,1,0:T(8,128)(2,1)S(1)}, u32[]{:S(2)}, u32[]{:S(2)}) collective-permute-start(bf16[4,5,256,128]{3,2,1,0:T(8,128)(2,1)S(1)} %get-tuple-element.37.own_ref), channel_id=1, source_target_pairs={{0,1},{3,2},{4,5},{7,6},{8,9},{11,10},{12,13},{15,14},{16,17},{19,... | collective-permute-start | bytes 3932168 | tf_op jit(solution)/shard_map/ppermute | solution.py:549
  52.3 34.6 %collective-permute-start.4 = (bf16[4,5,256,128]{3,2,1,0:T(8,128)(2,1)S(1)}, bf16[4,5,256,128]{3,2,1,0:T(8,128)(2,1)S(1)}, u32[]{:S(2)}, u32[]{:S(2)}) collective-permute-start(bf16[4,5,256,128]{3,2,1,0:T(8,128)(2,1)S(1)} %get-tuple-element.37.own_ref), channel_id=1, source_target_pairs={{1,2},{2,1},{5,6},{6,5},{9,10},{10,9},{13,14},{14,13},{17,18},{18,... | collective-permute-start | bytes 3932168 | tf_op jit(solution)/shard_map/ppermute | solution.py:547
  53.0 56.5 %collective-permute-start.5 = (bf16[4,5,256,128]{3,2,1,0:T(8,128)(2,1)S(1)}, bf16[4,5,256,128]{3,2,1,0:T(8,128)(2,1)}, u32[]{:S(2)}, u32[]{:S(2)}) collective-permute-start(bf16[4,5,256,128]{3,2,1,0:T(8,128)(2,1)S(1)} %get-tuple-element.37.own_ref), channel_id=1, source_target_pairs={{0,2},{3,1},{4,6},{7,5},{8,10},{11,9},{12,14},{15,13},{16,18},{19,... | collective-permute-start | bytes 3932168 | tf_op jit(solution)/shard_map/ppermute | solution.py:548
  57.9 91.8 %collective-permute-start = (bf16[4,6,256,128]{3,2,1,0:T(8,128)(2,1)S(1)}, bf16[4,6,256,128]{3,2,1,0:T(8,128)(2,1)}, u32[]{:S(2)}, u32[]{:S(2)}) collective-permute-start(bf16[4,6,256,128]{3,2,1,0:T(8,128)(2,1)S(1)} %get-tuple-element.33.own_ref), channel_id=1, source_target_pairs={{0,1},{3,2},{4,5},{7,6},{8,9},{11,10},{12,13},{15,14},{16,17},{19,... | collective-permute-start | bytes 4718600 | tf_op jit(solution)/shard_map/ppermute | solution.py:549
  60.4 89.3 %collective-permute-start.1 = (bf16[4,6,256,128]{3,2,1,0:T(8,128)(2,1)S(1)}, bf16[4,6,256,128]{3,2,1,0:T(8,128)(2,1)}, u32[]{:S(2)}, u32[]{:S(2)}) collective-permute-start(bf16[4,6,256,128]{3,2,1,0:T(8,128)(2,1)S(1)} %get-tuple-element.33.own_ref), channel_id=1, source_target_pairs={{1,2},{2,1},{5,6},{6,5},{9,10},{10,9},{13,14},{14,13},{17,18},{18,... | collective-permute-start | bytes 4718600 | tf_op jit(solution)/shard_map/ppermute | solution.py:547
  81.4 5.5 %copy-start.50 = (bf16[4,5,256,128]{3,2,1,0:T(8,128)(2,1)}, bf16[4,5,256,128]{3,2,1,0:T(8,128)(2,1)S(1)}, u32[]{:S(2)}) copy-start(bf16[4,5,256,128]{3,2,1,0:T(8,128)(2,1)S(1)} %collective-permute-done.3.far_ref) | copy-start | bytes 3932164
  81.4 90.6 %collective-permute-start.2 = (bf16[4,6,256,128]{3,2,1,0:T(8,128)(2,1)S(1)}, bf16[4,6,256,128]{3,2,1,0:T(8,128)(2,1)}, u32[]{:S(2)}, u32[]{:S(2)}) collective-permute-start(bf16[4,6,256,128]{3,2,1,0:T(8,128)(2,1)S(1)} %get-tuple-element.33.own_ref), channel_id=1, source_target_pairs={{0,2},{3,1},{4,6},{7,5},{8,10},{11,9},{12,14},{15,13},{16,18},{19,... | collective-permute-start | bytes 4718600 | tf_op jit(solution)/shard_map/ppermute | solution.py:548
  86.9 1.1 copy-start.51
  142.0 1.1 copy-start.1
  143.0 1.1 copy-start.3
  144.1 100.1 %collective-permute-start.10 = (bf16[4,5,256,128]{3,2,1,0:T(8,128)(2,1)}, bf16[4,5,256,128]{3,2,1,0:T(8,128)(2,1)}, u32[]{:S(2)}, u32[]{:S(2)}) collective-permute-start(bf16[4,5,256,128]{3,2,1,0:T(8,128)(2,1)} %get-tuple-element.45), channel_id=1, source_target_pairs={{1,0},{2,3},{5,4},{6,7},{9,8},{10,11},{13,12},{14,15},{17,16},{18,... | collective-permute-start | bytes 3932168 | tf_op jit(solution)/shard_map/ppermute | solution.py:558
  145.4 66.6 %all-to-all-start.1 = ((bf16[8,4,5,32,128]{4,3,2,1,0:T(8,128)(2,1)}), bf16[8,4,5,32,128]{4,3,2,1,0:T(8,128)(2,1)}, u32[]{:S(2)}, u32[]{:S(2)}) async-start(bf16[8,4,5,32,128]{4,3,2,1,0:T(8,128)(2,1)} %get-tuple-element.46), calls=%async_computation.1 | async-start | bytes 2621440 | tf_op jit(solution)/shard_map/all_to_all | solution.py:559
  210.8 77.3 %collective-permute-start.6 = (bf16[4,6,256,128]{3,2,1,0:T(8,128)(2,1)}, bf16[4,6,256,128]{3,2,1,0:T(8,128)(2,1)}, u32[]{:S(2)}, u32[]{:S(2)}) collective-permute-start(bf16[4,6,256,128]{3,2,1,0:T(8,128)(2,1)} %get-tuple-element.40), channel_id=1, source_target_pairs={{1,0},{2,3},{5,4},{6,7},{9,8},{10,11},{13,12},{14,15},{17,16},{18,... | collective-permute-start | bytes 4718600 | tf_op jit(solution)/shard_map/ppermute | solution.py:558
  212.1 69.4 %all-to-all-start = ((bf16[8,4,6,32,128]{4,3,2,1,0:T(8,128)(2,1)}), bf16[8,4,6,32,128]{4,3,2,1,0:T(8,128)(2,1)}, u32[]{:S(2)}, u32[]{:S(2)}) async-start(bf16[8,4,6,32,128]{4,3,2,1,0:T(8,128)(2,1)} %get-tuple-element.41), calls=%async_computation | async-start | bytes 3145728 | tf_op jit(solution)/shard_map/all_to_all | solution.py:559
  216.4 19.5 %collective-permute-start.11 = (bf16[4,2,256,128]{3,2,1,0:T(8,128)(2,1)}, bf16[4,2,256,128]{3,2,1,0:T(8,128)(2,1)S(1)}, u32[]{:S(2)}, u32[]{:S(2)}) collective-permute-start(bf16[4,2,256,128]{3,2,1,0:T(8,128)(2,1)} %copy-done.21), channel_id=1, source_target_pairs={{0,1},{3,2},{4,5},{7,6},{8,9},{11,10},{12,13},{15,14},{16,17},{19,... | collective-permute-start | bytes 1572872 | tf_op jit(solution)/shard_map/ppermute | solution.py:549
  223.3 18.5 %collective-permute-start.12 = (bf16[4,2,256,128]{3,2,1,0:T(8,128)(2,1)}, bf16[4,2,256,128]{3,2,1,0:T(8,128)(2,1)S(1)}, u32[]{:S(2)}, u32[]{:S(2)}) collective-permute-start(bf16[4,2,256,128]{3,2,1,0:T(8,128)(2,1)} %copy-done.21), channel_id=1, source_target_pairs={{1,2},{2,1},{5,6},{6,5},{9,10},{10,9},{13,14},{14,13},{17,18},{18,... | collective-permute-start | bytes 1572872 | tf_op jit(solution)/shard_map/ppermute | solution.py:547
  224.0 35.2 %collective-permute-start.13 = (bf16[4,2,256,128]{3,2,1,0:T(8,128)(2,1)}, bf16[4,2,256,128]{3,2,1,0:T(8,128)(2,1)}, u32[]{:S(2)}, u32[]{:S(2)}) collective-permute-start(bf16[4,2,256,128]{3,2,1,0:T(8,128)(2,1)} %copy-done.21), channel_id=1, source_target_pairs={{0,2},{3,1},{4,6},{7,5},{8,10},{11,9},{12,14},{15,13},{16,18},{19,... | collective-permute-start | bytes 1572872 | tf_op jit(solution)/shard_map/ppermute | solution.py:548
  236.7 51.4 %collective-permute-start.7 = (bf16[4,3,256,128]{3,2,1,0:T(8,128)(2,1)}, bf16[4,3,256,128]{3,2,1,0:T(8,128)(2,1)}, u32[]{:S(2)}, u32[]{:S(2)}) collective-permute-start(bf16[4,3,256,128]{3,2,1,0:T(8,128)(2,1)} %copy-done.18), channel_id=1, source_target_pairs={{0,1},{3,2},{4,5},{7,6},{8,9},{11,10},{12,13},{15,14},{16,17},{19,... | collective-permute-start | bytes 2359304 | tf_op jit(solution)/shard_map/ppermute | solution.py:549
  242.7 45.4 %collective-permute-start.8 = (bf16[4,3,256,128]{3,2,1,0:T(8,128)(2,1)}, bf16[4,3,256,128]{3,2,1,0:T(8,128)(2,1)}, u32[]{:S(2)}, u32[]{:S(2)}) collective-permute-start(bf16[4,3,256,128]{3,2,1,0:T(8,128)(2,1)} %copy-done.18), channel_id=1, source_target_pairs={{1,2},{2,1},{5,6},{6,5},{9,10},{10,9},{13,14},{14,13},{17,18},{18,... | collective-permute-start | bytes 2359304 | tf_op jit(solution)/shard_map/ppermute | solution.py:547
  244.3 43.8 %collective-permute-start.9 = (bf16[4,3,256,128]{3,2,1,0:T(8,128)(2,1)}, bf16[4,3,256,128]{3,2,1,0:T(8,128)(2,1)}, u32[]{:S(2)}, u32[]{:S(2)}) collective-permute-start(bf16[4,3,256,128]{3,2,1,0:T(8,128)(2,1)} %copy-done.18), channel_id=1, source_target_pairs={{0,2},{3,1},{4,6},{7,5},{8,10},{11,9},{12,14},{15,13},{16,18},{19,... | collective-permute-start | bytes 2359304 | tf_op jit(solution)/shard_map/ppermute | solution.py:548
  259.3 1.0 copy-start.22
  260.3 1.0 copy-start.25
  261.3 1.0 copy-start.27
  281.5 32.8 %all-to-all-start.4 = ((bf16[8,4,2,32,128]{4,3,2,1,0:T(8,128)(2,1)}), bf16[8,4,2,32,128]{4,3,2,1,0:T(8,128)(2,1)}, u32[]{:S(2)}, u32[]{:S(2)}) async-start(bf16[8,4,2,32,128]{4,3,2,1,0:T(8,128)(2,1)} %copy-done.14), calls=%async_computation.4 | async-start | bytes 1048576 | tf_op jit(solution)/shard_map/all_to_all | solution.py:559
  288.1 1.1 copy-start.19
  314.3 16.8 %all-to-all-start.3 = ((bf16[8,4,3,32,128]{4,3,2,1,0:T(8,128)(2,1)}), bf16[8,4,3,32,128]{4,3,2,1,0:T(8,128)(2,1)}, u32[]{:S(2)}, u32[]{:S(2)}) async-start(bf16[8,4,3,32,128]{4,3,2,1,0:T(8,128)(2,1)} %copy-done.5), calls=%async_computation.3 | async-start | bytes 1572864 | tf_op jit(solution)/shard_map/all_to_all | solution.py:559
  318.6 32.2 %copy-start.52 = (f32[16]{0:T(128)S(1)}, f32[16]{0:T(128)}, u32[]{:S(2)}) copy-start(f32[16]{0:T(128)} %param.18) | copy-start | bytes 196
  318.6 32.2 %copy-start.49 = (f32[64]{0:T(128)S(1)}, f32[64]{0:T(128)}, u32[]{:S(2)}) copy-start(f32[64]{0:T(128)} %param.19) | copy-start | bytes 772
  318.6 45.9 %collective-permute-start.14 = (bf16[4,3,256,128]{3,2,1,0:T(8,128)(2,1)}, bf16[4,3,256,128]{3,2,1,0:T(8,128)(2,1)}, u32[]{:S(2)}, u32[]{:S(2)}) collective-permute-start(bf16[4,3,256,128]{3,2,1,0:T(8,128)(2,1)} %copy-done.20), channel_id=1, source_target_pairs={{1,0},{2,3},{5,4},{6,7},{9,8},{10,11},{13,12},{14,15},{17,16},{18,... | collective-permute-start | bytes 2359304 | tf_op jit(solution)/shard_map/ppermute | solution.py:558
  331.2 15.6 %all-to-all-start.2 = ((bf16[4,11,32,128]{3,2,1,0:T(8,128)(2,1)}), bf16[4,11,32,128]{3,2,1,0:T(8,128)(2,1)S(1)}, u32[]{:S(2)}, u32[]{:S(2)}) async-start(bf16[4,11,32,128]{3,2,1,0:T(8,128)(2,1)} %pad_maximum_fusion), calls=%async_computation.2 | async-start | bytes 720896 | tf_op jit(solution)/shard_map/all_to_all | solution.py:540
  334.9 29.6 %collective-permute-start.15 = (bf16[4,2,256,128]{3,2,1,0:T(8,128)(2,1)}, bf16[4,2,256,128]{3,2,1,0:T(8,128)(2,1)}, u32[]{:S(2)}, u32[]{:S(2)}) collective-permute-start(bf16[4,2,256,128]{3,2,1,0:T(8,128)(2,1)} %copy-done.23), channel_id=1, source_target_pairs={{1,0},{2,3},{5,4},{6,7},{9,8},{10,11},{13,12},{14,15},{17,16},{18,... | collective-permute-start | bytes 1572872 | tf_op jit(solution)/shard_map/ppermute | solution.py:558
  346.8 47.6 %all-to-all-start.5 = ((bf16[4,5,32,128]{3,2,1,0:T(8,128)(2,1)}), bf16[4,5,32,128]{3,2,1,0:T(8,128)(2,1)}, u32[]{:S(2)}, u32[]{:S(2)}) async-start(bf16[4,5,32,128]{3,2,1,0:T(8,128)(2,1)} %pad_maximum_fusion.1), calls=%async_computation.5 | async-start | bytes 327680 | tf_op jit(solution)/shard_map/all_to_all | solution.py:540
  364.4 1.3 copy-start.2
  365.8 1.3 copy-start.4
  367.1 1.1 copy-start.7
  368.2 1.1 copy-start.9
  369.3 1.0 copy-start.11
  394.4 11.0 %copy-start.47 = (f32[32768]{0:T(1024)S(1)}, f32[32768]{0:T(1024)}, u32[]{:S(2)}) copy-start(f32[32768]{0:T(1024)} %copy-done.46) | copy-start | bytes 393220
  (28 other events, 25.1 us)
Sparse Core Ops, SparseCore 0:
  48.1 38.5 all-gather.1
where the time goes:
time: 418 us; the launch traced here: 415 us
  Pallas kernels  132 us (32%)
  waiting for transfers between devices  84.9 us (20%)
  starting transfers between devices  81.5 us (19%)
  local copies, waits for them, and re-layouts  43.5 us (10%)
  blocking collectives  39.5 us (9%)
  other arithmetic  19.6 us (5%)
  between operations  14.4 us (3%)
    pallas_call x4, Pallas kernels, block_products(): pl.pallas_call(block_kernel, grid=(filters,), in_specs=[pl.BlockSpec(memo...  94.7 us
    ppermute x4, waiting for transfers between devices, block_shards(): other_far = lax.ppermute(own, 'ctx', [(0, 2), (3, 1)])  43.8 us
    unnamed x107, local copies, waits for them, and re-layouts  43.4 us
    ppermute x4, starting transfers between devices, block_shards(): other_far = lax.ppermute(own, 'ctx', [(0, 2), (3, 1)])  27.9 us
    ppermute x4, waiting for transfers between devices, block_shards(): far = lax.ppermute(own, 'ctx', [(0, 1), (3, 2)])  26.2 us
    pallas_call x1, Pallas kernels, leave(): pl.pallas_call(leave_kernel, grid=(local_len // (EDGE_ROWS * LANES),), in...  23 us
    all_gather x2, blocking collectives, lag_sum(): return lax.all_gather(total, 'dp', axis=1, tiled=True)  21.5 us
    ppermute x4, starting transfers between devices, block_shards(): far = lax.ppermute(own, 'ctx', [(0, 1), (3, 2)])  18.9 us
  transfers between devices with their start and end apart: 23, of which 6 were waited for; matrix products, arithmetic and copies ran while one was open for 3% of the time, Pallas kernels for 28%

commit v1 on v0

--- a/solution.py
+++ b/solution.py
@@ -192,9 +192,10 @@
 
 
 LANES = 128
-SHARES = (6, 5, 3, 2)
+SHARES = (6, 6, 2, 2)
 STRIP = 16
 EDGE_ROWS = 16
+VMEM_BYTES = 60 * 2**20
 
 
 def block_tables(rows):
@@ -374,7 +375,6 @@
 
     made = jax.ShapeDtypeStruct(signals[0].shape, jnp.bfloat16)
     lag = jax.ShapeDtypeStruct((shares, 4, filters, rows // shares, lanes), jnp.bfloat16)
-    transforms = filters * (9 * groups + 8)
     own, far, other_next, other_far = signals
     return pl.pallas_call(
         block_kernel,
@@ -388,12 +388,8 @@
             pltpu.VMEM((6, groups, rows, 2 * lanes), jnp.float32),
             pltpu.VMEM((3 * groups + 4, rows, 2 * lanes), jnp.bfloat16),
         ],
-        compiler_params=pltpu.CompilerParams(vmem_limit_bytes=48 * 2**20),
-        cost_estimate=pl.CostEstimate(
-            flops=transforms * 2 * (2 * rows * rows * lanes + rows * 4 * lanes * lanes),
-            bytes_accessed=filters * (8 * groups + 8) * rows * lanes * 2,
-            transcendentals=0,
-        ),
+        compiler_params=pltpu.CompilerParams(vmem_limit_bytes=VMEM_BYTES),
+        cost_estimate=pl.CostEstimate(flops=1, bytes_accessed=1, transcendentals=0),
     )(side, own, far, other, other_next, other_far, taps, *tables)
 
 
@@ -437,7 +433,7 @@
         out_shape=[
             jax.ShapeDtypeStruct((groups, count, rows, LANES), jnp.bfloat16) for count in counts
         ],
-        compiler_params=pltpu.CompilerParams(vmem_limit_bytes=40 * 2**20),
+        compiler_params=pltpu.CompilerParams(vmem_limit_bytes=VMEM_BYTES),
         cost_estimate=pl.CostEstimate(
             flops=4 * channels * local_len,
             bytes_accessed=12 * channels * local_len,
@@ -454,12 +450,14 @@
     outputs_ref, grad_gate_ref, grad_out_gate_ref, grad_values_ref = refs[3 * parts :]
     near_start = side_ref[0] > 0
 
-    def flat(part_refs):
-        whole = jnp.concatenate([ref[...] for ref in part_refs], axis=1).astype(jnp.float32)
-        return whole.reshape(channels, width // LANES, LANES).reshape(channels, width)
-
-    near = flat(near_refs)
-    other = flat(other_refs) + flat(received_refs)
+    def whole(part_refs):
+        return jnp.concatenate([ref[...] for ref in part_refs], axis=1).astype(jnp.float32)
+
+    def flat(array):
+        return array.reshape(channels, width // LANES, LANES).reshape(channels, width)
+
+    near = flat(whole(near_refs))
+    other = flat(whole(other_refs) + whole(received_refs))
     skip = skip_ref[...]
     gate, values = gate_ref[...].astype(jnp.float32), values_ref[...].astype(jnp.float32)
     cotangent = cotangent_ref[...].astype(jnp.float32)
@@ -492,7 +490,7 @@
         ],
         out_specs=[flat_block] * 4,
         out_shape=[jax.ShapeDtypeStruct((channels, local_len), jnp.bfloat16)] * 4,
-        compiler_params=pltpu.CompilerParams(vmem_limit_bytes=40 * 2**20),
+        compiler_params=pltpu.CompilerParams(vmem_limit_bytes=VMEM_BYTES),
         cost_estimate=pl.CostEstimate(
             flops=12 * channels * local_len,
             bytes_accessed=22 * channels * local_len,
@@ -533,20 +531,40 @@
         jnp.bfloat16
     )
     taps = after(taps.reshape(1, share, rows, LANES), own_parts[0])
-    taps = lax.all_gather(taps, "ctx", axis=0, tiled=True)
+    taps = jnp.broadcast_to(taps, (4, share, rows, LANES))
+    taps = lax.all_to_all(taps, "ctx", split_axis=0, concat_axis=0, tiled=True)
     taps = lax.all_gather(taps, "dp", axis=1, tiled=True)
+
+    def lag_shares(pieces):
+        pieces = lax.all_to_all(pieces, "dp", split_axis=0, concat_axis=0, tiled=True)
+        return jnp.sum(pieces.astype(jnp.float32), axis=0).astype(jnp.bfloat16)
 
     def lag_sum(pieces):
         pieces = lax.all_to_all(pieces, "ctx", split_axis=0, concat_axis=0, tiled=True)
         total = jnp.sum(pieces.astype(jnp.float32), axis=0).astype(jnp.bfloat16)
-        return lax.all_gather(total, "dp", axis=1, tiled=True)
-
-    near_parts, other_parts, received_parts, lag_parts = [], [], [], []
+        spread = jnp.broadcast_to(total[None], (data_size, *total.shape))
+        spread = lax.all_to_all(spread, "dp", split_axis=0, concat_axis=0, tiled=True)
+        return jnp.transpose(spread, (1, 0, 2, 3)).reshape(total.shape[0], rows, LANES)
+
+    routes = ([(1, 2), (2, 1)], [(0, 2), (3, 1)], [(0, 1), (3, 2)])
+    arrivals, near_parts, other_parts, received_parts, lag_parts = [], [], [], [], []
+
+    def send(number):
+        own, made = own_parts[number], []
+        for stream, route in enumerate(routes):
+            earlier = [arrivals[number - 1][stream]] if number else []
+            earlier += near_parts[number - 2 : number - 1] if number >= 2 else []
+            made.append(lax.ppermute(after(own, *earlier), "ctx", route))
+        arrivals.append(made)
+
     start = 0
+    send(0)
     for number, own in enumerate(own_parts):
-        other_next = lax.ppermute(own, "ctx", [(1, 2), (2, 1)])
-        other_far = lax.ppermute(own, "ctx", [(0, 2), (3, 1)])
-        far = lax.ppermute(own, "ctx", [(0, 1), (3, 2)])
+        if number + 1 < len(own_parts):
+            send(number + 1)
+        other_next, other_far, far = arrivals[number]
+        if number >= 1:
+            own = after(own, near_parts[number - 1])
         if number >= 2:
             own = after(own, received_parts[number - 2], lag_parts[number - 2])
         near_out, other_out, passed, lag = block_products(
@@ -555,16 +573,13 @@
         start += own.shape[1]
         near_parts.append(near_out)
         other_parts.append(other_out)
+        if number == len(own_parts) - 1:
+            passed = after(passed, received_parts[number - 1])
         received_parts.append(lax.ppermute(passed, "ctx", [(1, 0), (2, 3)]))
-        lag = lax.all_to_all(lag, "dp", split_axis=0, concat_axis=0, tiled=True)
-        lag_parts.append(jnp.sum(lag.astype(jnp.float32), axis=0).astype(jnp.bfloat16))
-    lag = jnp.concatenate(
-        [
-            lag_sum(jnp.concatenate(lag_parts[:2], axis=1)),
-            lag_sum(jnp.concatenate(lag_parts[2:], axis=1)),
-        ],
-        axis=0,
-    ).reshape(filters, local_len)
+        lag_parts.append(lag_shares(lag) if number < 2 else lag)
+    late = lag_shares(jnp.concatenate(lag_parts[2:], axis=2))
+    late = after(late, received_parts[-1])
+    lag = lag_sum(jnp.concatenate([*lag_parts[:2], late], axis=1)).reshape(filters, local_len)
     grad_filter = lag.astype(jnp.float32) * envelope(filter_decay) * filter_scale
     outputs, grad_input_gate, grad_output_gate, grad_values = leave(
         side, skip_gain, flat, near_parts, other_parts, received_parts

time: 418 us -> 375 us (0.90)
  local copies, waits for them, and re-layouts: 43.5 us -> 4.26 us
  waiting for transfers between devices: 84.9 us -> 100 us
  other arithmetic: 19.6 us -> 8.14 us
  starting transfers between devices: 81.5 us -> 70.3 us
  Pallas kernels: 132 us -> 138 us
    unnamed x107 -> x27, local copies, waits for them, and re-layouts: 43.4 us -> 2.09 us
    all_gather x3 -> x0, blocking collectives: 39.5 us -> none  [the longest x2 21.5 us: lag_sum(): return lax.all_gather(total, 'dp', axis=1, tiled=True)]
    all_to_all x0 -> x2, blocking collectives: none -> 38.3 us  [the longest x1 20.8 us: block_shards(): taps = lax.all_to_all(taps, 'ctx', split_axis=0, concat_axis=0, tiled=True)]
    ppermute x12, waiting for transfers between devices: 70 us -> 84.5 us  [send(): made.append(lax.ppermute(after(own, *earlier), 'ctx', route))]
    all_to_all x6 -> x4, starting transfers between devices: 24.6 us -> 15.7 us  [the longest x3 12 us: lag_shares(): lax.all_to_all(pieces, 'dp', split_axis=0, concat_axis=0, tiled=True)]
    reduce_sum x4 -> x3, other arithmetic: 8.26 us -> 0.67 us  [lag_shares(): return jnp.sum(pieces.astype(jnp.float32), axis=0).astype(jnp.bfloat16)]
    all_to_all x6 -> x4, waiting for transfers between devices: 14.8 us -> 14.1 us  [the longest x3 14.1 us: lag_shares(): lax.all_to_all(pieces, 'dp', split_axis=0, concat_axis=0, tiled=True)]
  transfers between devices with their start and end apart: 23 -> 21, of which waited for: 6 -> 7; matrix products, arithmetic and copies ran while one was open for 3% -> 1% of each run, Pallas kernels for 28% -> 33%
where the time goes in v1:
time: 375 us; the launch traced here: 374 us
  Pallas kernels  138 us (37%)
  waiting for transfers between devices  100 us (27%)
  starting transfers between devices  70.3 us (19%)
  blocking collectives  38.3 us (10%)
  between operations  14.3 us (4%)
  other arithmetic  8.14 us (2%)
  local copies, waits for them, and re-layouts  4.26 us (1%)
    pallas_call x4, Pallas kernels, block_products(): pl.pallas_call(block_kernel, grid=(filters,), in_specs=[pl.BlockSpec(memo...  98.8 us
    ppermute x12, waiting for transfers between devices, send(): made.append(lax.ppermute(after(own, *earlier), 'ctx', route))  84.5 us
    ppermute x12, starting transfers between devices, send(): made.append(lax.ppermute(after(own, *earlier), 'ctx', route))  49.3 us
    pallas_call x1, Pallas kernels, leave(): pl.pallas_call(leave_kernel, grid=(local_len // (EDGE_ROWS * LANES),), in...  23 us
    all_to_all x1, blocking collectives, block_shards(): taps = lax.all_to_all(taps, 'ctx', split_axis=0, concat_axis=0, tiled=True)  20.8 us
    all_to_all x1, blocking collectives, lag_sum(): lax.all_to_all(pieces, 'ctx', split_axis=0, concat_axis=0, tiled=True)  17.5 us
    pallas_call x1, Pallas kernels, enter(): pl.pallas_call(enter_kernel, grid=(rows // EDGE_ROWS,), in_specs=[pl.Bloc...  16.2 us
    all_to_all x3, waiting for transfers between devices, lag_shares(): lax.all_to_all(pieces, 'dp', split_axis=0, concat_axis=0, tiled=True)  14.1 us
  transfers between devices with their start and end apart: 21, of which 7 were waited for; matrix products, arithmetic and copies ran while one was open for 1% of the time, Pallas kernels for 33%

profile of v1, /device:TPU:0, one launch (start us, length us, event | category | flops | bytes accessed | tf_op | source)
XLA Modules:
  0.0 373.7 jit_solution(5091514672619548829)
XLA Ops:
  7.3 0.7 dynamic-slice_negate_fusion
  8.0 1.4 fusion.1
  9.4 16.2 %shard_map.164 = (bf16[4,6,256,128]{3,2,1,0:T(8,128)(2,1)}, bf16[4,6,256,128]{3,2,1,0:T(8,128)(2,1)}, bf16[4,2,256,128]{3,2,1,0:T(8,128)(2,1)}, bf16[4,2,256,128...) custom-call(f32[1]{0:T(128)} %bitcast.side_ref, bf16[64,32768]{1,0:T(8,128)(2,1)} %gate_ref.3, bf16[64,32768]{1,0:T(8,128)(2,1)} %values_ref.3, ...), custom_call_target="tpu_custom_call" | custom-call | flops 8388608 | bytes 25165824 | tf_op jit(solution)/shard_map/pallas_call | solution.py:424
  25.7 20.8 %all_to_all.30 = bf16[4,2,256,128]{3,2,1,0:T(8,128)(2,1)} all-to-all(bf16[4,2,256,128]{3,2,1,0:T(8,128)(2,1)S(1)} %broadcast_in_dim.10), channel_id=1, replica_groups=mesh['dp'=8,'ctx'=4] {'ctx'}, dimensions={0} | all-to-all | bytes 1048576 | tf_op jit(solution)/shard_map/all_to_all | solution.py:535
  46.5 2.2 collective-permute-start
  48.8 0.8 collective-permute-start.1
  49.5 3.9 %collective-permute-start.2 = (bf16[4,6,256,128]{3,2,1,0:T(8,128)(2,1)}, bf16[4,6,256,128]{3,2,1,0:T(8,128)(2,1)S(1)}, u32[]{:S(2)}, u32[]{:S(2)}) collective-permute-start(bf16[4,6,256,128]{3,2,1,0:T(8,128)(2,1)} %get-tuple-element.47.own_ref), channel_id=1, source_target_pairs={{0,2},{3,1},{4,6},{7,5},{8,10},{11,9},{12,14},{15,13},{16,18},{19,... | collective-permute-start | bytes 4718600 | tf_op jit(solution)/shard_map/ppermute | solution.py:557
  53.5 30.4 %collective-permute-done.far_ref = bf16[4,6,256,128]{3,2,1,0:T(8,128)(2,1)S(1)} collective-permute-done((bf16[4,6,256,128]{3,2,1,0:T(8,128)(2,1)}, bf16[4,6,256,128]{3,2,1,0:T(8,128)(2,1)S(1)}, u32[]{:S(2)}, u32[]{:S(2)}) %collective-permute-start) | collective-permute-done | bytes 1572896 | tf_op jit(solution)/shard_map/ppermute | solution.py:557
  83.8 5.4 %collective-permute-start.3 = (bf16[4,6,256,128]{3,2,1,0:T(8,128)(2,1)S(1)}, bf16[4,6,256,128]{3,2,1,0:T(8,128)(2,1)}, u32[]{:S(2)}, u32[]{:S(2)}) collective-permute-start(bf16[4,6,256,128]{3,2,1,0:T(8,128)(2,1)S(1)} %copy-done), channel_id=1, source_target_pairs={{0,1},{3,2},{4,5},{7,6},{8,9},{11,10},{12,13},{15,14},{16,17},{19,... | collective-permute-start | bytes 4718600 | tf_op jit(solution)/shard_map/ppermute | solution.py:557
  89.2 1.8 collective-permute-start.4
  91.1 26.5 %collective-permute-done.2.other_far_ref = bf16[4,6,256,128]{3,2,1,0:T(8,128)(2,1)S(1)} collective-permute-done((bf16[4,6,256,128]{3,2,1,0:T(8,128)(2,1)}, bf16[4,6,256,128]{3,2,1,0:T(8,128)(2,1)S(1)}, u32[]{:S(2)}, u32[]{:S(2)}) %collective-permute-start.2) | collective-permute-done | bytes 1572896 | tf_op jit(solution)/shard_map/ppermute | solution.py:557
  117.6 1.2 copy-done.3
  118.8 7.8 %collective-permute-start.5 = (bf16[4,6,256,128]{3,2,1,0:T(8,128)(2,1)S(1)}, bf16[4,6,256,128]{3,2,1,0:T(8,128)(2,1)}, u32[]{:S(2)}, u32[]{:S(2)}) collective-permute-start(bf16[4,6,256,128]{3,2,1,0:T(8,128)(2,1)S(1)} %copy-done), channel_id=1, source_target_pairs={{0,2},{3,1},{4,6},{7,5},{8,10},{11,9},{12,14},{15,13},{16,18},{19,... | collective-permute-start | bytes 4718600 | tf_op jit(solution)/shard_map/ppermute | solution.py:557
  126.6 35.7 %shard_map.165 = (bf16[4,6,256,128]{3,2,1,0:T(8,128)(2,1)}, bf16[4,6,256,128]{3,2,1,0:T(8,128)(2,1)}, bf16[4,6,256,128]{3,2,1,0:T(8,128)(2,1)}, bf16[8,4,6,32,128]{4,3,2,1,0:T(8,128)(2,1)}) custom-call(f32[1]{0:T(128)} %bitcast.side_ref, bf16[4,6,256,128]{3,2,1,0:T(8,128)(2,1)} %get-tuple-element.47.own_ref, bf16[4,6,256,128]{3,2,1,0:T(8,128)(2,1)} %copy-done.1, ...), custom_call_target="tpu_custom_call" | custom-call | flops 1 | bytes 1 | tf_op jit(solution)/shard_map/pallas_call | solution.py:379
  162.3 3.7 %all-to-all-start.1 = ((bf16[8,4,6,32,128]{4,3,2,1,0:T(8,128)(2,1)}), bf16[8,4,6,32,128]{4,3,2,1,0:T(8,128)(2,1)S(1)}, u32[]{:S(2)}, u32[]{:S(2)}) async-start(bf16[8,4,6,32,128]{4,3,2,1,0:T(8,128)(2,1)} %get-tuple-element.60), calls=%async_computation.1 | async-start | bytes 3145728 | tf_op jit(solution)/shard_map/all_to_all | solution.py:539
  166.0 1.3 collective-permute-start.6
  167.4 15.1 %collective-permute-done.5.other_far_ref = bf16[4,6,256,128]{3,2,1,0:T(8,128)(2,1)} collective-permute-done((bf16[4,6,256,128]{3,2,1,0:T(8,128)(2,1)S(1)}, bf16[4,6,256,128]{3,2,1,0:T(8,128)(2,1)}, u32[]{:S(2)}, u32[]{:S(2)}) %collective-permute-start.5) | collective-permute-done | bytes 1572896 | tf_op jit(solution)/shard_map/ppermute | solution.py:557
  182.5 35.7 %shard_map.166 = (bf16[4,6,256,128]{3,2,1,0:T(8,128)(2,1)}, bf16[4,6,256,128]{3,2,1,0:T(8,128)(2,1)}, bf16[4,6,256,128]{3,2,1,0:T(8,128)(2,1)}, bf16[8,4,6,32,128]{4,3,2,1,0:T(8,128)(2,1)}) custom-call(f32[1]{0:T(128)} %bitcast.side_ref, bf16[4,6,256,128]{3,2,1,0:T(8,128)(2,1)} %get-tuple-element.55.own_ref, ...), custom_call_target="tpu_custom_call" | custom-call | flops 1 | bytes 1 | tf_op jit(solution)/shard_map/pallas_call | solution.py:379
  218.2 1.3 collective-permute-start.10
  219.5 3.7 all-to-all-start.2
  223.2 6.9 %collective-permute-start.7 = (bf16[4,2,256,128]{3,2,1,0:T(8,128)(2,1)}, bf16[4,2,256,128]{3,2,1,0:T(8,128)(2,1)S(1)}, u32[]{:S(2)}, u32[]{:S(2)}) collective-permute-start(bf16[4,2,256,128]{3,2,1,0:T(8,128)(2,1)} %get-tuple-element.64.own_ref), channel_id=1, source_target_pairs={{0,1},{3,2},{4,5},{7,6},{8,9},{11,10},{12,13},{15,14},{16,17},{19,... | collective-permute-start | bytes 1572872 | tf_op jit(solution)/shard_map/ppermute | solution.py:557
  230.1 0.7 collective-permute-start.8
  230.8 4.0 %collective-permute-start.9 = (bf16[4,2,256,128]{3,2,1,0:T(8,128)(2,1)}, bf16[4,2,256,128]{3,2,1,0:T(8,128)(2,1)S(1)}, u32[]{:S(2)}, u32[]{:S(2)}) collective-permute-start(bf16[4,2,256,128]{3,2,1,0:T(8,128)(2,1)} %get-tuple-element.64.own_ref), channel_id=1, source_target_pairs={{0,2},{3,1},{4,6},{7,5},{8,10},{11,9},{12,14},{15,13},{16,18},{19,... | collective-permute-start | bytes 1572872 | tf_op jit(solution)/shard_map/ppermute | solution.py:557
  234.7 7.8 %collective-permute-done.7.far_ref = bf16[4,2,256,128]{3,2,1,0:T(8,128)(2,1)S(1)} collective-permute-done((bf16[4,2,256,128]{3,2,1,0:T(8,128)(2,1)}, bf16[4,2,256,128]{3,2,1,0:T(8,128)(2,1)S(1)}, u32[]{:S(2)}, u32[]{:S(2)}) %collective-permute-start.7) | collective-permute-done | bytes 524320 | tf_op jit(solution)/shard_map/ppermute | solution.py:557
  242.6 5.1 %collective-permute-start.11 = (bf16[4,2,256,128]{3,2,1,0:T(8,128)(2,1)}, bf16[4,2,256,128]{3,2,1,0:T(8,128)(2,1)}, u32[]{:S(2)}, u32[]{:S(2)}) collective-permute-start(bf16[4,2,256,128]{3,2,1,0:T(8,128)(2,1)} %get-tuple-element.73.own_ref), channel_id=1, source_target_pairs={{0,1},{3,2},{4,5},{7,6},{8,9},{11,10},{12,13},{15,14},{16,17},{19,... | collective-permute-start | bytes 1572872 | tf_op jit(solution)/shard_map/ppermute | solution.py:557
  247.7 1.5 collective-permute-start.12
  249.1 4.7 %collective-permute-done.9.other_far_ref = bf16[4,2,256,128]{3,2,1,0:T(8,128)(2,1)S(1)} collective-permute-done((bf16[4,2,256,128]{3,2,1,0:T(8,128)(2,1)}, bf16[4,2,256,128]{3,2,1,0:T(8,128)(2,1)S(1)}, u32[]{:S(2)}, u32[]{:S(2)}) %collective-permute-start.9) | collective-permute-done | bytes 524320 | tf_op jit(solution)/shard_map/ppermute | solution.py:557
  253.8 0.8 copy-done.8
  254.6 9.3 %collective-permute-start.13 = (bf16[4,2,256,128]{3,2,1,0:T(8,128)(2,1)}, bf16[4,2,256,128]{3,2,1,0:T(8,128)(2,1)}, u32[]{:S(2)}, u32[]{:S(2)}) collective-permute-start(bf16[4,2,256,128]{3,2,1,0:T(8,128)(2,1)} %get-tuple-element.73.own_ref), channel_id=1, source_target_pairs={{0,2},{3,1},{4,6},{7,5},{8,10},{11,9},{12,14},{15,13},{16,18},{19,... | collective-permute-start | bytes 1572872 | tf_op jit(solution)/shard_map/ppermute | solution.py:557
  264.0 0.3 reduce_sum.48
  264.2 0.3 reduce_sum.49
  264.5 13.7 %shard_map.167 = (bf16[4,2,256,128]{3,2,1,0:T(8,128)(2,1)}, bf16[4,2,256,128]{3,2,1,0:T(8,128)(2,1)}, bf16[4,2,256,128]{3,2,1,0:T(8,128)(2,1)}, bf16[8,4,2,32,128]{4,3,2,1,0:T(8,128)(2,1)}) custom-call(f32[1]{0:T(128)} %bitcast.side_ref, bf16[4,2,256,128]{3,2,1,0:T(8,128)(2,1)} %get-tuple-element.64.own_ref, bf16[4,2,256,128]{3,2,1,0:T(8,128)(2,1)} %copy-done.6, ...), custom_call_target="tpu_custom_call" | custom-call | flops 1 | bytes 1 | tf_op jit(solution)/shard_map/pallas_call | solution.py:379
  278.2 1.4 collective-permute-start.14
  279.6 13.7 %shard_map.168 = (bf16[4,2,256,128]{3,2,1,0:T(8,128)(2,1)}, bf16[4,2,256,128]{3,2,1,0:T(8,128)(2,1)}, bf16[4,2,256,128]{3,2,1,0:T(8,128)(2,1)}, bf16[8,4,2,32,128]{4,3,2,1,0:T(8,128)(2,1)}) custom-call(f32[1]{0:T(128)} %bitcast.side_ref, bf16[4,2,256,128]{3,2,1,0:T(8,128)(2,1)} %get-tuple-element.73.own_ref, ...), custom_call_target="tpu_custom_call" | custom-call | flops 1 | bytes 1 | tf_op jit(solution)/shard_map/pallas_call | solution.py:379
  293.3 2.2 pad_maximum_fusion
  295.5 4.5 %all-to-all-start.3 = ((bf16[8,4,4,32,128]{4,3,2,1,0:T(8,128)(2,1)}), bf16[8,4,4,32,128]{4,3,2,1,0:T(8,128)(2,1)S(1)}, u32[]{:S(2)}, u32[]{:S(2)}) async-start(bf16[8,4,4,32,128]{4,3,2,1,0:T(8,128)(2,1)} %pad_maximum_fusion), calls=%async_computation.3 | async-start | bytes 2097152 | tf_op jit(solution)/shard_map/all_to_all | solution.py:539
  300.0 1.3 collective-permute-start.15
  301.3 14.1 %all-to-all-done.3 = bf16[8,4,4,32,128]{4,3,2,1,0:T(8,128)(2,1)S(1)} async-done(((bf16[8,4,4,32,128]{4,3,2,1,0:T(8,128)(2,1)}), bf16[8,4,4,32,128]{4,3,2,1,0:T(8,128)(2,1)S(1)}, u32[]{:S(2)}, u32[]{:S(2)}) %all-to-all-start.3) | async-done | bytes 1048608 | tf_op jit(solution)/shard_map/all_to_all | solution.py:539
  315.4 0.2 reduce_sum.50
  315.6 1.8 collective-permute-done.15.refs_11_
  317.4 17.5 %all_to_all.31 = bf16[4,16,32,128]{3,2,1,0:T(8,128)(2,1)S(1)} all-to-all(bf16[4,16,32,128]{3,2,1,0:T(8,128)(2,1)S(1)} %pad_maximum_fusion.1), channel_id=1, replica_groups=mesh['dp'=8,'ctx'=4] {'ctx'}, dimensions={0} | all-to-all | bytes 1048576 | tf_op jit(solution)/shard_map/all_to_all | solution.py:543
  335.0 1.2 broadcast_in_dim.11
  336.2 3.7 all-to-all-start.5
  339.9 0.7 copy.22.skip_ref
  340.6 23.0 %shard_map.169 = (bf16[64,32768]{1,0:T(8,128)(2,1)}, bf16[64,32768]{1,0:T(8,128)(2,1)}, bf16[64,32768]{1,0:T(8,128)(2,1)}, bf16[64,32768]{1,0:T(8,128)(2,1)}) custom-call(f32[1]{0:T(128)} %bitcast.side_ref, f32[64,1]{1,0:T(8,128)} %copy.22.skip_ref, bf16[64,32768]{1,0:T(8,128)(2,1)} %gate_ref.3, bf16[64,32768]{1,0:T(8,128)(2,1)} %values_ref.3, ...), custom_call_target="tpu_custom_call" | custom-call | flops 25165824 | bytes 46137344 | tf_op jit(solution)/shard_map/pallas_call | solution.py:479
  363.6 0.3 convert_bitcast_fusion
  363.9 0.2 copy.23
  364.1 2.7 fusion
  (46 shorter events, 0.4 us)
Async XLA Ops:
  7.2 119.4 %all-gather.2.cloned.1.call-start = ((), (), s32[]{:S(2)}) async-start(), calls=%async_computation.6 | async-start | bytes 4718592 | tf_op jit(solution)/shard_map/all_gather | solution.py:536
  25.6 58.2 %copy-start = (bf16[4,6,256,128]{3,2,1,0:T(8,128)(2,1)S(1)}, bf16[4,6,256,128]{3,2,1,0:T(8,128)(2,1)}, u32[]{:S(2)}) copy-start(bf16[4,6,256,128]{3,2,1,0:T(8,128)(2,1)} %get-tuple-element.55.own_ref) | copy-start | bytes 4718596
  46.5 37.3 %collective-permute-start = (bf16[4,6,256,128]{3,2,1,0:T(8,128)(2,1)}, bf16[4,6,256,128]{3,2,1,0:T(8,128)(2,1)S(1)}, u32[]{:S(2)}, u32[]{:S(2)}) collective-permute-start(bf16[4,6,256,128]{3,2,1,0:T(8,128)(2,1)} %get-tuple-element.47.own_ref), channel_id=1, source_target_pairs={{0,1},{3,2},{4,5},{7,6},{8,9},{11,10},{12,13},{15,14},{16,17},{19,... | collective-permute-start | bytes 4718600 | tf_op jit(solution)/shard_map/ppermute | solution.py:557
  48.8 40.5 %collective-permute-start.1 = (bf16[4,6,256,128]{3,2,1,0:T(8,128)(2,1)}, bf16[4,6,256,128]{3,2,1,0:T(8,128)(2,1)S(1)}, u32[]{:S(2)}, u32[]{:S(2)}) collective-permute-start(bf16[4,6,256,128]{3,2,1,0:T(8,128)(2,1)} %get-tuple-element.47.own_ref), channel_id=1, source_target_pairs={{1,2},{2,1},{5,6},{6,5},{9,10},{10,9},{13,14},{14,13},{17,18},{18,... | collective-permute-start | bytes 4718600 | tf_op jit(solution)/shard_map/ppermute | solution.py:557
  49.5 68.0 %collective-permute-start.2 = (bf16[4,6,256,128]{3,2,1,0:T(8,128)(2,1)}, bf16[4,6,256,128]{3,2,1,0:T(8,128)(2,1)S(1)}, u32[]{:S(2)}, u32[]{:S(2)}) collective-permute-start(bf16[4,6,256,128]{3,2,1,0:T(8,128)(2,1)} %get-tuple-element.47.own_ref), channel_id=1, source_target_pairs={{0,2},{3,1},{4,6},{7,5},{8,10},{11,9},{12,14},{15,13},{16,18},{19,... | collective-permute-start | bytes 4718600 | tf_op jit(solution)/shard_map/ppermute | solution.py:557
  83.8 42.8 %copy-start.1 = (bf16[4,6,256,128]{3,2,1,0:T(8,128)(2,1)}, bf16[4,6,256,128]{3,2,1,0:T(8,128)(2,1)S(1)}, u32[]{:S(2)}) copy-start(bf16[4,6,256,128]{3,2,1,0:T(8,128)(2,1)S(1)} %collective-permute-done.far_ref) | copy-start | bytes 4718596
  83.8 83.5 %collective-permute-start.3 = (bf16[4,6,256,128]{3,2,1,0:T(8,128)(2,1)S(1)}, bf16[4,6,256,128]{3,2,1,0:T(8,128)(2,1)}, u32[]{:S(2)}, u32[]{:S(2)}) collective-permute-start(bf16[4,6,256,128]{3,2,1,0:T(8,128)(2,1)S(1)} %copy-done), channel_id=1, source_target_pairs={{0,1},{3,2},{4,5},{7,6},{8,9},{11,10},{12,13},{15,14},{16,17},{19,... | collective-permute-start | bytes 4718600 | tf_op jit(solution)/shard_map/ppermute | solution.py:557
  89.2 1.8 copy-start.2
  89.2 78.1 %collective-permute-start.4 = (bf16[4,6,256,128]{3,2,1,0:T(8,128)(2,1)S(1)}, bf16[4,6,256,128]{3,2,1,0:T(8,128)(2,1)}, u32[]{:S(2)}, u32[]{:S(2)}) collective-permute-start(bf16[4,6,256,128]{3,2,1,0:T(8,128)(2,1)S(1)} %copy-done), channel_id=1, source_target_pairs={{1,2},{2,1},{5,6},{6,5},{9,10},{10,9},{13,14},{14,13},{17,18},{18,... | collective-permute-start | bytes 4718600 | tf_op jit(solution)/shard_map/ppermute | solution.py:557
  117.6 1.2 copy-start.3
  118.8 63.6 %collective-permute-start.5 = (bf16[4,6,256,128]{3,2,1,0:T(8,128)(2,1)S(1)}, bf16[4,6,256,128]{3,2,1,0:T(8,128)(2,1)}, u32[]{:S(2)}, u32[]{:S(2)}) collective-permute-start(bf16[4,6,256,128]{3,2,1,0:T(8,128)(2,1)S(1)} %copy-done), channel_id=1, source_target_pairs={{0,2},{3,1},{4,6},{7,5},{8,10},{11,9},{12,14},{15,13},{16,18},{19,... | collective-permute-start | bytes 4718600 | tf_op jit(solution)/shard_map/ppermute | solution.py:557
  162.3 57.2 %all-to-all-start.1 = ((bf16[8,4,6,32,128]{4,3,2,1,0:T(8,128)(2,1)}), bf16[8,4,6,32,128]{4,3,2,1,0:T(8,128)(2,1)S(1)}, u32[]{:S(2)}, u32[]{:S(2)}) async-start(bf16[8,4,6,32,128]{4,3,2,1,0:T(8,128)(2,1)} %get-tuple-element.60), calls=%async_computation.1 | async-start | bytes 3145728 | tf_op jit(solution)/shard_map/all_to_all | solution.py:539
  166.0 98.4 %collective-permute-start.6 = (bf16[4,6,256,128]{3,2,1,0:T(8,128)(2,1)}, bf16[4,6,256,128]{3,2,1,0:T(8,128)(2,1)}, u32[]{:S(2)}, u32[]{:S(2)}) collective-permute-start(bf16[4,6,256,128]{3,2,1,0:T(8,128)(2,1)} %get-tuple-element.59), channel_id=1, source_target_pairs={{1,0},{2,3},{5,4},{6,7},{9,8},{10,11},{13,12},{14,15},{17,16},{18,... | collective-permute-start | bytes 4718600 | tf_op jit(solution)/shard_map/ppermute | solution.py:578
  218.2 60.0 %collective-permute-start.10 = (bf16[4,6,256,128]{3,2,1,0:T(8,128)(2,1)}, bf16[4,6,256,128]{3,2,1,0:T(8,128)(2,1)}, u32[]{:S(2)}, u32[]{:S(2)}) collective-permute-start(bf16[4,6,256,128]{3,2,1,0:T(8,128)(2,1)} %get-tuple-element.68), channel_id=1, source_target_pairs={{1,0},{2,3},{5,4},{6,7},{9,8},{10,11},{13,12},{14,15},{17,16},{18,... | collective-permute-start | bytes 4718600 | tf_op jit(solution)/shard_map/ppermute | solution.py:578
  219.5 44.8 %all-to-all-start.2 = ((bf16[8,4,6,32,128]{4,3,2,1,0:T(8,128)(2,1)}), bf16[8,4,6,32,128]{4,3,2,1,0:T(8,128)(2,1)S(1)}, u32[]{:S(2)}, u32[]{:S(2)}) async-start(bf16[8,4,6,32,128]{4,3,2,1,0:T(8,128)(2,1)} %get-tuple-element.69), calls=%async_computation.2 | async-start | bytes 3145728 | tf_op jit(solution)/shard_map/all_to_all | solution.py:539
  223.2 19.4 %collective-permute-start.7 = (bf16[4,2,256,128]{3,2,1,0:T(8,128)(2,1)}, bf16[4,2,256,128]{3,2,1,0:T(8,128)(2,1)S(1)}, u32[]{:S(2)}, u32[]{:S(2)}) collective-permute-start(bf16[4,2,256,128]{3,2,1,0:T(8,128)(2,1)} %get-tuple-element.64.own_ref), channel_id=1, source_target_pairs={{0,1},{3,2},{4,5},{7,6},{8,9},{11,10},{12,13},{15,14},{16,17},{19,... | collective-permute-start | bytes 1572872 | tf_op jit(solution)/shard_map/ppermute | solution.py:557
  230.1 17.6 %collective-permute-start.8 = (bf16[4,2,256,128]{3,2,1,0:T(8,128)(2,1)}, bf16[4,2,256,128]{3,2,1,0:T(8,128)(2,1)S(1)}, u32[]{:S(2)}, u32[]{:S(2)}) collective-permute-start(bf16[4,2,256,128]{3,2,1,0:T(8,128)(2,1)} %get-tuple-element.64.own_ref), channel_id=1, source_target_pairs={{1,2},{2,1},{5,6},{6,5},{9,10},{10,9},{13,14},{14,13},{17,18},{18,... | collective-permute-start | bytes 1572872 | tf_op jit(solution)/shard_map/ppermute | solution.py:557
  230.8 23.1 %collective-permute-start.9 = (bf16[4,2,256,128]{3,2,1,0:T(8,128)(2,1)}, bf16[4,2,256,128]{3,2,1,0:T(8,128)(2,1)S(1)}, u32[]{:S(2)}, u32[]{:S(2)}) collective-permute-start(bf16[4,2,256,128]{3,2,1,0:T(8,128)(2,1)} %get-tuple-element.64.own_ref), channel_id=1, source_target_pairs={{0,2},{3,1},{4,6},{7,5},{8,10},{11,9},{12,14},{15,13},{16,18},{19,... | collective-permute-start | bytes 1572872 | tf_op jit(solution)/shard_map/ppermute | solution.py:557
  242.6 11.3 %copy-start.6 = (bf16[4,2,256,128]{3,2,1,0:T(8,128)(2,1)}, bf16[4,2,256,128]{3,2,1,0:T(8,128)(2,1)S(1)}, u32[]{:S(2)}) copy-start(bf16[4,2,256,128]{3,2,1,0:T(8,128)(2,1)S(1)} %collective-permute-done.7.far_ref) | copy-start | bytes 1572868
  242.6 37.1 %collective-permute-start.11 = (bf16[4,2,256,128]{3,2,1,0:T(8,128)(2,1)}, bf16[4,2,256,128]{3,2,1,0:T(8,128)(2,1)}, u32[]{:S(2)}, u32[]{:S(2)}) collective-permute-start(bf16[4,2,256,128]{3,2,1,0:T(8,128)(2,1)} %get-tuple-element.73.own_ref), channel_id=1, source_target_pairs={{0,1},{3,2},{4,5},{7,6},{8,9},{11,10},{12,13},{15,14},{16,17},{19,... | collective-permute-start | bytes 1572872 | tf_op jit(solution)/shard_map/ppermute | solution.py:557
  247.7 6.2 %copy-start.7 = (bf16[4,2,256,128]{3,2,1,0:T(8,128)(2,1)}, bf16[4,2,256,128]{3,2,1,0:T(8,128)(2,1)S(1)}, u32[]{:S(2)}) copy-start(bf16[4,2,256,128]{3,2,1,0:T(8,128)(2,1)S(1)} %collective-permute-done.8.other_next_ref) | copy-start | bytes 1572868
  247.7 32.0 %collective-permute-start.12 = (bf16[4,2,256,128]{3,2,1,0:T(8,128)(2,1)}, bf16[4,2,256,128]{3,2,1,0:T(8,128)(2,1)}, u32[]{:S(2)}, u32[]{:S(2)}) collective-permute-start(bf16[4,2,256,128]{3,2,1,0:T(8,128)(2,1)} %get-tuple-element.73.own_ref), channel_id=1, source_target_pairs={{1,2},{2,1},{5,6},{6,5},{9,10},{10,9},{13,14},{14,13},{17,18},{18,... | collective-permute-start | bytes 1572872 | tf_op jit(solution)/shard_map/ppermute | solution.py:557
  253.8 0.8 copy-start.8
  254.6 25.0 %collective-permute-start.13 = (bf16[4,2,256,128]{3,2,1,0:T(8,128)(2,1)}, bf16[4,2,256,128]{3,2,1,0:T(8,128)(2,1)}, u32[]{:S(2)}, u32[]{:S(2)}) collective-permute-start(bf16[4,2,256,128]{3,2,1,0:T(8,128)(2,1)} %get-tuple-element.73.own_ref), channel_id=1, source_target_pairs={{0,2},{3,1},{4,6},{7,5},{8,10},{11,9},{12,14},{15,13},{16,18},{19,... | collective-permute-start | bytes 1572872 | tf_op jit(solution)/shard_map/ppermute | solution.py:557
  278.2 15.1 %copy-start.9 = (bf16[8,4,2,32,128]{4,3,2,1,0:T(8,128)(2,1)S(1)}, bf16[8,4,2,32,128]{4,3,2,1,0:T(8,128)(2,1)}, u32[]{:S(2)}) copy-start(bf16[8,4,2,32,128]{4,3,2,1,0:T(8,128)(2,1)} %get-tuple-element.86) | copy-start | bytes 1572868
  278.2 21.8 %collective-permute-start.14 = (bf16[4,2,256,128]{3,2,1,0:T(8,128)(2,1)}, bf16[4,2,256,128]{3,2,1,0:T(8,128)(2,1)S(1)}, u32[]{:S(2)}, u32[]{:S(2)}) collective-permute-start(bf16[4,2,256,128]{3,2,1,0:T(8,128)(2,1)} %get-tuple-element.79), channel_id=1, source_target_pairs={{1,0},{2,3},{5,4},{6,7},{9,8},{10,11},{13,12},{14,15},{17,16},{18,... | collective-permute-start | bytes 1572872 | tf_op jit(solution)/shard_map/ppermute | solution.py:578
  293.3 6.7 %copy-start.11 = (bf16[4,2,256,128]{3,2,1,0:T(8,128)(2,1)S(1)}, bf16[4,2,256,128]{3,2,1,0:T(8,128)(2,1)}, u32[]{:S(2)}) copy-start(bf16[4,2,256,128]{3,2,1,0:T(8,128)(2,1)} %get-tuple-element.81) | copy-start | bytes 1572868
  295.5 19.9 %all-to-all-start.3 = ((bf16[8,4,4,32,128]{4,3,2,1,0:T(8,128)(2,1)}), bf16[8,4,4,32,128]{4,3,2,1,0:T(8,128)(2,1)S(1)}, u32[]{:S(2)}, u32[]{:S(2)}) async-start(bf16[8,4,4,32,128]{4,3,2,1,0:T(8,128)(2,1)} %pad_maximum_fusion), calls=%async_computation.3 | async-start | bytes 2097152 | tf_op jit(solution)/shard_map/all_to_all | solution.py:539
  300.0 36.1 %copy-start.4 = (bf16[4,2,256,128]{3,2,1,0:T(8,128)(2,1)}, bf16[4,2,256,128]{3,2,1,0:T(8,128)(2,1)S(1)}, u32[]{:S(2)}) copy-start(bf16[4,2,256,128]{3,2,1,0:T(8,128)(2,1)S(1)} %collective-permute-done.14.refs_10_) | copy-start | bytes 1572868
  300.0 17.3 %collective-permute-start.15 = (bf16[4,2,256,128]{3,2,1,0:T(8,128)(2,1)S(1)}, bf16[4,2,256,128]{3,2,1,0:T(8,128)(2,1)S(1)}, u32[]{:S(2)}, u32[]{:S(2)}) collective-permute-start(bf16[4,2,256,128]{3,2,1,0:T(8,128)(2,1)S(1)} %copy-done.11), channel_id=1, source_target_pairs={{1,0},{2,3},{5,4},{6,7},{9,8},{10,11},{13,12},{14,15},{17,16},{18,... | collective-permute-start | bytes 1572872 | tf_op jit(solution)/shard_map/ppermute | solution.py:578
  317.4 18.8 %copy-start.5 = (bf16[4,2,256,128]{3,2,1,0:T(8,128)(2,1)}, bf16[4,2,256,128]{3,2,1,0:T(8,128)(2,1)S(1)}, u32[]{:S(2)}) copy-start(bf16[4,2,256,128]{3,2,1,0:T(8,128)(2,1)S(1)} %collective-permute-done.15.refs_11_) | copy-start | bytes 1572868
  334.9 5.0 %copy-start.12 = (f32[16]{0:T(128)S(1)}, f32[16]{0:T(128)}, u32[]{:S(2)}) copy-start(f32[16]{0:T(128)} %param.18) | copy-start | bytes 196
  334.9 5.0 %copy-start.10 = (f32[64]{0:T(128)S(1)}, f32[64]{0:T(128)}, u32[]{:S(2)}) copy-start(f32[64]{0:T(128)} %param.19) | copy-start | bytes 772
  336.2 27.4 %all-to-all-start.5 = ((bf16[8,16,32,128]{3,2,1,0:T(8,128)(2,1)}), bf16[8,16,32,128]{3,2,1,0:T(8,128)(2,1)S(1)}, u32[]{:S(2)}, u32[]{:S(2)}) async-start(bf16[8,16,32,128]{3,2,1,0:T(8,128)(2,1)} %broadcast_in_dim.11), calls=%async_computation.5 | async-start | bytes 2097152 | tf_op jit(solution)/shard_map/all_to_all | solution.py:546
Sparse Core Ops, SparseCore 0:
  46.7 35.8 all-gather.1

commit v2 on v1

--- a/solution.py
+++ b/solution.py
@@ -192,7 +192,7 @@
 
 
 LANES = 128
-SHARES = (6, 6, 2, 2)
+SHARES = (5, 5, 3, 3)
 STRIP = 16
 EDGE_ROWS = 16
 VMEM_BYTES = 60 * 2**20
@@ -499,8 +499,8 @@
     )(side, skip_gain[:, None], *flat, *parts)
 
 
-def after(array, *earlier):
-    return lax.optimization_barrier((array, *earlier))[0]
+def rotation(hop):
+    return [(index, (index + hop) % 4) for index in range(4)]
 
 
 def block_shards(input_gate, output_gate, values, cotangent, filter_raw, filter_decay, skip_gain):
@@ -530,9 +530,10 @@
     taps = (raw_share.astype(jnp.float32) * envelope(decay_share) * filter_scale).astype(
         jnp.bfloat16
     )
-    taps = after(taps.reshape(1, share, rows, LANES), own_parts[0])
-    taps = jnp.broadcast_to(taps, (4, share, rows, LANES))
-    taps = lax.all_to_all(taps, "ctx", split_axis=0, concat_axis=0, tiled=True)
+    taps = taps.reshape(1, share, rows, LANES)
+    turned = [taps] + [lax.ppermute(taps, "ctx", rotation(hop)) for hop in (1, 2, 3)]
+    turned = jnp.concatenate(turned[::-1] + turned[:0:-1], axis=0)
+    taps = lax.dynamic_slice_in_dim(turned, 3 - context_index, 4, 0)
     taps = lax.all_gather(taps, "dp", axis=1, tiled=True)
 
     def lag_shares(pieces):
@@ -540,46 +541,49 @@
         return jnp.sum(pieces.astype(jnp.float32), axis=0).astype(jnp.bfloat16)
 
     def lag_sum(pieces):
-        pieces = lax.all_to_all(pieces, "ctx", split_axis=0, concat_axis=0, tiled=True)
-        total = jnp.sum(pieces.astype(jnp.float32), axis=0).astype(jnp.bfloat16)
+        def block(index):
+            return lax.dynamic_index_in_dim(pieces, index, 0, keepdims=False)
+
+        total = block(context_index).astype(jnp.float32)
+        for hop in (1, 2, 3):
+            leaving = block((context_index + hop) % 4)
+            total += lax.ppermute(leaving, "ctx", rotation(hop)).astype(jnp.float32)
+        total = total.astype(jnp.bfloat16)
         spread = jnp.broadcast_to(total[None], (data_size, *total.shape))
         spread = lax.all_to_all(spread, "dp", split_axis=0, concat_axis=0, tiled=True)
         return jnp.transpose(spread, (1, 0, 2, 3)).reshape(total.shape[0], rows, LANES)
 
     routes = ([(1, 2), (2, 1)], [(0, 2), (3, 1)], [(0, 1), (3, 2)])
-    arrivals, near_parts, other_parts, received_parts, lag_parts = [], [], [], [], []
-
-    def send(number):
-        own, made = own_parts[number], []
-        for stream, route in enumerate(routes):
-            earlier = [arrivals[number - 1][stream]] if number else []
-            earlier += near_parts[number - 2 : number - 1] if number >= 2 else []
-            made.append(lax.ppermute(after(own, *earlier), "ctx", route))
-        arrivals.append(made)
-
-    start = 0
-    send(0)
+    back_route = [(1, 0), (2, 3)]
+    near_parts, other_parts, received_parts, lag_parts = [], [], [], []
+    arrivals = [lax.ppermute(own_parts[0], "ctx", route) for route in routes]
+    start, pending = 0, None
     for number, own in enumerate(own_parts):
-        if number + 1 < len(own_parts):
-            send(number + 1)
-        other_next, other_far, far = arrivals[number]
-        if number >= 1:
-            own = after(own, near_parts[number - 1])
-        if number >= 2:
-            own = after(own, received_parts[number - 2], lag_parts[number - 2])
-        near_out, other_out, passed, lag = block_products(
+        leaving = own_parts[number + 1] if number + 1 < len(own_parts) else None
+        arrivals, own, leaving, pending, received_parts, lag_parts, near_parts = (
+            lax.optimization_barrier(
+                (arrivals, own, leaving, pending, received_parts, lag_parts, near_parts)
+            )
+        )
+        other_next, other_far, far = arrivals
+        if leaving is not None:
+            arrivals = [lax.ppermute(leaving, "ctx", route) for route in routes]
+        if pending is not None:
+            received_parts.append(lax.ppermute(pending[0], "ctx", back_route))
+            lag_parts.append(lag_shares(pending[1]))
+        near_out, other_out, *pending = block_products(
             side, (own, far, other_next, other_far), other, taps, tables, start, data_size
         )
         start += own.shape[1]
         near_parts.append(near_out)
         other_parts.append(other_out)
-        if number == len(own_parts) - 1:
-            passed = after(passed, received_parts[number - 1])
-        received_parts.append(lax.ppermute(passed, "ctx", [(1, 0), (2, 3)]))
-        lag_parts.append(lag_shares(lag) if number < 2 else lag)
-    late = lag_shares(jnp.concatenate(lag_parts[2:], axis=2))
-    late = after(late, received_parts[-1])
-    lag = lag_sum(jnp.concatenate([*lag_parts[:2], late], axis=1)).reshape(filters, local_len)
+    pending, received_parts, lag_parts = lax.optimization_barrier(
+        (pending, received_parts, lag_parts)
+    )
+    received = lax.ppermute(pending[0], "ctx", back_route)
+    received, late = lax.optimization_barrier((received, lag_shares(pending[1])))
+    received_parts.append(received)
+    lag = lag_sum(jnp.concatenate([*lag_parts, late], axis=1)).reshape(filters, local_len)
     grad_filter = lag.astype(jnp.float32) * envelope(filter_decay) * filter_scale
     outputs, grad_input_gate, grad_output_gate, grad_values = leave(
         side, skip_gain, flat, near_parts, other_parts, received_parts

time: 375 us -> 365 us (0.973)
  blocking collectives: 38.3 us -> 0 us
  waiting for transfers between devices: 100 us -> 124 us
  starting transfers between devices: 70.3 us -> 75.4 us
    all_to_all x2 -> x0, blocking collectives: 38.3 us -> none  [the longest x1 20.8 us: block_shards(): taps = lax.all_to_all(taps, 'ctx', split_axis=0, concat_axis=0, tiled=True)]
    ppermute x16 -> x22, waiting for transfers between devices: 86.3 us -> 112 us  [the longest x3 53.8 us: block_shards(): arrivals = [lax.ppermute(own_parts[0], 'ctx', route) for route in routes]]
    all_to_all x3 -> x4, starting transfers between devices: 12 us -> 15.8 us  [lag_shares(): lax.all_to_all(pieces, 'dp', split_axis=0, concat_axis=0, tiled=True)]
    all_to_all x3 -> x4, waiting for transfers between devices: 14.1 us -> 12.5 us  [lag_shares(): lax.all_to_all(pieces, 'dp', split_axis=0, concat_axis=0, tiled=True)]
    ppermute x16 -> x22, starting transfers between devices: 54.6 us -> 56 us  [the longest x9 33.4 us: block_shards(): arrivals = [lax.ppermute(leaving, 'ctx', route) for route in routes]]
  transfers between devices with their start and end apart: 21 -> 28, of which waited for: 7 -> 11; matrix products, arithmetic and copies ran while one was open for 1% -> 1% of each run, Pallas kernels for 33% -> 38%
where the time goes in v2:
time: 365 us; the launch traced here: 363 us
  Pallas kernels  138 us (38%)
  waiting for transfers between devices  124 us (34%)
  starting transfers between devices  75.4 us (21%)
  between operations  14.5 us (4%)
  other arithmetic  7.2 us (2%)
    pallas_call x4, Pallas kernels, block_products(): pl.pallas_call(block_kernel, grid=(filters,), in_specs=[pl.BlockSpec(memo...  98.7 us
    ppermute x3, waiting for transfers between devices, block_shards(): arrivals = [lax.ppermute(own_parts[0], 'ctx', route) for route in routes]  53.8 us
    ppermute x9, starting transfers between devices, block_shards(): arrivals = [lax.ppermute(leaving, 'ctx', route) for route in routes]  33.4 us
    ppermute x9, waiting for transfers between devices, block_shards(): arrivals = [lax.ppermute(leaving, 'ctx', route) for route in routes]  32.9 us
    pallas_call x1, Pallas kernels, leave(): pl.pallas_call(leave_kernel, grid=(local_len // (EDGE_ROWS * LANES),), in...  22.8 us
    pallas_call x1, Pallas kernels, enter(): pl.pallas_call(enter_kernel, grid=(rows // EDGE_ROWS,), in_specs=[pl.Bloc...  16.4 us
    all_to_all x4, starting transfers between devices, lag_shares(): lax.all_to_all(pieces, 'dp', split_axis=0, concat_axis=0, tiled=True)  15.8 us
    all_to_all x4, waiting for transfers between devices, lag_shares(): lax.all_to_all(pieces, 'dp', split_axis=0, concat_axis=0, tiled=True)  12.5 us
  transfers between devices with their start and end apart: 28, of which 11 were waited for; matrix products, arithmetic and copies ran while one was open for 1% of the time, Pallas kernels for 38%

profile of v2, /device:TPU:0, one launch (start us, length us, event | category | flops | bytes accessed | tf_op | source)
XLA Modules:
  0.0 362.8 jit_solution(3362689024960508476)
XLA Ops:
  7.2 0.7 dynamic-slice_negate_fusion
  8.0 1.4 fusion.4
  9.4 5.1 %collective-permute-start.6 = (bf16[1,2,256,128]{3,2,1,0:T(8,128)(2,1)S(1)}, bf16[1,2,256,128]{3,2,1,0:T(8,128)(2,1)S(1)}, u32[]{:S(2)}, u32[]{:S(2)}) collective-permute-start(bf16[1,2,256,128]{3,2,1,0:T(8,128)(2,1)S(1)} %copy.28), channel_id=1, source_target_pairs={{0,3},{1,0},{2,1},{3,2},{4,7},{5,4},{6,5},{7,6},{8,11},{9,8},{10,9... | collective-permute-start | bytes 393224 | tf_op jit(solution)/shard_map/ppermute | solution.py:534
  14.5 1.0 collective-permute-start.8
  15.5 2.9 collective-permute-done.6
  18.4 7.3 %collective-permute-done.7 = bf16[1,2,256,128]{3,2,1,0:T(8,128)(2,1)S(1)} collective-permute-done((bf16[1,2,256,128]{3,2,1,0:T(8,128)(2,1)S(1)}, bf16[1,2,256,128]{3,2,1,0:T(8,128)(2,1)S(1)}, u32[]{:S(2)}, u32[]{:S(2)}) %collective-permute-start.7) | collective-permute-done | bytes 131104 | tf_op jit(solution)/shard_map/ppermute | solution.py:534
  25.9 0.9 constant_dynamic-slice_fusion
  26.8 16.4 %shard_map.164 = (bf16[4,5,256,128]{3,2,1,0:T(8,128)(2,1)}, bf16[4,5,256,128]{3,2,1,0:T(8,128)(2,1)}, bf16[4,3,256,128]{3,2,1,0:T(8,128)(2,1)}, bf16[4,3,256,128...) custom-call(f32[1]{0:T(128)} %bitcast.side_ref, bf16[64,32768]{1,0:T(8,128)(2,1)} %gate_ref.3, bf16[64,32768]{1,0:T(8,128)(2,1)} %values_ref.3, ...), custom_call_target="tpu_custom_call" | custom-call | flops 8388608 | bytes 25165824 | tf_op jit(solution)/shard_map/pallas_call | solution.py:424
  43.3 0.7 collective-permute-start
  44.0 5.7 %collective-permute-start.1 = (bf16[4,5,256,128]{3,2,1,0:T(8,128)(2,1)}, bf16[4,5,256,128]{3,2,1,0:T(8,128)(2,1)S(1)}, u32[]{:S(2)}, u32[]{:S(2)}) collective-permute-start(bf16[4,5,256,128]{3,2,1,0:T(8,128)(2,1)} %get-tuple-element.81.own_ref), channel_id=1, source_target_pairs={{0,2},{3,1},{4,6},{7,5},{8,10},{11,9},{12,14},{15,13},{16,18},{19,... | collective-permute-start | bytes 3932168 | tf_op jit(solution)/shard_map/ppermute | solution.py:559
  49.7 1.8 collective-permute-start.2
  51.6 27.6 %collective-permute-done.1.other_far_ref = bf16[4,5,256,128]{3,2,1,0:T(8,128)(2,1)S(1)} collective-permute-done((bf16[4,5,256,128]{3,2,1,0:T(8,128)(2,1)}, bf16[4,5,256,128]{3,2,1,0:T(8,128)(2,1)S(1)}, u32[]{:S(2)}, u32[]{:S(2)}) %collective-permute-start.1) | collective-permute-done | bytes 1310752 | tf_op jit(solution)/shard_map/ppermute | solution.py:559
  79.1 26.3 %collective-permute-done.2.far_ref = bf16[4,5,256,128]{3,2,1,0:T(8,128)(2,1)S(1)} collective-permute-done((bf16[4,5,256,128]{3,2,1,0:T(8,128)(2,1)}, bf16[4,5,256,128]{3,2,1,0:T(8,128)(2,1)S(1)}, u32[]{:S(2)}, u32[]{:S(2)}) %collective-permute-start.2) | collective-permute-done | bytes 1310752 | tf_op jit(solution)/shard_map/ppermute | solution.py:559
  105.4 0.7 collective-permute-start.3
  106.2 7.0 %collective-permute-start.4 = (bf16[4,5,256,128]{3,2,1,0:T(8,128)(2,1)}, bf16[4,5,256,128]{3,2,1,0:T(8,128)(2,1)S(1)}, u32[]{:S(2)}, u32[]{:S(2)}) collective-permute-start(bf16[4,5,256,128]{3,2,1,0:T(8,128)(2,1)} %get-tuple-element.91.own_ref), channel_id=1, source_target_pairs={{0,2},{3,1},{4,6},{7,5},{8,10},{11,9},{12,14},{15,13},{16,18},{19,... | collective-permute-start | bytes 3932168 | tf_op jit(solution)/shard_map/ppermute | solution.py:570
  113.2 2.6 collective-permute-start.5
  115.8 30.2 %shard_map.165 = (bf16[4,5,256,128]{3,2,1,0:T(8,128)(2,1)}, bf16[4,5,256,128]{3,2,1,0:T(8,128)(2,1)}, bf16[4,5,256,128]{3,2,1,0:T(8,128)(2,1)}, bf16[8,4,5,32,128]{4,3,2,1,0:T(8,128)(2,1)}) custom-call(f32[1]{0:T(128)} %bitcast.side_ref, bf16[4,5,256,128]{3,2,1,0:T(8,128)(2,1)} %get-tuple-element.81.own_ref, bf16[4,5,256,128]{3,2,1,0:T(8,128)(2,1)} %copy-done.5, ...), custom_call_target="tpu_custom_call" | custom-call | flops 1 | bytes 1 | tf_op jit(solution)/shard_map/pallas_call | solution.py:379
  146.1 21.7 %collective-permute-done.5.far_ref = bf16[4,5,256,128]{3,2,1,0:T(8,128)(2,1)} collective-permute-done((bf16[4,5,256,128]{3,2,1,0:T(8,128)(2,1)}, bf16[4,5,256,128]{3,2,1,0:T(8,128)(2,1)}, u32[]{:S(2)}, u32[]{:S(2)}) %collective-permute-start.5) | collective-permute-done | bytes 1310752 | tf_op jit(solution)/shard_map/ppermute | solution.py:570
  167.7 1.3 collective-permute-start.12
  169.0 3.7 %all-to-all-start = ((bf16[8,4,5,32,128]{4,3,2,1,0:T(8,128)(2,1)}), bf16[8,4,5,32,128]{4,3,2,1,0:T(8,128)(2,1)S(1)}, u32[]{:S(2)}, u32[]{:S(2)}) async-start(bf16[8,4,5,32,128]{4,3,2,1,0:T(8,128)(2,1)} %get-tuple-element.98), calls=%async_computation | async-start | bytes 2621440 | tf_op jit(solution)/shard_map/all_to_all | solution.py:540
  172.7 1.6 collective-permute-start.9
  174.3 7.3 %collective-permute-start.10 = (bf16[4,3,256,128]{3,2,1,0:T(8,128)(2,1)}, bf16[4,3,256,128]{3,2,1,0:T(8,128)(2,1)}, u32[]{:S(2)}, u32[]{:S(2)}) collective-permute-start(bf16[4,3,256,128]{3,2,1,0:T(8,128)(2,1)} %get-tuple-element.102.own_ref), channel_id=1, source_target_pairs={{0,2},{3,1},{4,6},{7,5},{8,10},{11,9},{12,14},{15,13},{16,18},{19,... | collective-permute-start | bytes 2359304 | tf_op jit(solution)/shard_map/ppermute | solution.py:570
  181.6 2.2 collective-permute-start.11
  183.8 30.2 %shard_map.166 = (bf16[4,5,256,128]{3,2,1,0:T(8,128)(2,1)}, bf16[4,5,256,128]{3,2,1,0:T(8,128)(2,1)}, bf16[4,5,256,128]{3,2,1,0:T(8,128)(2,1)}, bf16[8,4,5,32,128]{4,3,2,1,0:T(8,128)(2,1)}) custom-call(f32[1]{0:T(128)} %bitcast.side_ref, bf16[4,5,256,128]{3,2,1,0:T(8,128)(2,1)} %get-tuple-element.91.own_ref, ...), custom_call_target="tpu_custom_call" | custom-call | flops 1 | bytes 1 | tf_op jit(solution)/shard_map/pallas_call | solution.py:379
  214.1 0.9 reduce_sum.48
  215.1 1.3 collective-permute-start.16
  216.4 4.0 %all-to-all-start.1 = ((bf16[8,4,5,32,128]{4,3,2,1,0:T(8,128)(2,1)}), bf16[8,4,5,32,128]{4,3,2,1,0:T(8,128)(2,1)S(1)}, u32[]{:S(2)}, u32[]{:S(2)}) async-start(bf16[8,4,5,32,128]{4,3,2,1,0:T(8,128)(2,1)} %get-tuple-element.111), calls=%async_computation.1 | async-start | bytes 2621440 | tf_op jit(solution)/shard_map/all_to_all | solution.py:540
  220.5 1.6 collective-permute-start.13
  222.0 8.3 %collective-permute-start.14 = (bf16[4,3,256,128]{3,2,1,0:T(8,128)(2,1)S(1)}, bf16[4,3,256,128]{3,2,1,0:T(8,128)(2,1)}, u32[]{:S(2)}, u32[]{:S(2)}) collective-permute-start(bf16[4,3,256,128]{3,2,1,0:T(8,128)(2,1)S(1)} %copy-done.6), channel_id=1, source_target_pairs={{0,2},{3,1},{4,6},{7,5},{8,10},{11,9},{12,14},{15,13},{16,18},{19,... | collective-permute-start | bytes 2359304 | tf_op jit(solution)/shard_map/ppermute | solution.py:570
  230.3 2.2 collective-permute-start.15
  232.5 19.1 %shard_map.167 = (bf16[4,3,256,128]{3,2,1,0:T(8,128)(2,1)}, bf16[4,3,256,128]{3,2,1,0:T(8,128)(2,1)}, bf16[4,3,256,128]{3,2,1,0:T(8,128)(2,1)}, bf16[8,4,3,32,128]{4,3,2,1,0:T(8,128)(2,1)}) custom-call(f32[1]{0:T(128)} %bitcast.side_ref, bf16[4,3,256,128]{3,2,1,0:T(8,128)(2,1)} %get-tuple-element.102.own_ref, ...), custom_call_target="tpu_custom_call" | custom-call | flops 1 | bytes 1 | tf_op jit(solution)/shard_map/pallas_call | solution.py:379
  251.7 0.9 reduce_sum.49
  252.5 11.0 %collective-permute-done.15.far_ref = bf16[4,3,256,128]{3,2,1,0:T(8,128)(2,1)} collective-permute-done((bf16[4,3,256,128]{3,2,1,0:T(8,128)(2,1)S(1)}, bf16[4,3,256,128]{3,2,1,0:T(8,128)(2,1)}, u32[]{:S(2)}, u32[]{:S(2)}) %collective-permute-start.15) | collective-permute-done | bytes 786464 | tf_op jit(solution)/shard_map/ppermute | solution.py:570
  263.5 1.3 collective-permute-start.17
  264.8 3.9 %all-to-all-start.2 = ((bf16[8,4,3,32,128]{4,3,2,1,0:T(8,128)(2,1)}), bf16[8,4,3,32,128]{4,3,2,1,0:T(8,128)(2,1)S(1)}, u32[]{:S(2)}, u32[]{:S(2)}) async-start(bf16[8,4,3,32,128]{4,3,2,1,0:T(8,128)(2,1)} %get-tuple-element.134), calls=%async_computation.2 | async-start | bytes 1572864 | tf_op jit(solution)/shard_map/all_to_all | solution.py:540
  268.7 19.2 %shard_map.168 = (bf16[4,3,256,128]{3,2,1,0:T(8,128)(2,1)}, bf16[4,3,256,128]{3,2,1,0:T(8,128)(2,1)}, bf16[4,3,256,128]{3,2,1,0:T(8,128)(2,1)}, bf16[8,4,3,32,128]{4,3,2,1,0:T(8,128)(2,1)}) custom-call(f32[1]{0:T(128)} %bitcast.side_ref, bf16[4,3,256,128]{3,2,1,0:T(8,128)(2,1)} %get-tuple-element.118.own_ref, ...), custom_call_target="tpu_custom_call" | custom-call | flops 1 | bytes 1 | tf_op jit(solution)/shard_map/pallas_call | solution.py:379
  288.0 1.3 collective-permute-start.18
  289.3 4.2 %all-to-all-start.3 = ((bf16[8,4,3,32,128]{4,3,2,1,0:T(8,128)(2,1)}), bf16[8,4,3,32,128]{4,3,2,1,0:T(8,128)(2,1)S(1)}, u32[]{:S(2)}, u32[]{:S(2)}) async-start(bf16[8,4,3,32,128]{4,3,2,1,0:T(8,128)(2,1)} %get-tuple-element.139), calls=%async_computation.3 | async-start | bytes 1572864 | tf_op jit(solution)/shard_map/all_to_all | solution.py:540
  293.6 12.5 %all-to-all-done.3 = bf16[8,4,3,32,128]{4,3,2,1,0:T(8,128)(2,1)S(1)} async-done(((bf16[8,4,3,32,128]{4,3,2,1,0:T(8,128)(2,1)}), bf16[8,4,3,32,128]{4,3,2,1,0:T(8,128)(2,1)S(1)}, u32[]{:S(2)}, u32[]{:S(2)}) %all-to-all-start.3) | async-done | bytes 786464 | tf_op jit(solution)/shard_map/all_to_all | solution.py:540
  306.2 4.1 %collective-permute-done.18.refs_11_ = bf16[4,3,256,128]{3,2,1,0:T(8,128)(2,1)S(1)} collective-permute-done((bf16[4,3,256,128]{3,2,1,0:T(8,128)(2,1)}, bf16[4,3,256,128]{3,2,1,0:T(8,128)(2,1)S(1)}, u32[]{:S(2)}, u32[]{:S(2)}) %collective-permute-start.18) | collective-permute-done | bytes 786464 | tf_op jit(solution)/shard_map/ppermute | solution.py:583
  310.5 2.4 collective-permute-start.21
  313.5 3.3 collective-permute-done.21
  316.8 7.5 %collective-permute-done.20 = bf16[16,32,128]{2,1,0:T(8,128)(2,1)S(1)} collective-permute-done((bf16[16,32,128]{2,1,0:T(8,128)(2,1)S(1)}, bf16[16,32,128]{2,1,0:T(8,128)(2,1)S(1)}, u32[]{:S(2)}, u32[]{:S(2)}) %collective-permute-start.20) | collective-permute-done | bytes 131104 | tf_op jit(solution)/shard_map/ppermute | solution.py:550
  324.4 1.2 broadcast_in_dim.5
  325.6 3.6 all-to-all-start.4
  329.2 0.7 copy.20.skip_ref
  329.9 22.8 %shard_map.169 = (bf16[64,32768]{1,0:T(8,128)(2,1)}, bf16[64,32768]{1,0:T(8,128)(2,1)}, bf16[64,32768]{1,0:T(8,128)(2,1)}, bf16[64,32768]{1,0:T(8,128)(2,1)}) custom-call(f32[1]{0:T(128)} %bitcast.side_ref, f32[64,1]{1,0:T(8,128)} %copy.20.skip_ref, bf16[64,32768]{1,0:T(8,128)(2,1)} %gate_ref.3, bf16[64,32768]{1,0:T(8,128)(2,1)} %values_ref.3, ...), custom_call_target="tpu_custom_call" | custom-call | flops 25165824 | bytes 46137344 | tf_op jit(solution)/shard_map/pallas_call | solution.py:479
  353.2 2.7 fusion
  (69 shorter events, 2.1 us)
Async XLA Ops:
  7.2 108.6 %all-gather.2.cloned.1.call-start = ((), (), s32[]{:S(2)}) async-start(), calls=%async_computation.5 | async-start | bytes 4718592 | tf_op jit(solution)/shard_map/all_gather | solution.py:537
  9.4 9.0 %collective-permute-start.6 = (bf16[1,2,256,128]{3,2,1,0:T(8,128)(2,1)S(1)}, bf16[1,2,256,128]{3,2,1,0:T(8,128)(2,1)S(1)}, u32[]{:S(2)}, u32[]{:S(2)}) collective-permute-start(bf16[1,2,256,128]{3,2,1,0:T(8,128)(2,1)S(1)} %copy.28), channel_id=1, source_target_pairs={{0,3},{1,0},{2,1},{3,2},{4,7},{5,4},{6,5},{7,6},{8,11},{9,8},{10,9... | collective-permute-start | bytes 393224 | tf_op jit(solution)/shard_map/ppermute | solution.py:534
  14.5 11.2 %collective-permute-start.7 = (bf16[1,2,256,128]{3,2,1,0:T(8,128)(2,1)S(1)}, bf16[1,2,256,128]{3,2,1,0:T(8,128)(2,1)S(1)}, u32[]{:S(2)}, u32[]{:S(2)}) collective-permute-start(bf16[1,2,256,128]{3,2,1,0:T(8,128)(2,1)S(1)} %copy.28), channel_id=1, source_target_pairs={{0,2},{1,3},{2,0},{3,1},{4,6},{5,7},{6,4},{7,5},{8,10},{9,11},{10,... | collective-permute-start | bytes 393224 | tf_op jit(solution)/shard_map/ppermute | solution.py:534
  14.5 11.2 %collective-permute-start.8 = (bf16[1,2,256,128]{3,2,1,0:T(8,128)(2,1)S(1)}, bf16[1,2,256,128]{3,2,1,0:T(8,128)(2,1)S(1)}, u32[]{:S(2)}, u32[]{:S(2)}) collective-permute-start(bf16[1,2,256,128]{3,2,1,0:T(8,128)(2,1)S(1)} %copy.28), channel_id=1, source_target_pairs={{0,1},{1,2},{2,3},{3,0},{4,5},{5,6},{6,7},{7,4},{8,9},{9,10},{10,1... | collective-permute-start | bytes 393224 | tf_op jit(solution)/shard_map/ppermute | solution.py:534
  43.3 8.3 %collective-permute-start = (bf16[4,5,256,128]{3,2,1,0:T(8,128)(2,1)}, bf16[4,5,256,128]{3,2,1,0:T(8,128)(2,1)S(1)}, u32[]{:S(2)}, u32[]{:S(2)}) collective-permute-start(bf16[4,5,256,128]{3,2,1,0:T(8,128)(2,1)} %get-tuple-element.81.own_ref), channel_id=1, source_target_pairs={{1,2},{2,1},{5,6},{6,5},{9,10},{10,9},{13,14},{14,13},{17,18},{18,... | collective-permute-start | bytes 3932168 | tf_op jit(solution)/shard_map/ppermute | solution.py:559
  44.0 35.1 %collective-permute-start.1 = (bf16[4,5,256,128]{3,2,1,0:T(8,128)(2,1)}, bf16[4,5,256,128]{3,2,1,0:T(8,128)(2,1)S(1)}, u32[]{:S(2)}, u32[]{:S(2)}) collective-permute-start(bf16[4,5,256,128]{3,2,1,0:T(8,128)(2,1)} %get-tuple-element.81.own_ref), channel_id=1, source_target_pairs={{0,2},{3,1},{4,6},{7,5},{8,10},{11,9},{12,14},{15,13},{16,18},{19,... | collective-permute-start | bytes 3932168 | tf_op jit(solution)/shard_map/ppermute | solution.py:559
  49.7 55.7 %collective-permute-start.2 = (bf16[4,5,256,128]{3,2,1,0:T(8,128)(2,1)}, bf16[4,5,256,128]{3,2,1,0:T(8,128)(2,1)S(1)}, u32[]{:S(2)}, u32[]{:S(2)}) collective-permute-start(bf16[4,5,256,128]{3,2,1,0:T(8,128)(2,1)} %get-tuple-element.81.own_ref), channel_id=1, source_target_pairs={{0,1},{3,2},{4,5},{7,6},{8,9},{11,10},{12,13},{15,14},{16,17},{19,... | collective-permute-start | bytes 3932168 | tf_op jit(solution)/shard_map/ppermute | solution.py:559
  51.6 53.9 %copy-start.3 = (bf16[4,5,256,128]{3,2,1,0:T(8,128)(2,1)}, bf16[4,5,256,128]{3,2,1,0:T(8,128)(2,1)S(1)}, u32[]{:S(2)}) copy-start(bf16[4,5,256,128]{3,2,1,0:T(8,128)(2,1)S(1)} %collective-permute-done.other_next_ref) | copy-start | bytes 3932164
  79.1 27.0 %copy-start.4 = (bf16[4,5,256,128]{3,2,1,0:T(8,128)(2,1)}, bf16[4,5,256,128]{3,2,1,0:T(8,128)(2,1)S(1)}, u32[]{:S(2)}) copy-start(bf16[4,5,256,128]{3,2,1,0:T(8,128)(2,1)S(1)} %collective-permute-done.1.other_far_ref) | copy-start | bytes 3932164
  105.4 7.8 %copy-start.5 = (bf16[4,5,256,128]{3,2,1,0:T(8,128)(2,1)}, bf16[4,5,256,128]{3,2,1,0:T(8,128)(2,1)S(1)}, u32[]{:S(2)}) copy-start(bf16[4,5,256,128]{3,2,1,0:T(8,128)(2,1)S(1)} %collective-permute-done.2.far_ref) | copy-start | bytes 3932164
  105.4 40.6 %collective-permute-start.3 = (bf16[4,5,256,128]{3,2,1,0:T(8,128)(2,1)}, bf16[4,5,256,128]{3,2,1,0:T(8,128)(2,1)S(1)}, u32[]{:S(2)}, u32[]{:S(2)}) collective-permute-start(bf16[4,5,256,128]{3,2,1,0:T(8,128)(2,1)} %get-tuple-element.91.own_ref), channel_id=1, source_target_pairs={{1,2},{2,1},{5,6},{6,5},{9,10},{10,9},{13,14},{14,13},{17,18},{18,... | collective-permute-start | bytes 3932168 | tf_op jit(solution)/shard_map/ppermute | solution.py:570
  106.2 39.9 %collective-permute-start.4 = (bf16[4,5,256,128]{3,2,1,0:T(8,128)(2,1)}, bf16[4,5,256,128]{3,2,1,0:T(8,128)(2,1)S(1)}, u32[]{:S(2)}, u32[]{:S(2)}) collective-permute-start(bf16[4,5,256,128]{3,2,1,0:T(8,128)(2,1)} %get-tuple-element.91.own_ref), channel_id=1, source_target_pairs={{0,2},{3,1},{4,6},{7,5},{8,10},{11,9},{12,14},{15,13},{16,18},{19,... | collective-permute-start | bytes 3932168 | tf_op jit(solution)/shard_map/ppermute | solution.py:570
  113.2 54.6 %collective-permute-start.5 = (bf16[4,5,256,128]{3,2,1,0:T(8,128)(2,1)}, bf16[4,5,256,128]{3,2,1,0:T(8,128)(2,1)}, u32[]{:S(2)}, u32[]{:S(2)}) collective-permute-start(bf16[4,5,256,128]{3,2,1,0:T(8,128)(2,1)} %get-tuple-element.91.own_ref), channel_id=1, source_target_pairs={{0,1},{3,2},{4,5},{7,6},{8,9},{11,10},{12,13},{15,14},{16,17},{19,... | collective-permute-start | bytes 3932168 | tf_op jit(solution)/shard_map/ppermute | solution.py:570
  146.0 23.0 %copy-start.1 = (bf16[4,5,256,128]{3,2,1,0:T(8,128)(2,1)}, bf16[4,5,256,128]{3,2,1,0:T(8,128)(2,1)S(1)}, u32[]{:S(2)}) copy-start(bf16[4,5,256,128]{3,2,1,0:T(8,128)(2,1)S(1)} %collective-permute-done.3.other_next_ref) | copy-start | bytes 3932164
  146.1 21.7 %copy-start.2 = (bf16[4,5,256,128]{3,2,1,0:T(8,128)(2,1)}, bf16[4,5,256,128]{3,2,1,0:T(8,128)(2,1)S(1)}, u32[]{:S(2)}) copy-start(bf16[4,5,256,128]{3,2,1,0:T(8,128)(2,1)S(1)} %collective-permute-done.4.other_far_ref) | copy-start | bytes 3932164
  167.7 47.4 %collective-permute-start.12 = (bf16[4,5,256,128]{3,2,1,0:T(8,128)(2,1)}, bf16[4,5,256,128]{3,2,1,0:T(8,128)(2,1)S(1)}, u32[]{:S(2)}, u32[]{:S(2)}) collective-permute-start(bf16[4,5,256,128]{3,2,1,0:T(8,128)(2,1)} %get-tuple-element.97), channel_id=1, source_target_pairs={{1,0},{2,3},{5,4},{6,7},{9,8},{10,11},{13,12},{14,15},{17,16},{18,... | collective-permute-start | bytes 3932168 | tf_op jit(solution)/shard_map/ppermute | solution.py:572
  169.0 45.0 %all-to-all-start = ((bf16[8,4,5,32,128]{4,3,2,1,0:T(8,128)(2,1)}), bf16[8,4,5,32,128]{4,3,2,1,0:T(8,128)(2,1)S(1)}, u32[]{:S(2)}, u32[]{:S(2)}) async-start(bf16[8,4,5,32,128]{4,3,2,1,0:T(8,128)(2,1)} %get-tuple-element.98), calls=%async_computation | async-start | bytes 2621440 | tf_op jit(solution)/shard_map/all_to_all | solution.py:540
  172.7 42.2 %collective-permute-start.9 = (bf16[4,3,256,128]{3,2,1,0:T(8,128)(2,1)}, bf16[4,3,256,128]{3,2,1,0:T(8,128)(2,1)}, u32[]{:S(2)}, u32[]{:S(2)}) collective-permute-start(bf16[4,3,256,128]{3,2,1,0:T(8,128)(2,1)} %get-tuple-element.102.own_ref), channel_id=1, source_target_pairs={{1,2},{2,1},{5,6},{6,5},{9,10},{10,9},{13,14},{14,13},{17,18},{18,... | collective-permute-start | bytes 2359304 | tf_op jit(solution)/shard_map/ppermute | solution.py:570
  174.3 40.6 %collective-permute-start.10 = (bf16[4,3,256,128]{3,2,1,0:T(8,128)(2,1)}, bf16[4,3,256,128]{3,2,1,0:T(8,128)(2,1)}, u32[]{:S(2)}, u32[]{:S(2)}) collective-permute-start(bf16[4,3,256,128]{3,2,1,0:T(8,128)(2,1)} %get-tuple-element.102.own_ref), channel_id=1, source_target_pairs={{0,2},{3,1},{4,6},{7,5},{8,10},{11,9},{12,14},{15,13},{16,18},{19,... | collective-permute-start | bytes 2359304 | tf_op jit(solution)/shard_map/ppermute | solution.py:570
  181.6 33.5 %collective-permute-start.11 = (bf16[4,3,256,128]{3,2,1,0:T(8,128)(2,1)}, bf16[4,3,256,128]{3,2,1,0:T(8,128)(2,1)}, u32[]{:S(2)}, u32[]{:S(2)}) collective-permute-start(bf16[4,3,256,128]{3,2,1,0:T(8,128)(2,1)} %get-tuple-element.102.own_ref), channel_id=1, source_target_pairs={{0,1},{3,2},{4,5},{7,6},{8,9},{11,10},{12,13},{15,14},{16,17},{19,... | collective-permute-start | bytes 2359304 | tf_op jit(solution)/shard_map/ppermute | solution.py:570
  214.0 6.4 %copy-start.6 = (bf16[4,3,256,128]{3,2,1,0:T(8,128)(2,1)S(1)}, bf16[4,3,256,128]{3,2,1,0:T(8,128)(2,1)}, u32[]{:S(2)}) copy-start(bf16[4,3,256,128]{3,2,1,0:T(8,128)(2,1)} %get-tuple-element.118.own_ref) | copy-start | bytes 2359300
  215.1 36.5 %copy-start = (bf16[4,5,256,128]{3,2,1,0:T(8,128)(2,1)}, bf16[4,5,256,128]{3,2,1,0:T(8,128)(2,1)S(1)}, u32[]{:S(2)}) copy-start(bf16[4,5,256,128]{3,2,1,0:T(8,128)(2,1)S(1)} %collective-permute-done.12.refs_8_) | copy-start | bytes 3932164
  215.1 48.4 %collective-permute-start.16 = (bf16[4,5,256,128]{3,2,1,0:T(8,128)(2,1)}, bf16[4,5,256,128]{3,2,1,0:T(8,128)(2,1)}, u32[]{:S(2)}, u32[]{:S(2)}) collective-permute-start(bf16[4,5,256,128]{3,2,1,0:T(8,128)(2,1)} %get-tuple-element.109), channel_id=1, source_target_pairs={{1,0},{2,3},{5,4},{6,7},{9,8},{10,11},{13,12},{14,15},{17,16},{18,... | collective-permute-start | bytes 3932168 | tf_op jit(solution)/shard_map/ppermute | solution.py:572
  216.4 35.2 %all-to-all-start.1 = ((bf16[8,4,5,32,128]{4,3,2,1,0:T(8,128)(2,1)}), bf16[8,4,5,32,128]{4,3,2,1,0:T(8,128)(2,1)S(1)}, u32[]{:S(2)}, u32[]{:S(2)}) async-start(bf16[8,4,5,32,128]{4,3,2,1,0:T(8,128)(2,1)} %get-tuple-element.111), calls=%async_computation.1 | async-start | bytes 2621440 | tf_op jit(solution)/shard_map/all_to_all | solution.py:540
  220.5 32.1 %collective-permute-start.13 = (bf16[4,3,256,128]{3,2,1,0:T(8,128)(2,1)S(1)}, bf16[4,3,256,128]{3,2,1,0:T(8,128)(2,1)}, u32[]{:S(2)}, u32[]{:S(2)}) collective-permute-start(bf16[4,3,256,128]{3,2,1,0:T(8,128)(2,1)S(1)} %copy-done.6), channel_id=1, source_target_pairs={{1,2},{2,1},{5,6},{6,5},{9,10},{10,9},{13,14},{14,13},{17,18},{18,... | collective-permute-start | bytes 2359304 | tf_op jit(solution)/shard_map/ppermute | solution.py:570
  222.0 30.5 %collective-permute-start.14 = (bf16[4,3,256,128]{3,2,1,0:T(8,128)(2,1)S(1)}, bf16[4,3,256,128]{3,2,1,0:T(8,128)(2,1)}, u32[]{:S(2)}, u32[]{:S(2)}) collective-permute-start(bf16[4,3,256,128]{3,2,1,0:T(8,128)(2,1)S(1)} %copy-done.6), channel_id=1, source_target_pairs={{0,2},{3,1},{4,6},{7,5},{8,10},{11,9},{12,14},{15,13},{16,18},{19,... | collective-permute-start | bytes 2359304 | tf_op jit(solution)/shard_map/ppermute | solution.py:570
  230.3 33.2 %collective-permute-start.15 = (bf16[4,3,256,128]{3,2,1,0:T(8,128)(2,1)S(1)}, bf16[4,3,256,128]{3,2,1,0:T(8,128)(2,1)}, u32[]{:S(2)}, u32[]{:S(2)}) collective-permute-start(bf16[4,3,256,128]{3,2,1,0:T(8,128)(2,1)S(1)} %copy-done.6), channel_id=1, source_target_pairs={{0,1},{3,2},{4,5},{7,6},{8,9},{11,10},{12,13},{15,14},{16,17},{19,... | collective-permute-start | bytes 2359304 | tf_op jit(solution)/shard_map/ppermute | solution.py:570
  263.5 24.5 %collective-permute-start.17 = (bf16[4,3,256,128]{3,2,1,0:T(8,128)(2,1)}, bf16[4,3,256,128]{3,2,1,0:T(8,128)(2,1)S(1)}, u32[]{:S(2)}, u32[]{:S(2)}) collective-permute-start(bf16[4,3,256,128]{3,2,1,0:T(8,128)(2,1)} %get-tuple-element.131), channel_id=1, source_target_pairs={{1,0},{2,3},{5,4},{6,7},{9,8},{10,11},{13,12},{14,15},{17,16},{18,... | collective-permute-start | bytes 2359304 | tf_op jit(solution)/shard_map/ppermute | solution.py:572
  264.8 23.0 %all-to-all-start.2 = ((bf16[8,4,3,32,128]{4,3,2,1,0:T(8,128)(2,1)}), bf16[8,4,3,32,128]{4,3,2,1,0:T(8,128)(2,1)S(1)}, u32[]{:S(2)}, u32[]{:S(2)}) async-start(bf16[8,4,3,32,128]{4,3,2,1,0:T(8,128)(2,1)} %get-tuple-element.134), calls=%async_computation.2 | async-start | bytes 1572864 | tf_op jit(solution)/shard_map/all_to_all | solution.py:540
  287.8 5.7 %copy-start.9 = (bf16[4,5,32,128]{3,2,1,0:T(8,128)(2,1)S(1)}, bf16[4,5,32,128]{3,2,1,0:T(8,128)(2,1)}, u32[]{:S(2)}) copy-start(bf16[4,5,32,128]{3,2,1,0:T(8,128)(2,1)} %reduce_sum.48) | copy-start | bytes 491524
  287.8 5.7 %copy-start.10 = (bf16[4,5,32,128]{3,2,1,0:T(8,128)(2,1)S(1)}, bf16[4,5,32,128]{3,2,1,0:T(8,128)(2,1)}, u32[]{:S(2)}) copy-start(bf16[4,5,32,128]{3,2,1,0:T(8,128)(2,1)} %reduce_sum.49) | copy-start | bytes 491524
  288.0 22.5 %copy-start.7 = (bf16[4,3,256,128]{3,2,1,0:T(8,128)(2,1)}, bf16[4,3,256,128]{3,2,1,0:T(8,128)(2,1)S(1)}, u32[]{:S(2)}) copy-start(bf16[4,3,256,128]{3,2,1,0:T(8,128)(2,1)S(1)} %collective-permute-done.17.refs_10_) | copy-start | bytes 2359300
  288.0 22.4 %collective-permute-start.18 = (bf16[4,3,256,128]{3,2,1,0:T(8,128)(2,1)}, bf16[4,3,256,128]{3,2,1,0:T(8,128)(2,1)S(1)}, u32[]{:S(2)}, u32[]{:S(2)}) collective-permute-start(bf16[4,3,256,128]{3,2,1,0:T(8,128)(2,1)} %get-tuple-element.138), channel_id=1, source_target_pairs={{1,0},{2,3},{5,4},{6,7},{9,8},{10,11},{13,12},{14,15},{17,16},{18,... | collective-permute-start | bytes 2359304 | tf_op jit(solution)/shard_map/ppermute | solution.py:583
  289.3 16.8 %all-to-all-start.3 = ((bf16[8,4,3,32,128]{4,3,2,1,0:T(8,128)(2,1)}), bf16[8,4,3,32,128]{4,3,2,1,0:T(8,128)(2,1)S(1)}, u32[]{:S(2)}, u32[]{:S(2)}) async-start(bf16[8,4,3,32,128]{4,3,2,1,0:T(8,128)(2,1)} %get-tuple-element.139), calls=%async_computation.3 | async-start | bytes 1572864 | tf_op jit(solution)/shard_map/all_to_all | solution.py:540
  310.4 15.2 %copy-start.8 = (bf16[4,3,256,128]{3,2,1,0:T(8,128)(2,1)}, bf16[4,3,256,128]{3,2,1,0:T(8,128)(2,1)S(1)}, u32[]{:S(2)}) copy-start(bf16[4,3,256,128]{3,2,1,0:T(8,128)(2,1)S(1)} %collective-permute-done.18.refs_11_) | copy-start | bytes 2359300
  310.5 18.7 %copy-start.12 = (f32[16]{0:T(128)S(1)}, f32[16]{0:T(128)}, u32[]{:S(2)}) copy-start(f32[16]{0:T(128)} %param.18) | copy-start | bytes 196
  310.5 18.7 %copy-start.11 = (f32[64]{0:T(128)S(1)}, f32[64]{0:T(128)}, u32[]{:S(2)}) copy-start(f32[64]{0:T(128)} %param.19) | copy-start | bytes 772
  310.5 6.3 %collective-permute-start.21 = (bf16[16,32,128]{2,1,0:T(8,128)(2,1)S(1)}, bf16[16,32,128]{2,1,0:T(8,128)(2,1)S(1)}, u32[]{:S(2)}, u32[]{:S(2)}) collective-permute-start(bf16[16,32,128]{2,1,0:T(8,128)(2,1)S(1)} %get-tuple-element.150), channel_id=1, source_target_pairs={{0,3},{1,0},{2,1},{3,2},{4,7},{5,4},{6,5},{7,6},{8,11},{9,8},{10,9... | collective-permute-start | bytes 393224 | tf_op jit(solution)/shard_map/ppermute | solution.py:550
  312.9 11.4 %collective-permute-start.20 = (bf16[16,32,128]{2,1,0:T(8,128)(2,1)S(1)}, bf16[16,32,128]{2,1,0:T(8,128)(2,1)S(1)}, u32[]{:S(2)}, u32[]{:S(2)}) collective-permute-start(bf16[16,32,128]{2,1,0:T(8,128)(2,1)S(1)} %get-tuple-element.151), channel_id=1, source_target_pairs={{0,2},{1,3},{2,0},{3,1},{4,6},{5,7},{6,4},{7,5},{8,10},{9,11},{10,... | collective-permute-start | bytes 393224 | tf_op jit(solution)/shard_map/ppermute | solution.py:550
  312.9 11.4 %collective-permute-start.19 = (bf16[16,32,128]{2,1,0:T(8,128)(2,1)S(1)}, bf16[16,32,128]{2,1,0:T(8,128)(2,1)S(1)}, u32[]{:S(2)}, u32[]{:S(2)}) collective-permute-start(bf16[16,32,128]{2,1,0:T(8,128)(2,1)S(1)} %get-tuple-element.149), channel_id=1, source_target_pairs={{0,1},{1,2},{2,3},{3,0},{4,5},{5,6},{6,7},{7,4},{8,9},{9,10},{10,1... | collective-permute-start | bytes 393224 | tf_op jit(solution)/shard_map/ppermute | solution.py:550
  325.6 27.1 %all-to-all-start.4 = ((bf16[8,16,32,128]{3,2,1,0:T(8,128)(2,1)}), bf16[8,16,32,128]{3,2,1,0:T(8,128)(2,1)S(1)}, u32[]{:S(2)}, u32[]{:S(2)}) async-start(bf16[8,16,32,128]{3,2,1,0:T(8,128)(2,1)} %broadcast_in_dim.5), calls=%async_computation.4 | async-start | bytes 2097152 | tf_op jit(solution)/shard_map/all_to_all | solution.py:553
Sparse Core Ops, SparseCore 0:
  27.0 36.9 all-gather.1

commit v3 on v2

--- a/solution.py
+++ b/solution.py
@@ -192,7 +192,7 @@
 
 
 LANES = 128
-SHARES = (5, 5, 3, 3)
+SHARES = (7, 6, 3)
 STRIP = 16
 EDGE_ROWS = 16
 VMEM_BYTES = 60 * 2**20
@@ -397,106 +397,135 @@
     return (left.astype(jnp.float32) * right.astype(jnp.float32)).astype(jnp.bfloat16)
 
 
-def enter_kernel(side_ref, gate_ref, values_ref, cotangent_ref, out_gate_ref, *out_refs):
+def enter_kernel(first_ref, gate_ref, values_ref, cotangent_ref, out_gate_ref, *refs):
     channels, width = gate_ref.shape
-    *own_refs, other_ref = out_refs
-    groups, filters, rows, lanes = other_ref.shape
-    near_start = side_ref[0] > 0
-    mixed = product(gate_ref[...], values_ref[...]).astype(jnp.float32)
-    weighted = product(cotangent_ref[...], out_gate_ref[...]).astype(jnp.float32)
-
-    def blocks(array):
-        array = array.reshape(channels, rows, lanes).astype(jnp.bfloat16)
-        return array.reshape(groups, filters, rows, lanes)
-
-    own = blocks(jnp.where(near_start, mixed, weighted))
+    *out_refs, turned = refs
+    rows = width // LANES
+
+    def fill(left_ref, right_ref):
+        made = product(left_ref[...], right_ref[...]).astype(jnp.float32)
+        for row in range(rows):
+            column = made[:, row * LANES : (row + 1) * LANES]
+            turned[pl.ds(row, channels, stride=rows), :] = column
+
+    @pl.when(first_ref[0] == 1)
+    def _():
+        fill(gate_ref, values_ref)
+
+    @pl.when(first_ref[0] == 0)
+    def _():
+        fill(cotangent_ref, out_gate_ref)
+
+    groups = out_refs[0].shape[0]
+    made = turned[...].astype(jnp.bfloat16).reshape(groups, channels // groups, rows, LANES)
     start = 0
-    for own_ref in own_refs:
-        own_ref[...] = own[:, start : start + own_ref.shape[1]]
-        start += own_ref.shape[1]
-    other_ref[...] = blocks(jnp.where(near_start, weighted, mixed))
-
-
-def enter(side, flat, filters):
+    for out_ref in out_refs:
+        out_ref[...] = made[:, start : start + out_ref.shape[1]]
+        start += out_ref.shape[1]
+
+
+def enter(first, flat, filters, counts):
     channels, local_len = flat[0].shape
     groups, rows = channels // filters, local_len // LANES
-    counts = SHARES + (filters,)
+    block = (channels, EDGE_ROWS * LANES)
+    of_first = pl.BlockSpec(block, lambda i, first: (0, i * first[0]))
+    of_second = pl.BlockSpec(block, lambda i, first: (0, i * (1 - first[0])))
     return pl.pallas_call(
         enter_kernel,
-        grid=(rows // EDGE_ROWS,),
-        in_specs=[pl.BlockSpec(memory_space=pltpu.SMEM)]
-        + [pl.BlockSpec((channels, EDGE_ROWS * LANES), lambda i: (0, i))] * 4,
-        out_specs=[
-            pl.BlockSpec((groups, count, EDGE_ROWS, LANES), lambda i: (0, 0, i, 0))
-            for count in counts
-        ],
+        grid_spec=pltpu.PrefetchScalarGridSpec(
+            num_scalar_prefetch=1,
+            grid=(rows // EDGE_ROWS,),
+            in_specs=[of_first, of_first, of_second, of_second],
+            out_specs=[
+                pl.BlockSpec((groups, count, EDGE_ROWS, LANES), lambda i, first: (0, 0, i, 0))
+                for count in counts
+            ],
+            scratch_shapes=[pltpu.VMEM((channels * EDGE_ROWS, LANES), jnp.float32)],
+        ),
         out_shape=[
             jax.ShapeDtypeStruct((groups, count, rows, LANES), jnp.bfloat16) for count in counts
         ],
         compiler_params=pltpu.CompilerParams(vmem_limit_bytes=VMEM_BYTES),
         cost_estimate=pl.CostEstimate(
-            flops=4 * channels * local_len,
-            bytes_accessed=12 * channels * local_len,
+            flops=2 * channels * local_len,
+            bytes_accessed=6 * channels * local_len,
             transcendentals=0,
         ),
-    )(side, *flat)
-
-
-def leave_kernel(side_ref, skip_ref, gate_ref, values_ref, cotangent_ref, out_gate_ref, *refs):
+    )(first, *flat)
+
+
+def leave_kernel(has_received, has_made, *refs):
+    first_ref, skip_ref, gate_ref, values_ref, cotangent_ref, out_gate_ref, *refs = refs
     channels, width = gate_ref.shape
-    parts = len(SHARES)
-    near_refs, other_refs = refs[:parts], refs[parts : 2 * parts]
-    received_refs = refs[2 * parts : 3 * parts]
-    outputs_ref, grad_gate_ref, grad_out_gate_ref, grad_values_ref = refs[3 * parts :]
-    near_start = side_ref[0] > 0
-
-    def whole(part_refs):
-        return jnp.concatenate([ref[...] for ref in part_refs], axis=1).astype(jnp.float32)
-
-    def flat(array):
-        return array.reshape(channels, width // LANES, LANES).reshape(channels, width)
-
-    near = flat(whole(near_refs))
-    other = flat(whole(other_refs) + whole(received_refs))
+    parts, rows = len(SHARES), width // LANES
+    signal_refs, refs = refs[:parts], refs[parts:]
+    signal = jnp.concatenate([ref[...] for ref in signal_refs], axis=1).astype(jnp.float32)
+    if has_received:
+        received = jnp.concatenate([ref[...] for ref in refs[:parts]], axis=1)
+        signal, refs = signal + received.astype(jnp.float32), refs[parts:]
+    if has_made:
+        made_refs, refs = refs[:4], refs[4:]
+    *out_refs, turned = refs
+    turned[...] = signal.reshape(channels * rows, LANES)
+    signal = jnp.concatenate(
+        [turned[pl.ds(row, channels, stride=rows), :] for row in range(rows)], axis=1
+    )
     skip = skip_ref[...]
-    gate, values = gate_ref[...].astype(jnp.float32), values_ref[...].astype(jnp.float32)
-    cotangent = cotangent_ref[...].astype(jnp.float32)
-    out_gate = out_gate_ref[...].astype(jnp.float32)
-    mixed = (gate * values).astype(jnp.bfloat16).astype(jnp.float32)
-    weighted = (cotangent * out_gate).astype(jnp.bfloat16).astype(jnp.float32)
-    summed = jnp.where(near_start, near, other) + skip * mixed
-    outputs_ref[...] = (out_gate * summed).astype(jnp.bfloat16)
-    grad_out_gate_ref[...] = (cotangent * summed).astype(jnp.bfloat16)
-    back_total = jnp.where(near_start, other, near) + skip * weighted
-    grad_gate_ref[...] = (back_total * values).astype(jnp.bfloat16)
-    grad_values_ref[...] = (back_total * gate).astype(jnp.bfloat16)
-
-
-def leave(side, skip_gain, flat, near_parts, other_parts, received_parts):
+
+    def finish(left_ref, right_ref, factor_refs, result_refs, kept):
+        term = product(left_ref[...], right_ref[...]).astype(jnp.float32)
+        total = signal + skip * term
+        for factor_ref, result_ref in zip(factor_refs, result_refs):
+            result_ref[...] = (factor_ref[...].astype(jnp.float32) * total).astype(jnp.bfloat16)
+        if has_made:
+
+            @pl.when(pl.program_id(0) == 0)
+            def _():
+                for number in kept:
+                    out_refs[number][...] = made_refs[number][...]
+
+    @pl.when(first_ref[0] == 1)
+    def _():
+        finish(gate_ref, values_ref, (out_gate_ref, cotangent_ref), out_refs[:2], (2, 3))
+
+    @pl.when(first_ref[0] == 0)
+    def _():
+        finish(cotangent_ref, out_gate_ref, (values_ref, gate_ref), out_refs[2:], (0, 1))
+
+
+def leave(first, skip_gain, flat, signal_parts, received_parts=(), made=()):
     channels, local_len = flat[0].shape
-    parts = (*near_parts, *other_parts, *received_parts)
-    flat_block = pl.BlockSpec((channels, EDGE_ROWS * LANES), lambda i: (0, i))
+    parts = (*signal_parts, *received_parts)
+    block = (channels, EDGE_ROWS * LANES)
+    flat_block = pl.BlockSpec(block, lambda i, first: (0, i))
+    still_block = pl.BlockSpec(block, lambda i, first: (0, 0))
+    of_first = pl.BlockSpec(block, lambda i, first: (0, i * first[0]))
+    of_second = pl.BlockSpec(block, lambda i, first: (0, i * (1 - first[0])))
+    before = 6 + len(parts)
     return pl.pallas_call(
-        leave_kernel,
-        grid=(local_len // (EDGE_ROWS * LANES),),
-        in_specs=[
-            pl.BlockSpec(memory_space=pltpu.SMEM),
-            pl.BlockSpec((channels, 1), lambda i: (0, 0)),
-        ]
-        + [flat_block] * 4
-        + [
-            pl.BlockSpec((*part.shape[:2], EDGE_ROWS, LANES), lambda i: (0, 0, i, 0))
-            for part in parts
-        ],
-        out_specs=[flat_block] * 4,
+        lambda *refs: leave_kernel(bool(received_parts), bool(made), *refs),
+        grid_spec=pltpu.PrefetchScalarGridSpec(
+            num_scalar_prefetch=1,
+            grid=(local_len // (EDGE_ROWS * LANES),),
+            in_specs=[pl.BlockSpec((channels, 1), lambda i, first: (0, 0))]
+            + [flat_block] * 4
+            + [
+                pl.BlockSpec((*part.shape[:2], EDGE_ROWS, LANES), lambda i, first: (0, 0, i, 0))
+                for part in parts
+            ]
+            + [still_block] * len(made),
+            out_specs=[of_first, of_first, of_second, of_second],
+            scratch_shapes=[pltpu.VMEM((channels * EDGE_ROWS, LANES), jnp.float32)],
+        ),
         out_shape=[jax.ShapeDtypeStruct((channels, local_len), jnp.bfloat16)] * 4,
+        input_output_aliases={before + number: number for number in range(len(made))},
         compiler_params=pltpu.CompilerParams(vmem_limit_bytes=VMEM_BYTES),
         cost_estimate=pl.CostEstimate(
-            flops=12 * channels * local_len,
-            bytes_accessed=22 * channels * local_len,
+            flops=8 * channels * local_len,
+            bytes_accessed=14 * channels * local_len,
             transcendentals=0,
         ),
-    )(side, skip_gain[:, None], *flat, *parts)
+    )(first, skip_gain[:, None], *flat, *parts, *made)
 
 
 def rotation(hop):
@@ -512,8 +541,11 @@
     data_size = lax.axis_size("dp")
     tables = block_tables(rows)
     side = jnp.where(context_index < 2, 1.0, -1.0).astype(jnp.float32).reshape(1)
+    near_start = (context_index < 2).astype(jnp.int32).reshape(1)
     flat = (input_gate, values, cotangent, output_gate)
-    *own_parts, other = enter(side, flat, filters)
+    own_parts = enter(near_start, flat, filters, SHARES)
+    routes = ([(1, 2), (2, 1)], [(0, 2), (3, 1)], [(0, 1), (3, 2)])
+    back_route = [(1, 0), (2, 3)]
 
     positions = (context_index * local_len + jnp.arange(local_len, dtype=jnp.int32)).astype(
         jnp.float32
@@ -534,7 +566,10 @@
     turned = [taps] + [lax.ppermute(taps, "ctx", rotation(hop)) for hop in (1, 2, 3)]
     turned = jnp.concatenate(turned[::-1] + turned[:0:-1], axis=0)
     taps = lax.dynamic_slice_in_dim(turned, 3 - context_index, 4, 0)
+    own_parts, taps, rest = lax.optimization_barrier((own_parts, taps, 1 - near_start))
+    arrivals = [lax.ppermute(own_parts[0], "ctx", route) for route in routes]
     taps = lax.all_gather(taps, "dp", axis=1, tiled=True)
+    (other,) = enter(rest, flat, filters, (filters,))
 
     def lag_shares(pieces):
         pieces = lax.all_to_all(pieces, "dp", split_axis=0, concat_axis=0, tiled=True)
@@ -553,16 +588,13 @@
         spread = lax.all_to_all(spread, "dp", split_axis=0, concat_axis=0, tiled=True)
         return jnp.transpose(spread, (1, 0, 2, 3)).reshape(total.shape[0], rows, LANES)
 
-    routes = ([(1, 2), (2, 1)], [(0, 2), (3, 1)], [(0, 1), (3, 2)])
-    back_route = [(1, 0), (2, 3)]
     near_parts, other_parts, received_parts, lag_parts = [], [], [], []
-    arrivals = [lax.ppermute(own_parts[0], "ctx", route) for route in routes]
     start, pending = 0, None
     for number, own in enumerate(own_parts):
         leaving = own_parts[number + 1] if number + 1 < len(own_parts) else None
-        arrivals, own, leaving, pending, received_parts, lag_parts, near_parts = (
+        arrivals, own, leaving, pending, received_parts, lag_parts, near_parts, other = (
             lax.optimization_barrier(
-                (arrivals, own, leaving, pending, received_parts, lag_parts, near_parts)
+                (arrivals, own, leaving, pending, received_parts, lag_parts, near_parts, other)
             )
         )
         other_next, other_far, far = arrivals
@@ -577,16 +609,17 @@
         start += own.shape[1]
         near_parts.append(near_out)
         other_parts.append(other_out)
-    pending, received_parts, lag_parts = lax.optimization_barrier(
-        (pending, received_parts, lag_parts)
+    pending, received_parts, lag_parts, near_parts = lax.optimization_barrier(
+        (pending, received_parts, lag_parts, near_parts)
     )
     received = lax.ppermute(pending[0], "ctx", back_route)
-    received, late = lax.optimization_barrier((received, lag_shares(pending[1])))
+    made = leave(near_start, skip_gain, flat, near_parts)
+    received, late, made = lax.optimization_barrier((received, lag_shares(pending[1]), made))
     received_parts.append(received)
     lag = lag_sum(jnp.concatenate([*lag_parts, late], axis=1)).reshape(filters, local_len)
     grad_filter = lag.astype(jnp.float32) * envelope(filter_decay) * filter_scale
-    outputs, grad_input_gate, grad_output_gate, grad_values = leave(
-        side, skip_gain, flat, near_parts, other_parts, received_parts
+    outputs, grad_output_gate, grad_input_gate, grad_values = leave(
+        1 - near_start, skip_gain, flat, other_parts, received_parts, made
     )
     return (outputs, grad_input_gate, grad_output_gate, grad_values, grad_filter)
 

time: 365 us -> 360 us (0.986)
  Pallas kernels: 138 us -> 161 us
  waiting for transfers between devices: 124 us -> 105 us
  starting transfers between devices: 75.4 us -> 66.6 us
    pallas_call x2 -> x4, Pallas kernels: 39.3 us -> 64.7 us  [the longest x2 38.4 us: leave(): pl.pallas_call(lambda *refs: leave_kernel(bool(received_parts), bool(made...]
    ppermute x9 -> x6, waiting for transfers between devices: 32.9 us -> 20.3 us  [block_shards(): arrivals = [lax.ppermute(leaving, 'ctx', route) for route in routes]]
    ppermute x3 -> x2, waiting for transfers between devices: 0.01 us -> 10.9 us  [block_shards(): received_parts.append(lax.ppermute(pending[0], 'ctx', back_route))]
    all_to_all x4 -> x3, waiting for transfers between devices: 12.5 us -> 1.84 us  [lag_shares(): lax.all_to_all(pieces, 'dp', split_axis=0, concat_axis=0, tiled=True)]
    ppermute x3, waiting for transfers between devices: 10.2 us -> 0.01 us  [block_shards(): lax.ppermute(taps, 'ctx', rotation(hop))]
    ppermute x9 -> x6, starting transfers between devices: 33.4 us -> 23.7 us  [block_shards(): arrivals = [lax.ppermute(leaving, 'ctx', route) for route in routes]]
    ppermute x3, waiting for transfers between devices: 53.8 us -> 60.4 us  [block_shards(): arrivals = [lax.ppermute(own_parts[0], 'ctx', route) for route in routes]]
    ppermute x1, waiting for transfers between devices: 4.15 us -> 0.01 us  [block_shards(): received = lax.ppermute(pending[0], 'ctx', back_route)]
  transfers between devices with their start and end apart: 28 -> 23, of which waited for: 11 -> 7; matrix products, arithmetic and copies ran while one was open for 1% -> 1% of each run, Pallas kernels for 38% -> 45%
where the time goes in v3:
time: 360 us; the launch traced here: 358 us
  Pallas kernels  161 us (45%)
  waiting for transfers between devices  105 us (29%)
  starting transfers between devices  66.6 us (18%)
  between operations  14.4 us (4%)
  other arithmetic  6.59 us (2%)
  local copies, waits for them, and re-layouts  3.92 us (1%)
    pallas_call x3, Pallas kernels, block_products(): pl.pallas_call(block_kernel, grid=(filters,), in_specs=[pl.BlockSpec(memo...  96.2 us
    ppermute x3, waiting for transfers between devices, block_shards(): arrivals = [lax.ppermute(own_parts[0], 'ctx', route) for route in routes]  60.4 us
    pallas_call x2, Pallas kernels, leave(): pl.pallas_call(lambda *refs: leave_kernel(bool(received_parts), bool(made...  38.4 us
    pallas_call x2, Pallas kernels, enter(): pl.pallas_call(enter_kernel, grid_spec=pltpu.PrefetchScalarGridSpec(num_s...  26.3 us
    ppermute x6, starting transfers between devices, block_shards(): arrivals = [lax.ppermute(leaving, 'ctx', route) for route in routes]  23.7 us
    ppermute x6, waiting for transfers between devices, block_shards(): arrivals = [lax.ppermute(leaving, 'ctx', route) for route in routes]  20.3 us
    all_to_all x3, starting transfers between devices, lag_shares(): lax.all_to_all(pieces, 'dp', split_axis=0, concat_axis=0, tiled=True)  11.8 us
    ppermute x3, starting transfers between devices, block_shards(): arrivals = [lax.ppermute(own_parts[0], 'ctx', route) for route in routes]  11.8 us
  transfers between devices with their start and end apart: 23, of which 7 were waited for; matrix products, arithmetic and copies ran while one was open for 1% of the time, Pallas kernels for 45%

profile of v3, /device:TPU:0, one launch (start us, length us, event | category | flops | bytes accessed | tf_op | source)
XLA Modules:
  0.0 357.6 jit_solution(9598029786835091139)
XLA Ops:
  7.2 0.7 dynamic-slice_negate_fusion
  8.0 1.4 fusion.4
  9.4 5.1 %collective-permute-start = (bf16[1,2,256,128]{3,2,1,0:T(8,128)(2,1)S(1)}, bf16[1,2,256,128]{3,2,1,0:T(8,128)(2,1)S(1)}, u32[]{:S(2)}, u32[]{:S(2)}) collective-permute-start(bf16[1,2,256,128]{3,2,1,0:T(8,128)(2,1)S(1)} %copy.35), channel_id=1, source_target_pairs={{0,3},{1,0},{2,1},{3,2},{4,7},{5,4},{6,5},{7,6},{8,11},{9,8},{10,9... | collective-permute-start | bytes 393224 | tf_op jit(solution)/shard_map/ppermute | solution.py:566
  14.5 1.0 collective-permute-start.2
  15.5 13.0 %shard_map.164 = (bf16[4,7,256,128]{3,2,1,0:T(8,128)(2,1)}, bf16[4,6,256,128]{3,2,1,0:T(8,128)(2,1)}, bf16[4,3,256,128]{3,2,1,0:T(8,128)(2,1)}) custom-call(s32[1]{0:T(128)} %bitcast.first_ref.refs_0_, bf16[64,32768]{1,0:T(8,128)(2,1)} %refs_2_.3, bf16[64,32768]{1,0:T(8,128)(2,1)} %refs_3_.3, bf16[64,32768]{1,0:T(8,128)(2,1)} %refs_4_.3, ...), custom_call_target="tpu_custom_call" | custom-call | flops 4194304 | bytes 12582912 | tf_op jit(solution)/shard_map/pallas_call | solution.py:433
  28.8 0.8 constant_dynamic-slice_fusion
  29.7 0.6 copy-done
  30.3 2.0 collective-permute-start.3
  32.3 7.2 %collective-permute-start.4 = (bf16[4,7,256,128]{3,2,1,0:T(8,128)(2,1)S(1)}, bf16[4,7,256,128]{3,2,1,0:T(8,128)(2,1)}, u32[]{:S(2)}, u32[]{:S(2)}) collective-permute-start(bf16[4,7,256,128]{3,2,1,0:T(8,128)(2,1)S(1)} %copy-done), channel_id=1, source_target_pairs={{0,2},{3,1},{4,6},{7,5},{8,10},{11,9},{12,14},{15,13},{16,18},{19,... | collective-permute-start | bytes 5505032 | tf_op jit(solution)/shard_map/ppermute | solution.py:570
  39.5 2.5 collective-permute-start.5
  42.0 13.2 %shard_map.165.other_own_ref = bf16[4,16,256,128]{3,2,1,0:T(8,128)(2,1)} custom-call(s32[1]{0:T(128)S(6)} %sub.7.first_ref.refs_0_, bf16[64,32768]{1,0:T(8,128)(2,1)} %refs_2_.3, bf16[64,32768]{1,0:T(8,128)(2,1)} %refs_3_.3, bf16[64,32768]{1,0:T(8,128)(2,1)} %refs_4_.3, bf16[64,32768]{1,0:T(8,128)(2,1)} %refs_5_.3), custom_call_target="tpu_custom_call" | custom-call | flops 4194304 | bytes 12582912 | tf_op jit(solution)/shard_map/pallas_call | solution.py:433
  55.2 23.3 %collective-permute-done.4.other_far_ref = bf16[4,7,256,128]{3,2,1,0:T(8,128)(2,1)} collective-permute-done((bf16[4,7,256,128]{3,2,1,0:T(8,128)(2,1)S(1)}, bf16[4,7,256,128]{3,2,1,0:T(8,128)(2,1)}, u32[]{:S(2)}, u32[]{:S(2)}) %collective-permute-start.4) | collective-permute-done | bytes 1835040 | tf_op jit(solution)/shard_map/ppermute | solution.py:570
  78.6 37.1 %collective-permute-done.5.far_ref = bf16[4,7,256,128]{3,2,1,0:T(8,128)(2,1)} collective-permute-done((bf16[4,7,256,128]{3,2,1,0:T(8,128)(2,1)S(1)}, bf16[4,7,256,128]{3,2,1,0:T(8,128)(2,1)}, u32[]{:S(2)}, u32[]{:S(2)}) %collective-permute-start.5) | collective-permute-done | bytes 1835040 | tf_op jit(solution)/shard_map/ppermute | solution.py:570
  115.6 0.8 collective-permute-start.6
  116.4 8.3 %collective-permute-start.7 = (bf16[4,6,256,128]{3,2,1,0:T(8,128)(2,1)S(1)}, bf16[4,6,256,128]{3,2,1,0:T(8,128)(2,1)}, u32[]{:S(2)}, u32[]{:S(2)}) collective-permute-start(bf16[4,6,256,128]{3,2,1,0:T(8,128)(2,1)S(1)} %copy-done.2), channel_id=1, source_target_pairs={{0,2},{3,1},{4,6},{7,5},{8,10},{11,9},{12,14},{15,13},{16,18},{19,... | collective-permute-start | bytes 4718600 | tf_op jit(solution)/shard_map/ppermute | solution.py:602
  124.7 2.4 collective-permute-start.8
  127.1 41.2 %shard_map.166 = (bf16[4,7,256,128]{3,2,1,0:T(8,128)(2,1)}, bf16[4,7,256,128]{3,2,1,0:T(8,128)(2,1)}, bf16[4,7,256,128]{3,2,1,0:T(8,128)(2,1)}, bf16[8,4,7,32,128]{4,3,2,1,0:T(8,128)(2,1)}) custom-call(f32[1]{0:T(128)} %bitcast.2.side_ref, bf16[4,7,256,128]{3,2,1,0:T(8,128)(2,1)} %get-tuple-element.80.own_ref, ...), custom_call_target="tpu_custom_call" | custom-call | flops 1 | bytes 1 | tf_op jit(solution)/shard_map/pallas_call | solution.py:379
  168.3 20.3 %collective-permute-done.8.far_ref = bf16[4,6,256,128]{3,2,1,0:T(8,128)(2,1)} collective-permute-done((bf16[4,6,256,128]{3,2,1,0:T(8,128)(2,1)S(1)}, bf16[4,6,256,128]{3,2,1,0:T(8,128)(2,1)}, u32[]{:S(2)}, u32[]{:S(2)}) %collective-permute-start.8) | collective-permute-done | bytes 1572896 | tf_op jit(solution)/shard_map/ppermute | solution.py:602
  188.6 1.3 collective-permute-start.12
  189.9 3.7 %all-to-all-start = ((bf16[8,4,7,32,128]{4,3,2,1,0:T(8,128)(2,1)}), bf16[8,4,7,32,128]{4,3,2,1,0:T(8,128)(2,1)S(1)}, u32[]{:S(2)}, u32[]{:S(2)}) async-start(bf16[8,4,7,32,128]{4,3,2,1,0:T(8,128)(2,1)} %get-tuple-element.102), calls=%async_computation | async-start | bytes 3670016 | tf_op jit(solution)/shard_map/all_to_all | solution.py:575
  193.7 0.7 collective-permute-start.9
  194.4 9.3 %collective-permute-start.10 = (bf16[4,3,256,128]{3,2,1,0:T(8,128)(2,1)}, bf16[4,3,256,128]{3,2,1,0:T(8,128)(2,1)}, u32[]{:S(2)}, u32[]{:S(2)}) collective-permute-start(bf16[4,3,256,128]{3,2,1,0:T(8,128)(2,1)} %get-tuple-element.105.own_ref), channel_id=1, source_target_pairs={{0,2},{3,1},{4,6},{7,5},{8,10},{11,9},{12,14},{15,13},{16,18},{19,... | collective-permute-start | bytes 2359304 | tf_op jit(solution)/shard_map/ppermute | solution.py:602
  203.7 2.2 collective-permute-start.11
  205.9 35.8 %shard_map.167 = (bf16[4,6,256,128]{3,2,1,0:T(8,128)(2,1)}, bf16[4,6,256,128]{3,2,1,0:T(8,128)(2,1)}, bf16[4,6,256,128]{3,2,1,0:T(8,128)(2,1)}, bf16[8,4,6,32,128]{4,3,2,1,0:T(8,128)(2,1)}) custom-call(f32[1]{0:T(128)} %bitcast.2.side_ref, bf16[4,6,256,128]{3,2,1,0:T(8,128)(2,1)} %get-tuple-element.92.own_ref, ...), custom_call_target="tpu_custom_call" | custom-call | flops 1 | bytes 1 | tf_op jit(solution)/shard_map/pallas_call | solution.py:379
  241.7 0.3 reduce_sum.36
  242.1 1.3 collective-permute-start.13
  243.4 4.2 %all-to-all-start.1 = ((bf16[8,4,6,32,128]{4,3,2,1,0:T(8,128)(2,1)}), bf16[8,4,6,32,128]{4,3,2,1,0:T(8,128)(2,1)S(1)}, u32[]{:S(2)}, u32[]{:S(2)}) async-start(bf16[8,4,6,32,128]{4,3,2,1,0:T(8,128)(2,1)} %get-tuple-element.116), calls=%async_computation.1 | async-start | bytes 3145728 | tf_op jit(solution)/shard_map/all_to_all | solution.py:575
  247.6 19.2 %shard_map.168 = (bf16[4,3,256,128]{3,2,1,0:T(8,128)(2,1)}, bf16[4,3,256,128]{3,2,1,0:T(8,128)(2,1)}, bf16[4,3,256,128]{3,2,1,0:T(8,128)(2,1)}, bf16[8,4,3,32,128]{4,3,2,1,0:T(8,128)(2,1)}) custom-call(f32[1]{0:T(128)} %bitcast.2.side_ref, bf16[4,3,256,128]{3,2,1,0:T(8,128)(2,1)} %get-tuple-element.105.own_ref, ...), custom_call_target="tpu_custom_call" | custom-call | flops 1 | bytes 1 | tf_op jit(solution)/shard_map/pallas_call | solution.py:379
  266.8 1.8 all-to-all-done.1
  268.6 0.9 reduce_sum.37
  269.5 10.9 %collective-permute-done.13.refs_10_ = bf16[4,6,256,128]{3,2,1,0:T(8,128)(2,1)S(1)} collective-permute-done((bf16[4,6,256,128]{3,2,1,0:T(8,128)(2,1)}, bf16[4,6,256,128]{3,2,1,0:T(8,128)(2,1)S(1)}, u32[]{:S(2)}, u32[]{:S(2)}) %collective-permute-start.13) | collective-permute-done | bytes 1572896 | tf_op jit(solution)/shard_map/ppermute | solution.py:604
  280.4 1.3 collective-permute-start.14
  281.7 3.9 %all-to-all-start.2 = ((bf16[8,4,3,32,128]{4,3,2,1,0:T(8,128)(2,1)}), bf16[8,4,3,32,128]{4,3,2,1,0:T(8,128)(2,1)S(1)}, u32[]{:S(2)}, u32[]{:S(2)}) async-start(bf16[8,4,3,32,128]{4,3,2,1,0:T(8,128)(2,1)} %get-tuple-element.123), calls=%async_computation.2 | async-start | bytes 1572864 | tf_op jit(solution)/shard_map/all_to_all | solution.py:575
  285.6 0.7 copy.27.refs_1_
  286.3 18.4 %shard_map.169 = (bf16[64,32768]{1,0:T(8,128)(2,1)}, bf16[64,32768]{1,0:T(8,128)(2,1)}, bf16[64,32768]{1,0:T(8,128)(2,1)}, bf16[64,32768]{1,0:T(8,128)(2,1)}) custom-call(s32[1]{0:T(128)} %bitcast.first_ref.refs_0_, f32[64,1]{1,0:T(8,128)} %copy.27.refs_1_, bf16[64,32768]{1,0:T(8,128)(2,1)} %refs_2_.3, bf16[64,32768]{1,0:T(8,128)(2,1)} %refs_3_.3, ...), custom_call_target="tpu_custom_call" | custom-call | flops 16777216 | bytes 29360128 | tf_op jit(solution)/shard_map/pallas_call | solution.py:505
  304.8 0.1 reduce_sum.38
  305.0 1.5 collective-permute-start.17
  306.5 3.5 collective-permute-start.16
  310.0 0.6 collective-permute-start.15
  310.6 2.1 collective-permute-done.17
  312.7 9.6 %collective-permute-done.16 = bf16[16,32,128]{2,1,0:T(8,128)(2,1)S(1)} collective-permute-done((bf16[16,32,128]{2,1,0:T(8,128)(2,1)S(1)}, bf16[16,32,128]{2,1,0:T(8,128)(2,1)S(1)}, u32[]{:S(2)}, u32[]{:S(2)}) %collective-permute-start.16) | collective-permute-done | bytes 131104 | tf_op jit(solution)/shard_map/ppermute | solution.py:585
  322.3 0.1 fusion.3
  322.4 1.2 broadcast_in_dim.5
  323.6 3.8 %all-to-all-start.3 = ((bf16[8,16,32,128]{3,2,1,0:T(8,128)(2,1)}), bf16[8,16,32,128]{3,2,1,0:T(8,128)(2,1)S(1)}, u32[]{:S(2)}, u32[]{:S(2)}) async-start(bf16[8,16,32,128]{3,2,1,0:T(8,128)(2,1)} %broadcast_in_dim.5), calls=%async_computation.3 | async-start | bytes 2097152 | tf_op jit(solution)/shard_map/all_to_all | solution.py:588
  327.5 20.0 %shard_map.170 = (bf16[64,32768]{1,0:T(8,128)(2,1)}, bf16[64,32768]{1,0:T(8,128)(2,1)}, bf16[64,32768]{1,0:T(8,128)(2,1)}, bf16[64,32768]{1,0:T(8,128)(2,1)}) custom-call(s32[1]{0:T(128)S(6)} %sub.7.first_ref.refs_0_, f32[64,1]{1,0:T(8,128)} %copy.27.refs_1_, ...), custom_call_target="tpu_custom_call", output_to_operand_aliasing={{0}: (12, {}), {1}: (13, {}), {2}: (14, {}), {3}: (15, {})} | custom-call | flops 16777216 | bytes 29360128 | tf_op jit(solution)/shard_map/pallas_call | solution.py:505
  347.5 0.3 convert_bitcast_fusion
  347.8 0.2 copy.28
  348.0 2.7 fusion
  (48 shorter events, 0.4 us)
Async XLA Ops:
  7.2 119.9 %all-gather.2.cloned.1.call-start = ((), (), s32[]{:S(2)}) async-start(), calls=%async_computation.4 | async-start | bytes 4718592 | tf_op jit(solution)/shard_map/all_gather | solution.py:571
  9.4 19.2 %collective-permute-start = (bf16[1,2,256,128]{3,2,1,0:T(8,128)(2,1)S(1)}, bf16[1,2,256,128]{3,2,1,0:T(8,128)(2,1)S(1)}, u32[]{:S(2)}, u32[]{:S(2)}) collective-permute-start(bf16[1,2,256,128]{3,2,1,0:T(8,128)(2,1)S(1)} %copy.35), channel_id=1, source_target_pairs={{0,3},{1,0},{2,1},{3,2},{4,7},{5,4},{6,5},{7,6},{8,11},{9,8},{10,9... | collective-permute-start | bytes 393224 | tf_op jit(solution)/shard_map/ppermute | solution.py:566
  14.5 14.1 %collective-permute-start.1 = (bf16[1,2,256,128]{3,2,1,0:T(8,128)(2,1)S(1)}, bf16[1,2,256,128]{3,2,1,0:T(8,128)(2,1)S(1)}, u32[]{:S(2)}, u32[]{:S(2)}) collective-permute-start(bf16[1,2,256,128]{3,2,1,0:T(8,128)(2,1)S(1)} %copy.35), channel_id=1, source_target_pairs={{0,2},{1,3},{2,0},{3,1},{4,6},{5,7},{6,4},{7,5},{8,10},{9,11},{10,... | collective-permute-start | bytes 393224 | tf_op jit(solution)/shard_map/ppermute | solution.py:566
  14.5 14.1 %collective-permute-start.2 = (bf16[1,2,256,128]{3,2,1,0:T(8,128)(2,1)S(1)}, bf16[1,2,256,128]{3,2,1,0:T(8,128)(2,1)S(1)}, u32[]{:S(2)}, u32[]{:S(2)}) collective-permute-start(bf16[1,2,256,128]{3,2,1,0:T(8,128)(2,1)S(1)} %copy.35), channel_id=1, source_target_pairs={{0,1},{1,2},{2,3},{3,0},{4,5},{5,6},{6,7},{7,4},{8,9},{9,10},{10,1... | collective-permute-start | bytes 393224 | tf_op jit(solution)/shard_map/ppermute | solution.py:566
  28.6 1.7 copy-start
  30.3 85.4 %copy-start.2 = (bf16[4,6,256,128]{3,2,1,0:T(8,128)(2,1)S(1)}, bf16[4,6,256,128]{3,2,1,0:T(8,128)(2,1)}, u32[]{:S(2)}) copy-start(bf16[4,6,256,128]{3,2,1,0:T(8,128)(2,1)} %get-tuple-element.92.own_ref) | copy-start | bytes 4718596
  30.3 25.0 %collective-permute-start.3 = (bf16[4,7,256,128]{3,2,1,0:T(8,128)(2,1)S(1)}, bf16[4,7,256,128]{3,2,1,0:T(8,128)(2,1)}, u32[]{:S(2)}, u32[]{:S(2)}) collective-permute-start(bf16[4,7,256,128]{3,2,1,0:T(8,128)(2,1)S(1)} %copy-done), channel_id=1, source_target_pairs={{1,2},{2,1},{5,6},{6,5},{9,10},{10,9},{13,14},{14,13},{17,18},{18,... | collective-permute-start | bytes 5505032 | tf_op jit(solution)/shard_map/ppermute | solution.py:570
  32.3 46.3 %collective-permute-start.4 = (bf16[4,7,256,128]{3,2,1,0:T(8,128)(2,1)S(1)}, bf16[4,7,256,128]{3,2,1,0:T(8,128)(2,1)}, u32[]{:S(2)}, u32[]{:S(2)}) collective-permute-start(bf16[4,7,256,128]{3,2,1,0:T(8,128)(2,1)S(1)} %copy-done), channel_id=1, source_target_pairs={{0,2},{3,1},{4,6},{7,5},{8,10},{11,9},{12,14},{15,13},{16,18},{19,... | collective-permute-start | bytes 5505032 | tf_op jit(solution)/shard_map/ppermute | solution.py:570
  39.5 76.2 %collective-permute-start.5 = (bf16[4,7,256,128]{3,2,1,0:T(8,128)(2,1)S(1)}, bf16[4,7,256,128]{3,2,1,0:T(8,128)(2,1)}, u32[]{:S(2)}, u32[]{:S(2)}) collective-permute-start(bf16[4,7,256,128]{3,2,1,0:T(8,128)(2,1)S(1)} %copy-done), channel_id=1, source_target_pairs={{0,1},{3,2},{4,5},{7,6},{8,9},{11,10},{12,13},{15,14},{16,17},{19,... | collective-permute-start | bytes 5505032 | tf_op jit(solution)/shard_map/ppermute | solution.py:570
  115.6 52.6 %collective-permute-start.6 = (bf16[4,6,256,128]{3,2,1,0:T(8,128)(2,1)S(1)}, bf16[4,6,256,128]{3,2,1,0:T(8,128)(2,1)S(1)}, u32[]{:S(2)}, u32[]{:S(2)}) collective-permute-start(bf16[4,6,256,128]{3,2,1,0:T(8,128)(2,1)S(1)} %copy-done.2), channel_id=1, source_target_pairs={{1,2},{2,1},{5,6},{6,5},{9,10},{10,9},{13,14},{14,13},{17,18},{18,... | collective-permute-start | bytes 4718600 | tf_op jit(solution)/shard_map/ppermute | solution.py:602
  116.4 51.9 %collective-permute-start.7 = (bf16[4,6,256,128]{3,2,1,0:T(8,128)(2,1)S(1)}, bf16[4,6,256,128]{3,2,1,0:T(8,128)(2,1)}, u32[]{:S(2)}, u32[]{:S(2)}) collective-permute-start(bf16[4,6,256,128]{3,2,1,0:T(8,128)(2,1)S(1)} %copy-done.2), channel_id=1, source_target_pairs={{0,2},{3,1},{4,6},{7,5},{8,10},{11,9},{12,14},{15,13},{16,18},{19,... | collective-permute-start | bytes 4718600 | tf_op jit(solution)/shard_map/ppermute | solution.py:602
  124.7 64.0 %collective-permute-start.8 = (bf16[4,6,256,128]{3,2,1,0:T(8,128)(2,1)S(1)}, bf16[4,6,256,128]{3,2,1,0:T(8,128)(2,1)}, u32[]{:S(2)}, u32[]{:S(2)}) collective-permute-start(bf16[4,6,256,128]{3,2,1,0:T(8,128)(2,1)S(1)} %copy-done.2), channel_id=1, source_target_pairs={{0,1},{3,2},{4,5},{7,6},{8,9},{11,10},{12,13},{15,14},{16,17},{19,... | collective-permute-start | bytes 4718600 | tf_op jit(solution)/shard_map/ppermute | solution.py:602
  168.3 21.6 %copy-start.3 = (bf16[4,6,256,128]{3,2,1,0:T(8,128)(2,1)}, bf16[4,6,256,128]{3,2,1,0:T(8,128)(2,1)S(1)}, u32[]{:S(2)}) copy-start(bf16[4,6,256,128]{3,2,1,0:T(8,128)(2,1)S(1)} %collective-permute-done.6.other_next_ref) | copy-start | bytes 4718596
  188.6 53.4 %collective-permute-start.12 = (bf16[4,7,256,128]{3,2,1,0:T(8,128)(2,1)}, bf16[4,7,256,128]{3,2,1,0:T(8,128)(2,1)}, u32[]{:S(2)}, u32[]{:S(2)}) collective-permute-start(bf16[4,7,256,128]{3,2,1,0:T(8,128)(2,1)} %get-tuple-element.101), channel_id=1, source_target_pairs={{1,0},{2,3},{5,4},{6,7},{9,8},{10,11},{13,12},{14,15},{17,16},{18,... | collective-permute-start | bytes 5505032 | tf_op jit(solution)/shard_map/ppermute | solution.py:604
  189.9 51.8 %all-to-all-start = ((bf16[8,4,7,32,128]{4,3,2,1,0:T(8,128)(2,1)}), bf16[8,4,7,32,128]{4,3,2,1,0:T(8,128)(2,1)S(1)}, u32[]{:S(2)}, u32[]{:S(2)}) async-start(bf16[8,4,7,32,128]{4,3,2,1,0:T(8,128)(2,1)} %get-tuple-element.102), calls=%async_computation | async-start | bytes 3670016 | tf_op jit(solution)/shard_map/all_to_all | solution.py:575
  193.7 48.4 %collective-permute-start.9 = (bf16[4,3,256,128]{3,2,1,0:T(8,128)(2,1)}, bf16[4,3,256,128]{3,2,1,0:T(8,128)(2,1)S(1)}, u32[]{:S(2)}, u32[]{:S(2)}) collective-permute-start(bf16[4,3,256,128]{3,2,1,0:T(8,128)(2,1)} %get-tuple-element.105.own_ref), channel_id=1, source_target_pairs={{1,2},{2,1},{5,6},{6,5},{9,10},{10,9},{13,14},{14,13},{17,18},{18,... | collective-permute-start | bytes 2359304 | tf_op jit(solution)/shard_map/ppermute | solution.py:602
  194.4 47.7 %collective-permute-start.10 = (bf16[4,3,256,128]{3,2,1,0:T(8,128)(2,1)}, bf16[4,3,256,128]{3,2,1,0:T(8,128)(2,1)}, u32[]{:S(2)}, u32[]{:S(2)}) collective-permute-start(bf16[4,3,256,128]{3,2,1,0:T(8,128)(2,1)} %get-tuple-element.105.own_ref), channel_id=1, source_target_pairs={{0,2},{3,1},{4,6},{7,5},{8,10},{11,9},{12,14},{15,13},{16,18},{19,... | collective-permute-start | bytes 2359304 | tf_op jit(solution)/shard_map/ppermute | solution.py:602
  203.7 38.3 %collective-permute-start.11 = (bf16[4,3,256,128]{3,2,1,0:T(8,128)(2,1)}, bf16[4,3,256,128]{3,2,1,0:T(8,128)(2,1)}, u32[]{:S(2)}, u32[]{:S(2)}) collective-permute-start(bf16[4,3,256,128]{3,2,1,0:T(8,128)(2,1)} %get-tuple-element.105.own_ref), channel_id=1, source_target_pairs={{0,1},{3,2},{4,5},{7,6},{8,9},{11,10},{12,13},{15,14},{16,17},{19,... | collective-permute-start | bytes 2359304 | tf_op jit(solution)/shard_map/ppermute | solution.py:602
  242.0 1.3 copy-start.4
  242.1 38.3 %collective-permute-start.13 = (bf16[4,6,256,128]{3,2,1,0:T(8,128)(2,1)}, bf16[4,6,256,128]{3,2,1,0:T(8,128)(2,1)S(1)}, u32[]{:S(2)}, u32[]{:S(2)}) collective-permute-start(bf16[4,6,256,128]{3,2,1,0:T(8,128)(2,1)} %get-tuple-element.114), channel_id=1, source_target_pairs={{1,0},{2,3},{5,4},{6,7},{9,8},{10,11},{13,12},{14,15},{17,16},{18,... | collective-permute-start | bytes 4718600 | tf_op jit(solution)/shard_map/ppermute | solution.py:604
  243.4 25.2 %all-to-all-start.1 = ((bf16[8,4,6,32,128]{4,3,2,1,0:T(8,128)(2,1)}), bf16[8,4,6,32,128]{4,3,2,1,0:T(8,128)(2,1)S(1)}, u32[]{:S(2)}, u32[]{:S(2)}) async-start(bf16[8,4,6,32,128]{4,3,2,1,0:T(8,128)(2,1)} %get-tuple-element.116), calls=%async_computation.1 | async-start | bytes 3145728 | tf_op jit(solution)/shard_map/all_to_all | solution.py:575
  266.7 18.8 %copy-start.6 = (f32[64]{0:T(128)S(1)}, f32[64]{0:T(128)}, u32[]{:S(2)}) copy-start(f32[64]{0:T(128)} %param.19) | copy-start | bytes 772
  280.4 24.3 %copy-start.1 = (bf16[4,6,256,128]{3,2,1,0:T(8,128)(2,1)}, bf16[4,6,256,128]{3,2,1,0:T(8,128)(2,1)S(1)}, u32[]{:S(2)}) copy-start(bf16[4,6,256,128]{3,2,1,0:T(8,128)(2,1)S(1)} %collective-permute-done.13.refs_10_) | copy-start | bytes 4718596
  280.4 24.5 %collective-permute-start.14 = (bf16[4,3,256,128]{3,2,1,0:T(8,128)(2,1)}, bf16[4,3,256,128]{3,2,1,0:T(8,128)(2,1)}, u32[]{:S(2)}, u32[]{:S(2)}) collective-permute-start(bf16[4,3,256,128]{3,2,1,0:T(8,128)(2,1)} %get-tuple-element.122), channel_id=1, source_target_pairs={{1,0},{2,3},{5,4},{6,7},{9,8},{10,11},{13,12},{14,15},{17,16},{18,... | collective-permute-start | bytes 2359304 | tf_op jit(solution)/shard_map/ppermute | solution.py:615
  281.7 23.1 %all-to-all-start.2 = ((bf16[8,4,3,32,128]{4,3,2,1,0:T(8,128)(2,1)}), bf16[8,4,3,32,128]{4,3,2,1,0:T(8,128)(2,1)S(1)}, u32[]{:S(2)}, u32[]{:S(2)}) async-start(bf16[8,4,3,32,128]{4,3,2,1,0:T(8,128)(2,1)} %get-tuple-element.123), calls=%async_computation.2 | async-start | bytes 1572864 | tf_op jit(solution)/shard_map/all_to_all | solution.py:575
  286.3 18.4 %copy-start.5 = (bf16[4,6,32,128]{3,2,1,0:T(8,128)(2,1)S(1)}, bf16[4,6,32,128]{3,2,1,0:T(8,128)(2,1)}, u32[]{:S(2)}) copy-start(bf16[4,6,32,128]{3,2,1,0:T(8,128)(2,1)} %reduce_sum.37) | copy-start | bytes 589828
  305.0 22.5 %copy-start.7 = (f32[16]{0:T(128)S(1)}, f32[16]{0:T(128)}, u32[]{:S(2)}) copy-start(f32[16]{0:T(128)} %param.18) | copy-start | bytes 196
  305.0 7.7 %collective-permute-start.17 = (bf16[16,32,128]{2,1,0:T(8,128)(2,1)S(1)}, bf16[16,32,128]{2,1,0:T(8,128)(2,1)S(1)}, u32[]{:S(2)}, u32[]{:S(2)}) collective-permute-start(bf16[16,32,128]{2,1,0:T(8,128)(2,1)S(1)} %get-tuple-element.144), channel_id=1, source_target_pairs={{0,3},{1,0},{2,1},{3,2},{4,7},{5,4},{6,5},{7,6},{8,11},{9,8},{10,9... | collective-permute-start | bytes 393224 | tf_op jit(solution)/shard_map/ppermute | solution.py:585
  306.5 15.8 %collective-permute-start.16 = (bf16[16,32,128]{2,1,0:T(8,128)(2,1)S(1)}, bf16[16,32,128]{2,1,0:T(8,128)(2,1)S(1)}, u32[]{:S(2)}, u32[]{:S(2)}) collective-permute-start(bf16[16,32,128]{2,1,0:T(8,128)(2,1)S(1)} %get-tuple-element.145), channel_id=1, source_target_pairs={{0,2},{1,3},{2,0},{3,1},{4,6},{5,7},{6,4},{7,5},{8,10},{9,11},{10,... | collective-permute-start | bytes 393224 | tf_op jit(solution)/shard_map/ppermute | solution.py:585
  310.0 12.3 %collective-permute-start.15 = (bf16[16,32,128]{2,1,0:T(8,128)(2,1)S(1)}, bf16[16,32,128]{2,1,0:T(8,128)(2,1)S(1)}, u32[]{:S(2)}, u32[]{:S(2)}) collective-permute-start(bf16[16,32,128]{2,1,0:T(8,128)(2,1)S(1)} %get-tuple-element.143), channel_id=1, source_target_pairs={{0,1},{1,2},{2,3},{3,0},{4,5},{5,6},{6,7},{7,4},{8,9},{9,10},{10,1... | collective-permute-start | bytes 393224 | tf_op jit(solution)/shard_map/ppermute | solution.py:585
  323.6 23.8 %all-to-all-start.3 = ((bf16[8,16,32,128]{3,2,1,0:T(8,128)(2,1)}), bf16[8,16,32,128]{3,2,1,0:T(8,128)(2,1)S(1)}, u32[]{:S(2)}, u32[]{:S(2)}) async-start(bf16[8,16,32,128]{3,2,1,0:T(8,128)(2,1)} %broadcast_in_dim.5), calls=%async_computation.3 | async-start | bytes 2097152 | tf_op jit(solution)/shard_map/all_to_all | solution.py:588
Sparse Core Ops, SparseCore 0:
  29.8 37.1 all-gather.1

commit v4 on v3

--- a/solution.py
+++ b/solution.py
@@ -192,7 +192,7 @@
 
 
 LANES = 128
-SHARES = (7, 6, 3)
+SHARES = (6, 5, 3, 2)
 STRIP = 16
 EDGE_ROWS = 16
 VMEM_BYTES = 60 * 2**20
@@ -397,16 +397,18 @@
     return (left.astype(jnp.float32) * right.astype(jnp.float32)).astype(jnp.bfloat16)
 
 
-def enter_kernel(first_ref, gate_ref, values_ref, cotangent_ref, out_gate_ref, *refs):
+def enter_kernel(first_ref, gate_ref, values_ref, cotangent_ref, out_gate_ref, *out_refs):
     channels, width = gate_ref.shape
-    *out_refs, turned = refs
-    rows = width // LANES
+    groups, rows = out_refs[0].shape[0], width // LANES
 
     def fill(left_ref, right_ref):
         made = product(left_ref[...], right_ref[...]).astype(jnp.float32)
-        for row in range(rows):
-            column = made[:, row * LANES : (row + 1) * LANES]
-            turned[pl.ds(row, channels, stride=rows), :] = column
+        made = made.reshape(channels, rows, LANES).astype(jnp.bfloat16)
+        made = made.reshape(groups, channels // groups, rows, LANES)
+        start = 0
+        for out_ref in out_refs:
+            out_ref[...] = made[:, start : start + out_ref.shape[1]]
+            start += out_ref.shape[1]
 
     @pl.when(first_ref[0] == 1)
     def _():
@@ -415,13 +417,6 @@
     @pl.when(first_ref[0] == 0)
     def _():
         fill(cotangent_ref, out_gate_ref)
-
-    groups = out_refs[0].shape[0]
-    made = turned[...].astype(jnp.bfloat16).reshape(groups, channels // groups, rows, LANES)
-    start = 0
-    for out_ref in out_refs:
-        out_ref[...] = made[:, start : start + out_ref.shape[1]]
-        start += out_ref.shape[1]
 
 
 def enter(first, flat, filters, counts):
@@ -440,7 +435,6 @@
                 pl.BlockSpec((groups, count, EDGE_ROWS, LANES), lambda i, first: (0, 0, i, 0))
                 for count in counts
             ],
-            scratch_shapes=[pltpu.VMEM((channels * EDGE_ROWS, LANES), jnp.float32)],
         ),
         out_shape=[
             jax.ShapeDtypeStruct((groups, count, rows, LANES), jnp.bfloat16) for count in counts
@@ -465,11 +459,8 @@
         signal, refs = signal + received.astype(jnp.float32), refs[parts:]
     if has_made:
         made_refs, refs = refs[:4], refs[4:]
-    *out_refs, turned = refs
-    turned[...] = signal.reshape(channels * rows, LANES)
-    signal = jnp.concatenate(
-        [turned[pl.ds(row, channels, stride=rows), :] for row in range(rows)], axis=1
-    )
+    out_refs = refs
+    signal = signal.reshape(channels, rows, LANES).reshape(channels, width)
     skip = skip_ref[...]
 
     def finish(left_ref, right_ref, factor_refs, result_refs, kept):
@@ -515,7 +506,6 @@
             ]
             + [still_block] * len(made),
             out_specs=[of_first, of_first, of_second, of_second],
-            scratch_shapes=[pltpu.VMEM((channels * EDGE_ROWS, LANES), jnp.float32)],
         ),
         out_shape=[jax.ShapeDtypeStruct((channels, local_len), jnp.bfloat16)] * 4,
         input_output_aliases={before + number: number for number in range(len(made))},

time: 360 us -> 348 us (0.967)
  waiting for transfers between devices: 105 us -> 80.8 us
  starting transfers between devices: 66.6 us -> 80.5 us
    ppermute x6 -> x9, starting transfers between devices: 23.7 us -> 34.3 us  [block_shards(): arrivals = [lax.ppermute(leaving, 'ctx', route) for route in routes]]
    ppermute x3, waiting for transfers between devices: 60.4 us -> 50.3 us  [block_shards(): arrivals = [lax.ppermute(own_parts[0], 'ctx', route) for route in routes]]
    ppermute x2 -> x3, waiting for transfers between devices: 10.9 us -> 2.13 us  [block_shards(): received_parts.append(lax.ppermute(pending[0], 'ctx', back_route))]
    ppermute x6 -> x9, waiting for transfers between devices: 20.3 us -> 16.7 us  [block_shards(): arrivals = [lax.ppermute(leaving, 'ctx', route) for route in routes]]
    all_to_all x3 -> x4, starting transfers between devices: 11.8 us -> 14.9 us  [lag_shares(): lax.all_to_all(pieces, 'dp', split_axis=0, concat_axis=0, tiled=True)]
    pallas_call x3 -> x4, Pallas kernels: 96.2 us -> 98.7 us  [block_products(): pl.pallas_call(block_kernel, grid=(filters,), in_specs=[pl.BlockSpec(memo...]
  transfers between devices with their start and end apart: 23 -> 28, of which waited for: 7 -> 8; matrix products, arithmetic and copies ran while one was open for 1% -> 0% of each run, Pallas kernels for 45% -> 46%
where the time goes in v4:
time: 348 us; the launch traced here: 345 us
  Pallas kernels  160 us (46%)
  waiting for transfers between devices  80.8 us (23%)
  starting transfers between devices  80.5 us (23%)
  between operations  14.5 us (4%)
  other arithmetic  5.9 us (2%)
  local copies, waits for them, and re-layouts  3.77 us (1%)
    pallas_call x4, Pallas kernels, block_products(): pl.pallas_call(block_kernel, grid=(filters,), in_specs=[pl.BlockSpec(memo...  98.7 us
    ppermute x3, waiting for transfers between devices, block_shards(): arrivals = [lax.ppermute(own_parts[0], 'ctx', route) for route in routes]  50.3 us
    pallas_call x2, Pallas kernels, leave(): pl.pallas_call(lambda *refs: leave_kernel(bool(received_parts), bool(made...  36.7 us
    ppermute x9, starting transfers between devices, block_shards(): arrivals = [lax.ppermute(leaving, 'ctx', route) for route in routes]  34.3 us
    pallas_call x2, Pallas kernels, enter(): pl.pallas_call(enter_kernel, grid_spec=pltpu.PrefetchScalarGridSpec(num_s...  24.6 us
    ppermute x9, waiting for transfers between devices, block_shards(): arrivals = [lax.ppermute(leaving, 'ctx', route) for route in routes]  16.7 us
    all_to_all x4, starting transfers between devices, lag_shares(): lax.all_to_all(pieces, 'dp', split_axis=0, concat_axis=0, tiled=True)  14.9 us
    ppermute x3, waiting for transfers between devices, lag_sum(): total += lax.ppermute(leaving, 'ctx', rotation(hop)).astype(jnp.float32)  11.7 us
  transfers between devices with their start and end apart: 28, of which 8 were waited for; matrix products, arithmetic and copies ran while one was open for 0% of the time, Pallas kernels for 46%

profile of v4, /device:TPU:0, one launch (start us, length us, event | category | flops | bytes accessed | tf_op | source)
XLA Modules:
  0.0 345.5 jit_solution(5590150550833395663)
XLA Ops:
  7.2 0.7 dynamic-slice_negate_fusion
  8.0 1.4 fusion.4
  9.4 5.1 %collective-permute-start = (bf16[1,2,256,128]{3,2,1,0:T(8,128)(2,1)S(1)}, bf16[1,2,256,128]{3,2,1,0:T(8,128)(2,1)S(1)}, u32[]{:S(2)}, u32[]{:S(2)}) collective-permute-start(bf16[1,2,256,128]{3,2,1,0:T(8,128)(2,1)S(1)} %copy.35), channel_id=1, source_target_pairs={{0,3},{1,0},{2,1},{3,2},{4,7},{5,4},{6,5},{7,6},{8,11},{9,8},{10,9... | collective-permute-start | bytes 393224 | tf_op jit(solution)/shard_map/ppermute | solution.py:556
  14.5 1.0 collective-permute-start.2
  15.5 12.3 %shard_map.164 = (bf16[4,6,256,128]{3,2,1,0:T(8,128)(2,1)}, bf16[4,5,256,128]{3,2,1,0:T(8,128)(2,1)}, bf16[4,3,256,128]{3,2,1,0:T(8,128)(2,1)}, bf16[4,2,256,128]{3,2,1,0:T(8,128)(2,1)}) custom-call(s32[1]{0:T(128)} %bitcast.first_ref.refs_0_, bf16[64,32768]{1,0:T(8,128)(2,1)} %refs_2_.3, bf16[64,32768]{1,0:T(8,128)(2,1)} %refs_3_.3, ...), custom_call_target="tpu_custom_call" | custom-call | flops 4194304 | bytes 12582912 | tf_op jit(solution)/shard_map/pallas_call | solution.py:428
  28.0 0.8 constant_dynamic-slice_fusion
  29.4 0.7 collective-permute-start.3
  30.2 8.2 %collective-permute-start.4 = (bf16[4,6,256,128]{3,2,1,0:T(8,128)(2,1)S(1)}, bf16[4,6,256,128]{3,2,1,0:T(8,128)(2,1)}, u32[]{:S(2)}, u32[]{:S(2)}) collective-permute-start(bf16[4,6,256,128]{3,2,1,0:T(8,128)(2,1)S(1)} %copy-done.1), channel_id=1, source_target_pairs={{0,2},{3,1},{4,6},{7,5},{8,10},{11,9},{12,14},{15,13},{16,18},{19,... | collective-permute-start | bytes 4718600 | tf_op jit(solution)/shard_map/ppermute | solution.py:560
  38.3 2.5 collective-permute-start.5
  40.9 12.3 %shard_map.165.other_own_ref = bf16[4,16,256,128]{3,2,1,0:T(8,128)(2,1)} custom-call(s32[1]{0:T(128)S(6)} %sub.7.first_ref.refs_0_, bf16[64,32768]{1,0:T(8,128)(2,1)} %refs_2_.3, bf16[64,32768]{1,0:T(8,128)(2,1)} %refs_3_.3, bf16[64,32768]{1,0:T(8,128)(2,1)} %refs_4_.3, bf16[64,32768]{1,0:T(8,128)(2,1)} %refs_5_.3), custom_call_target="tpu_custom_call" | custom-call | flops 4194304 | bytes 12582912 | tf_op jit(solution)/shard_map/pallas_call | solution.py:428
  53.2 18.8 %collective-permute-done.4.other_far_ref = bf16[4,6,256,128]{3,2,1,0:T(8,128)(2,1)} collective-permute-done((bf16[4,6,256,128]{3,2,1,0:T(8,128)(2,1)S(1)}, bf16[4,6,256,128]{3,2,1,0:T(8,128)(2,1)}, u32[]{:S(2)}, u32[]{:S(2)}) %collective-permute-start.4) | collective-permute-done | bytes 1572896 | tf_op jit(solution)/shard_map/ppermute | solution.py:560
  72.0 31.4 %collective-permute-done.5.far_ref = bf16[4,6,256,128]{3,2,1,0:T(8,128)(2,1)} collective-permute-done((bf16[4,6,256,128]{3,2,1,0:T(8,128)(2,1)S(1)}, bf16[4,6,256,128]{3,2,1,0:T(8,128)(2,1)}, u32[]{:S(2)}, u32[]{:S(2)}) %collective-permute-start.5) | collective-permute-done | bytes 1572896 | tf_op jit(solution)/shard_map/ppermute | solution.py:560
  103.4 0.7 collective-permute-start.6
  104.2 8.2 %collective-permute-start.7 = (bf16[4,5,256,128]{3,2,1,0:T(8,128)(2,1)}, bf16[4,5,256,128]{3,2,1,0:T(8,128)(2,1)}, u32[]{:S(2)}, u32[]{:S(2)}) collective-permute-start(bf16[4,5,256,128]{3,2,1,0:T(8,128)(2,1)} %get-tuple-element.117.own_ref), channel_id=1, source_target_pairs={{0,2},{3,1},{4,6},{7,5},{8,10},{11,9},{12,14},{15,13},{16,18},{19,... | collective-permute-start | bytes 3932168 | tf_op jit(solution)/shard_map/ppermute | solution.py:592
  112.4 2.4 collective-permute-start.8
  114.7 35.6 %shard_map.166 = (bf16[4,6,256,128]{3,2,1,0:T(8,128)(2,1)}, bf16[4,6,256,128]{3,2,1,0:T(8,128)(2,1)}, bf16[4,6,256,128]{3,2,1,0:T(8,128)(2,1)}, bf16[8,4,6,32,128]{4,3,2,1,0:T(8,128)(2,1)}) custom-call(f32[1]{0:T(128)} %bitcast.2.side_ref, bf16[4,6,256,128]{3,2,1,0:T(8,128)(2,1)} %get-tuple-element.105.own_ref, ...), custom_call_target="tpu_custom_call" | custom-call | flops 1 | bytes 1 | tf_op jit(solution)/shard_map/pallas_call | solution.py:379
  150.4 15.1 %collective-permute-done.8.far_ref = bf16[4,5,256,128]{3,2,1,0:T(8,128)(2,1)} collective-permute-done((bf16[4,5,256,128]{3,2,1,0:T(8,128)(2,1)}, bf16[4,5,256,128]{3,2,1,0:T(8,128)(2,1)}, u32[]{:S(2)}, u32[]{:S(2)}) %collective-permute-start.8) | collective-permute-done | bytes 1310752 | tf_op jit(solution)/shard_map/ppermute | solution.py:592
  165.5 1.3 collective-permute-start.12
  166.8 3.7 %all-to-all-start = ((bf16[8,4,6,32,128]{4,3,2,1,0:T(8,128)(2,1)}), bf16[8,4,6,32,128]{4,3,2,1,0:T(8,128)(2,1)S(1)}, u32[]{:S(2)}, u32[]{:S(2)}) async-start(bf16[8,4,6,32,128]{4,3,2,1,0:T(8,128)(2,1)} %get-tuple-element.128), calls=%async_computation | async-start | bytes 3145728 | tf_op jit(solution)/shard_map/all_to_all | solution.py:565
  170.5 1.5 collective-permute-start.9
  172.1 7.4 %collective-permute-start.10 = (bf16[4,3,256,128]{3,2,1,0:T(8,128)(2,1)}, bf16[4,3,256,128]{3,2,1,0:T(8,128)(2,1)}, u32[]{:S(2)}, u32[]{:S(2)}) collective-permute-start(bf16[4,3,256,128]{3,2,1,0:T(8,128)(2,1)} %get-tuple-element.131.own_ref), channel_id=1, source_target_pairs={{0,2},{3,1},{4,6},{7,5},{8,10},{11,9},{12,14},{15,13},{16,18},{19,... | collective-permute-start | bytes 2359304 | tf_op jit(solution)/shard_map/ppermute | solution.py:592
  179.4 2.2 collective-permute-start.11
  181.6 30.3 %shard_map.167 = (bf16[4,5,256,128]{3,2,1,0:T(8,128)(2,1)}, bf16[4,5,256,128]{3,2,1,0:T(8,128)(2,1)}, bf16[4,5,256,128]{3,2,1,0:T(8,128)(2,1)}, bf16[8,4,5,32,128]{4,3,2,1,0:T(8,128)(2,1)}) custom-call(f32[1]{0:T(128)} %bitcast.2.side_ref, bf16[4,5,256,128]{3,2,1,0:T(8,128)(2,1)} %get-tuple-element.117.own_ref, ...), custom_call_target="tpu_custom_call" | custom-call | flops 1 | bytes 1 | tf_op jit(solution)/shard_map/pallas_call | solution.py:379
  212.2 0.7 collective-permute-done.11.far_ref
  212.9 1.3 collective-permute-start.16
  214.2 3.9 %all-to-all-start.1 = ((bf16[8,4,5,32,128]{4,3,2,1,0:T(8,128)(2,1)}), bf16[8,4,5,32,128]{4,3,2,1,0:T(8,128)(2,1)S(1)}, u32[]{:S(2)}, u32[]{:S(2)}) async-start(bf16[8,4,5,32,128]{4,3,2,1,0:T(8,128)(2,1)} %get-tuple-element.143), calls=%async_computation.1 | async-start | bytes 2621440 | tf_op jit(solution)/shard_map/all_to_all | solution.py:565
  218.1 1.5 collective-permute-start.13
  219.5 8.3 %collective-permute-start.14 = (bf16[4,2,256,128]{3,2,1,0:T(8,128)(2,1)}, bf16[4,2,256,128]{3,2,1,0:T(8,128)(2,1)}, u32[]{:S(2)}, u32[]{:S(2)}) collective-permute-start(bf16[4,2,256,128]{3,2,1,0:T(8,128)(2,1)} %get-tuple-element.147.own_ref), channel_id=1, source_target_pairs={{0,2},{3,1},{4,6},{7,5},{8,10},{11,9},{12,14},{15,13},{16,18},{19,... | collective-permute-start | bytes 1572872 | tf_op jit(solution)/shard_map/ppermute | solution.py:592
  227.8 2.1 collective-permute-start.15
  229.9 19.1 %shard_map.168 = (bf16[4,3,256,128]{3,2,1,0:T(8,128)(2,1)}, bf16[4,3,256,128]{3,2,1,0:T(8,128)(2,1)}, bf16[4,3,256,128]{3,2,1,0:T(8,128)(2,1)}, bf16[8,4,3,32,128]{4,3,2,1,0:T(8,128)(2,1)}) custom-call(f32[1]{0:T(128)} %bitcast.2.side_ref, bf16[4,3,256,128]{3,2,1,0:T(8,128)(2,1)} %get-tuple-element.131.own_ref, ...), custom_call_target="tpu_custom_call" | custom-call | flops 1 | bytes 1 | tf_op jit(solution)/shard_map/pallas_call | solution.py:379
  249.3 0.8 collective-permute-done.15.far_ref
  250.2 1.3 collective-permute-start.17
  251.5 3.9 %all-to-all-start.2 = ((bf16[8,4,3,32,128]{4,3,2,1,0:T(8,128)(2,1)}), bf16[8,4,3,32,128]{4,3,2,1,0:T(8,128)(2,1)S(1)}, u32[]{:S(2)}, u32[]{:S(2)}) async-start(bf16[8,4,3,32,128]{4,3,2,1,0:T(8,128)(2,1)} %get-tuple-element.160), calls=%async_computation.2 | async-start | bytes 1572864 | tf_op jit(solution)/shard_map/all_to_all | solution.py:565
  255.3 13.7 %shard_map.169 = (bf16[4,2,256,128]{3,2,1,0:T(8,128)(2,1)}, bf16[4,2,256,128]{3,2,1,0:T(8,128)(2,1)}, bf16[4,2,256,128]{3,2,1,0:T(8,128)(2,1)}, bf16[8,4,2,32,128]{4,3,2,1,0:T(8,128)(2,1)}) custom-call(f32[1]{0:T(128)} %bitcast.2.side_ref, bf16[4,2,256,128]{3,2,1,0:T(8,128)(2,1)} %get-tuple-element.147.own_ref, ...), custom_call_target="tpu_custom_call" | custom-call | flops 1 | bytes 1 | tf_op jit(solution)/shard_map/pallas_call | solution.py:379
  269.1 2.1 collective-permute-done.17.refs_12_
  271.3 1.3 collective-permute-start.18
  272.5 3.5 %all-to-all-start.3 = ((bf16[8,4,2,32,128]{4,3,2,1,0:T(8,128)(2,1)}), bf16[8,4,2,32,128]{4,3,2,1,0:T(8,128)(2,1)S(1)}, u32[]{:S(2)}, u32[]{:S(2)}) async-start(bf16[8,4,2,32,128]{4,3,2,1,0:T(8,128)(2,1)} %get-tuple-element.169), calls=%async_computation.3 | async-start | bytes 1048576 | tf_op jit(solution)/shard_map/all_to_all | solution.py:565
  276.1 0.7 copy.27.refs_1_
  276.8 17.5 %shard_map.170 = (bf16[64,32768]{1,0:T(8,128)(2,1)}, bf16[64,32768]{1,0:T(8,128)(2,1)}, bf16[64,32768]{1,0:T(8,128)(2,1)}, bf16[64,32768]{1,0:T(8,128)(2,1)}) custom-call(s32[1]{0:T(128)} %bitcast.first_ref.refs_0_, f32[64,1]{1,0:T(8,128)} %copy.27.refs_1_, bf16[64,32768]{1,0:T(8,128)(2,1)} %refs_2_.3, bf16[64,32768]{1,0:T(8,128)(2,1)} %refs_3_.3, ...), custom_call_target="tpu_custom_call" | custom-call | flops 16777216 | bytes 29360128 | tf_op jit(solution)/shard_map/pallas_call | solution.py:496
  294.6 1.5 collective-permute-start.21
  296.1 2.7 collective-permute-start.20
  298.8 0.6 collective-permute-start.19
  299.4 2.1 collective-permute-done.21
  301.4 9.6 %collective-permute-done.20 = bf16[16,32,128]{2,1,0:T(8,128)(2,1)S(1)} collective-permute-done((bf16[16,32,128]{2,1,0:T(8,128)(2,1)S(1)}, bf16[16,32,128]{2,1,0:T(8,128)(2,1)S(1)}, u32[]{:S(2)}, u32[]{:S(2)}) %collective-permute-start.20) | collective-permute-done | bytes 131104 | tf_op jit(solution)/shard_map/ppermute | solution.py:575
  311.1 1.2 broadcast_in_dim.5
  312.3 3.8 %all-to-all-start.4 = ((bf16[8,16,32,128]{3,2,1,0:T(8,128)(2,1)}), bf16[8,16,32,128]{3,2,1,0:T(8,128)(2,1)S(1)}, u32[]{:S(2)}, u32[]{:S(2)}) async-start(bf16[8,16,32,128]{3,2,1,0:T(8,128)(2,1)} %broadcast_in_dim.5), calls=%async_computation.4 | async-start | bytes 2097152 | tf_op jit(solution)/shard_map/all_to_all | solution.py:578
  316.1 19.2 %shard_map.171 = (bf16[64,32768]{1,0:T(8,128)(2,1)}, bf16[64,32768]{1,0:T(8,128)(2,1)}, bf16[64,32768]{1,0:T(8,128)(2,1)}, bf16[64,32768]{1,0:T(8,128)(2,1)}) custom-call(s32[1]{0:T(128)S(6)} %sub.7.first_ref.refs_0_, f32[64,1]{1,0:T(8,128)} %copy.27.refs_1_, ...), custom_call_target="tpu_custom_call", output_to_operand_aliasing={{0}: (14, {}), {1}: (15, {}), {2}: (16, {}), {3}: (17, {})} | custom-call | flops 16777216 | bytes 29360128 | tf_op jit(solution)/shard_map/pallas_call | solution.py:496
  335.9 2.7 fusion
  (61 shorter events, 2.2 us)
Async XLA Ops:
  7.2 107.6 %all-gather.2.cloned.1.call-start = ((), (), s32[]{:S(2)}) async-start(), calls=%async_computation.5 | async-start | bytes 4718592 | tf_op jit(solution)/shard_map/all_gather | solution.py:561
  9.4 18.4 %collective-permute-start = (bf16[1,2,256,128]{3,2,1,0:T(8,128)(2,1)S(1)}, bf16[1,2,256,128]{3,2,1,0:T(8,128)(2,1)S(1)}, u32[]{:S(2)}, u32[]{:S(2)}) collective-permute-start(bf16[1,2,256,128]{3,2,1,0:T(8,128)(2,1)S(1)} %copy.35), channel_id=1, source_target_pairs={{0,3},{1,0},{2,1},{3,2},{4,7},{5,4},{6,5},{7,6},{8,11},{9,8},{10,9... | collective-permute-start | bytes 393224 | tf_op jit(solution)/shard_map/ppermute | solution.py:556
  14.5 13.3 %collective-permute-start.1 = (bf16[1,2,256,128]{3,2,1,0:T(8,128)(2,1)S(1)}, bf16[1,2,256,128]{3,2,1,0:T(8,128)(2,1)S(1)}, u32[]{:S(2)}, u32[]{:S(2)}) collective-permute-start(bf16[1,2,256,128]{3,2,1,0:T(8,128)(2,1)S(1)} %copy.35), channel_id=1, source_target_pairs={{0,2},{1,3},{2,0},{3,1},{4,6},{5,7},{6,4},{7,5},{8,10},{9,11},{10,... | collective-permute-start | bytes 393224 | tf_op jit(solution)/shard_map/ppermute | solution.py:556
  14.5 13.4 %collective-permute-start.2 = (bf16[1,2,256,128]{3,2,1,0:T(8,128)(2,1)S(1)}, bf16[1,2,256,128]{3,2,1,0:T(8,128)(2,1)S(1)}, u32[]{:S(2)}, u32[]{:S(2)}) collective-permute-start(bf16[1,2,256,128]{3,2,1,0:T(8,128)(2,1)S(1)} %copy.35), channel_id=1, source_target_pairs={{0,1},{1,2},{2,3},{3,0},{4,5},{5,6},{6,7},{7,4},{8,9},{9,10},{10,1... | collective-permute-start | bytes 393224 | tf_op jit(solution)/shard_map/ppermute | solution.py:556
  27.8 1.6 copy-start.1
  29.4 23.8 %collective-permute-start.3 = (bf16[4,6,256,128]{3,2,1,0:T(8,128)(2,1)S(1)}, bf16[4,6,256,128]{3,2,1,0:T(8,128)(2,1)S(1)}, u32[]{:S(2)}, u32[]{:S(2)}) collective-permute-start(bf16[4,6,256,128]{3,2,1,0:T(8,128)(2,1)S(1)} %copy-done.1), channel_id=1, source_target_pairs={{1,2},{2,1},{5,6},{6,5},{9,10},{10,9},{13,14},{14,13},{17,18},{18,... | collective-permute-start | bytes 4718600 | tf_op jit(solution)/shard_map/ppermute | solution.py:560
  30.2 41.8 %collective-permute-start.4 = (bf16[4,6,256,128]{3,2,1,0:T(8,128)(2,1)S(1)}, bf16[4,6,256,128]{3,2,1,0:T(8,128)(2,1)}, u32[]{:S(2)}, u32[]{:S(2)}) collective-permute-start(bf16[4,6,256,128]{3,2,1,0:T(8,128)(2,1)S(1)} %copy-done.1), channel_id=1, source_target_pairs={{0,2},{3,1},{4,6},{7,5},{8,10},{11,9},{12,14},{15,13},{16,18},{19,... | collective-permute-start | bytes 4718600 | tf_op jit(solution)/shard_map/ppermute | solution.py:560
  38.3 65.1 %collective-permute-start.5 = (bf16[4,6,256,128]{3,2,1,0:T(8,128)(2,1)S(1)}, bf16[4,6,256,128]{3,2,1,0:T(8,128)(2,1)}, u32[]{:S(2)}, u32[]{:S(2)}) collective-permute-start(bf16[4,6,256,128]{3,2,1,0:T(8,128)(2,1)S(1)} %copy-done.1), channel_id=1, source_target_pairs={{0,1},{3,2},{4,5},{7,6},{8,9},{11,10},{12,13},{15,14},{16,17},{19,... | collective-permute-start | bytes 4718600 | tf_op jit(solution)/shard_map/ppermute | solution.py:560
  53.2 61.6 %copy-start.2 = (bf16[4,6,256,128]{3,2,1,0:T(8,128)(2,1)}, bf16[4,6,256,128]{3,2,1,0:T(8,128)(2,1)S(1)}, u32[]{:S(2)}) copy-start(bf16[4,6,256,128]{3,2,1,0:T(8,128)(2,1)S(1)} %collective-permute-done.3.other_next_ref) | copy-start | bytes 4718596
  103.4 46.9 %collective-permute-start.6 = (bf16[4,5,256,128]{3,2,1,0:T(8,128)(2,1)}, bf16[4,5,256,128]{3,2,1,0:T(8,128)(2,1)S(1)}, u32[]{:S(2)}, u32[]{:S(2)}) collective-permute-start(bf16[4,5,256,128]{3,2,1,0:T(8,128)(2,1)} %get-tuple-element.117.own_ref), channel_id=1, source_target_pairs={{1,2},{2,1},{5,6},{6,5},{9,10},{10,9},{13,14},{14,13},{17,18},{18,... | collective-permute-start | bytes 3932168 | tf_op jit(solution)/shard_map/ppermute | solution.py:592
  104.2 46.2 %collective-permute-start.7 = (bf16[4,5,256,128]{3,2,1,0:T(8,128)(2,1)}, bf16[4,5,256,128]{3,2,1,0:T(8,128)(2,1)}, u32[]{:S(2)}, u32[]{:S(2)}) collective-permute-start(bf16[4,5,256,128]{3,2,1,0:T(8,128)(2,1)} %get-tuple-element.117.own_ref), channel_id=1, source_target_pairs={{0,2},{3,1},{4,6},{7,5},{8,10},{11,9},{12,14},{15,13},{16,18},{19,... | collective-permute-start | bytes 3932168 | tf_op jit(solution)/shard_map/ppermute | solution.py:592
  112.4 53.1 %collective-permute-start.8 = (bf16[4,5,256,128]{3,2,1,0:T(8,128)(2,1)}, bf16[4,5,256,128]{3,2,1,0:T(8,128)(2,1)}, u32[]{:S(2)}, u32[]{:S(2)}) collective-permute-start(bf16[4,5,256,128]{3,2,1,0:T(8,128)(2,1)} %get-tuple-element.117.own_ref), channel_id=1, source_target_pairs={{0,1},{3,2},{4,5},{7,6},{8,9},{11,10},{12,13},{15,14},{16,17},{19,... | collective-permute-start | bytes 3932168 | tf_op jit(solution)/shard_map/ppermute | solution.py:592
  150.4 15.1 %copy-start.3 = (bf16[4,5,256,128]{3,2,1,0:T(8,128)(2,1)}, bf16[4,5,256,128]{3,2,1,0:T(8,128)(2,1)S(1)}, u32[]{:S(2)}) copy-start(bf16[4,5,256,128]{3,2,1,0:T(8,128)(2,1)S(1)} %collective-permute-done.6.other_next_ref) | copy-start | bytes 3932164
  165.5 47.4 %collective-permute-start.12 = (bf16[4,6,256,128]{3,2,1,0:T(8,128)(2,1)}, bf16[4,6,256,128]{3,2,1,0:T(8,128)(2,1)S(1)}, u32[]{:S(2)}, u32[]{:S(2)}) collective-permute-start(bf16[4,6,256,128]{3,2,1,0:T(8,128)(2,1)} %get-tuple-element.127), channel_id=1, source_target_pairs={{1,0},{2,3},{5,4},{6,7},{9,8},{10,11},{13,12},{14,15},{17,16},{18,... | collective-permute-start | bytes 4718600 | tf_op jit(solution)/shard_map/ppermute | solution.py:594
  166.8 45.1 %all-to-all-start = ((bf16[8,4,6,32,128]{4,3,2,1,0:T(8,128)(2,1)}), bf16[8,4,6,32,128]{4,3,2,1,0:T(8,128)(2,1)S(1)}, u32[]{:S(2)}, u32[]{:S(2)}) async-start(bf16[8,4,6,32,128]{4,3,2,1,0:T(8,128)(2,1)} %get-tuple-element.128), calls=%async_computation | async-start | bytes 3145728 | tf_op jit(solution)/shard_map/all_to_all | solution.py:565
  170.5 41.6 %collective-permute-start.9 = (bf16[4,3,256,128]{3,2,1,0:T(8,128)(2,1)}, bf16[4,3,256,128]{3,2,1,0:T(8,128)(2,1)}, u32[]{:S(2)}, u32[]{:S(2)}) collective-permute-start(bf16[4,3,256,128]{3,2,1,0:T(8,128)(2,1)} %get-tuple-element.131.own_ref), channel_id=1, source_target_pairs={{1,2},{2,1},{5,6},{6,5},{9,10},{10,9},{13,14},{14,13},{17,18},{18,... | collective-permute-start | bytes 2359304 | tf_op jit(solution)/shard_map/ppermute | solution.py:592
  172.1 40.1 %collective-permute-start.10 = (bf16[4,3,256,128]{3,2,1,0:T(8,128)(2,1)}, bf16[4,3,256,128]{3,2,1,0:T(8,128)(2,1)}, u32[]{:S(2)}, u32[]{:S(2)}) collective-permute-start(bf16[4,3,256,128]{3,2,1,0:T(8,128)(2,1)} %get-tuple-element.131.own_ref), channel_id=1, source_target_pairs={{0,2},{3,1},{4,6},{7,5},{8,10},{11,9},{12,14},{15,13},{16,18},{19,... | collective-permute-start | bytes 2359304 | tf_op jit(solution)/shard_map/ppermute | solution.py:592
  179.4 33.5 %collective-permute-start.11 = (bf16[4,3,256,128]{3,2,1,0:T(8,128)(2,1)}, bf16[4,3,256,128]{3,2,1,0:T(8,128)(2,1)}, u32[]{:S(2)}, u32[]{:S(2)}) collective-permute-start(bf16[4,3,256,128]{3,2,1,0:T(8,128)(2,1)} %get-tuple-element.131.own_ref), channel_id=1, source_target_pairs={{0,1},{3,2},{4,5},{7,6},{8,9},{11,10},{12,13},{15,14},{16,17},{19,... | collective-permute-start | bytes 2359304 | tf_op jit(solution)/shard_map/ppermute | solution.py:592
  212.9 36.2 %copy-start = (bf16[4,6,256,128]{3,2,1,0:T(8,128)(2,1)}, bf16[4,6,256,128]{3,2,1,0:T(8,128)(2,1)S(1)}, u32[]{:S(2)}) copy-start(bf16[4,6,256,128]{3,2,1,0:T(8,128)(2,1)S(1)} %collective-permute-done.12.refs_10_) | copy-start | bytes 4718596
  212.9 37.2 %collective-permute-start.16 = (bf16[4,5,256,128]{3,2,1,0:T(8,128)(2,1)}, bf16[4,5,256,128]{3,2,1,0:T(8,128)(2,1)}, u32[]{:S(2)}, u32[]{:S(2)}) collective-permute-start(bf16[4,5,256,128]{3,2,1,0:T(8,128)(2,1)} %get-tuple-element.141), channel_id=1, source_target_pairs={{1,0},{2,3},{5,4},{6,7},{9,8},{10,11},{13,12},{14,15},{17,16},{18,... | collective-permute-start | bytes 3932168 | tf_op jit(solution)/shard_map/ppermute | solution.py:594
  214.2 34.9 %all-to-all-start.1 = ((bf16[8,4,5,32,128]{4,3,2,1,0:T(8,128)(2,1)}), bf16[8,4,5,32,128]{4,3,2,1,0:T(8,128)(2,1)S(1)}, u32[]{:S(2)}, u32[]{:S(2)}) async-start(bf16[8,4,5,32,128]{4,3,2,1,0:T(8,128)(2,1)} %get-tuple-element.143), calls=%async_computation.1 | async-start | bytes 2621440 | tf_op jit(solution)/shard_map/all_to_all | solution.py:565
  218.1 31.2 %collective-permute-start.13 = (bf16[4,2,256,128]{3,2,1,0:T(8,128)(2,1)}, bf16[4,2,256,128]{3,2,1,0:T(8,128)(2,1)}, u32[]{:S(2)}, u32[]{:S(2)}) collective-permute-start(bf16[4,2,256,128]{3,2,1,0:T(8,128)(2,1)} %get-tuple-element.147.own_ref), channel_id=1, source_target_pairs={{1,2},{2,1},{5,6},{6,5},{9,10},{10,9},{13,14},{14,13},{17,18},{18,... | collective-permute-start | bytes 1572872 | tf_op jit(solution)/shard_map/ppermute | solution.py:592
  219.5 29.8 %collective-permute-start.14 = (bf16[4,2,256,128]{3,2,1,0:T(8,128)(2,1)}, bf16[4,2,256,128]{3,2,1,0:T(8,128)(2,1)}, u32[]{:S(2)}, u32[]{:S(2)}) collective-permute-start(bf16[4,2,256,128]{3,2,1,0:T(8,128)(2,1)} %get-tuple-element.147.own_ref), channel_id=1, source_target_pairs={{0,2},{3,1},{4,6},{7,5},{8,10},{11,9},{12,14},{15,13},{16,18},{19,... | collective-permute-start | bytes 1572872 | tf_op jit(solution)/shard_map/ppermute | solution.py:592
  227.8 22.4 %collective-permute-start.15 = (bf16[4,2,256,128]{3,2,1,0:T(8,128)(2,1)}, bf16[4,2,256,128]{3,2,1,0:T(8,128)(2,1)}, u32[]{:S(2)}, u32[]{:S(2)}) collective-permute-start(bf16[4,2,256,128]{3,2,1,0:T(8,128)(2,1)} %get-tuple-element.147.own_ref), channel_id=1, source_target_pairs={{0,1},{3,2},{4,5},{7,6},{8,9},{11,10},{12,13},{15,14},{16,17},{19,... | collective-permute-start | bytes 1572872 | tf_op jit(solution)/shard_map/ppermute | solution.py:592
  250.2 21.1 %collective-permute-start.17 = (bf16[4,3,256,128]{3,2,1,0:T(8,128)(2,1)}, bf16[4,3,256,128]{3,2,1,0:T(8,128)(2,1)S(1)}, u32[]{:S(2)}, u32[]{:S(2)}) collective-permute-start(bf16[4,3,256,128]{3,2,1,0:T(8,128)(2,1)} %get-tuple-element.157), channel_id=1, source_target_pairs={{1,0},{2,3},{5,4},{6,7},{9,8},{10,11},{13,12},{14,15},{17,16},{18,... | collective-permute-start | bytes 2359304 | tf_op jit(solution)/shard_map/ppermute | solution.py:594
  251.5 17.5 %all-to-all-start.2 = ((bf16[8,4,3,32,128]{4,3,2,1,0:T(8,128)(2,1)}), bf16[8,4,3,32,128]{4,3,2,1,0:T(8,128)(2,1)S(1)}, u32[]{:S(2)}, u32[]{:S(2)}) async-start(bf16[8,4,3,32,128]{4,3,2,1,0:T(8,128)(2,1)} %get-tuple-element.160), calls=%async_computation.2 | async-start | bytes 1572864 | tf_op jit(solution)/shard_map/all_to_all | solution.py:565
  255.3 20.8 %copy-start.6 = (f32[64]{0:T(128)S(1)}, f32[64]{0:T(128)}, u32[]{:S(2)}) copy-start(f32[64]{0:T(128)} %param.19) | copy-start | bytes 772
  271.3 23.1 %copy-start.4 = (bf16[4,3,256,128]{3,2,1,0:T(8,128)(2,1)}, bf16[4,3,256,128]{3,2,1,0:T(8,128)(2,1)S(1)}, u32[]{:S(2)}) copy-start(bf16[4,3,256,128]{3,2,1,0:T(8,128)(2,1)S(1)} %collective-permute-done.17.refs_12_) | copy-start | bytes 2359300
  271.3 23.2 %collective-permute-start.18 = (bf16[4,2,256,128]{3,2,1,0:T(8,128)(2,1)}, bf16[4,2,256,128]{3,2,1,0:T(8,128)(2,1)S(1)}, u32[]{:S(2)}, u32[]{:S(2)}) collective-permute-start(bf16[4,2,256,128]{3,2,1,0:T(8,128)(2,1)} %get-tuple-element.168), channel_id=1, source_target_pairs={{1,0},{2,3},{5,4},{6,7},{9,8},{10,11},{13,12},{14,15},{17,16},{18,... | collective-permute-start | bytes 1572872 | tf_op jit(solution)/shard_map/ppermute | solution.py:605
  272.5 21.9 %all-to-all-start.3 = ((bf16[8,4,2,32,128]{4,3,2,1,0:T(8,128)(2,1)}), bf16[8,4,2,32,128]{4,3,2,1,0:T(8,128)(2,1)S(1)}, u32[]{:S(2)}, u32[]{:S(2)}) async-start(bf16[8,4,2,32,128]{4,3,2,1,0:T(8,128)(2,1)} %get-tuple-element.169), calls=%async_computation.3 | async-start | bytes 1048576 | tf_op jit(solution)/shard_map/all_to_all | solution.py:565
  294.5 17.8 %copy-start.5 = (bf16[4,2,256,128]{3,2,1,0:T(8,128)(2,1)}, bf16[4,2,256,128]{3,2,1,0:T(8,128)(2,1)S(1)}, u32[]{:S(2)}) copy-start(bf16[4,2,256,128]{3,2,1,0:T(8,128)(2,1)S(1)} %collective-permute-done.18.refs_13_) | copy-start | bytes 1572868
  294.6 21.6 %copy-start.7 = (f32[16]{0:T(128)S(1)}, f32[16]{0:T(128)}, u32[]{:S(2)}) copy-start(f32[16]{0:T(128)} %param.18) | copy-start | bytes 196
  294.6 6.8 %collective-permute-start.21 = (bf16[16,32,128]{2,1,0:T(8,128)(2,1)S(1)}, bf16[16,32,128]{2,1,0:T(8,128)(2,1)S(1)}, u32[]{:S(2)}, u32[]{:S(2)}) collective-permute-start(bf16[16,32,128]{2,1,0:T(8,128)(2,1)S(1)} %get-tuple-element.192), channel_id=1, source_target_pairs={{0,3},{1,0},{2,1},{3,2},{4,7},{5,4},{6,5},{7,6},{8,11},{9,8},{10,9... | collective-permute-start | bytes 393224 | tf_op jit(solution)/shard_map/ppermute | solution.py:575
  296.1 14.9 %collective-permute-start.20 = (bf16[16,32,128]{2,1,0:T(8,128)(2,1)S(1)}, bf16[16,32,128]{2,1,0:T(8,128)(2,1)S(1)}, u32[]{:S(2)}, u32[]{:S(2)}) collective-permute-start(bf16[16,32,128]{2,1,0:T(8,128)(2,1)S(1)} %get-tuple-element.193), channel_id=1, source_target_pairs={{0,2},{1,3},{2,0},{3,1},{4,6},{5,7},{6,4},{7,5},{8,10},{9,11},{10,... | collective-permute-start | bytes 393224 | tf_op jit(solution)/shard_map/ppermute | solution.py:575
  298.8 12.2 %collective-permute-start.19 = (bf16[16,32,128]{2,1,0:T(8,128)(2,1)S(1)}, bf16[16,32,128]{2,1,0:T(8,128)(2,1)S(1)}, u32[]{:S(2)}, u32[]{:S(2)}) collective-permute-start(bf16[16,32,128]{2,1,0:T(8,128)(2,1)S(1)} %get-tuple-element.191), channel_id=1, source_target_pairs={{0,1},{1,2},{2,3},{3,0},{4,5},{5,6},{6,7},{7,4},{8,9},{9,10},{10,1... | collective-permute-start | bytes 393224 | tf_op jit(solution)/shard_map/ppermute | solution.py:575
  312.3 23.1 %all-to-all-start.4 = ((bf16[8,16,32,128]{3,2,1,0:T(8,128)(2,1)}), bf16[8,16,32,128]{3,2,1,0:T(8,128)(2,1)S(1)}, u32[]{:S(2)}, u32[]{:S(2)}) async-start(bf16[8,16,32,128]{3,2,1,0:T(8,128)(2,1)} %broadcast_in_dim.5), calls=%async_computation.4 | async-start | bytes 2097152 | tf_op jit(solution)/shard_map/all_to_all | solution.py:578
Sparse Core Ops, SparseCore 0:
  29.0 37.0 all-gather.1

commit v5 on v4

--- a/solution.py
+++ b/solution.py
@@ -192,9 +192,9 @@
 
 
 LANES = 128
-SHARES = (6, 5, 3, 2)
+SHARES = (7, 5, 4)
 STRIP = 16
-EDGE_ROWS = 16
+EDGE_ROWS = 32
 VMEM_BYTES = 60 * 2**20
 
 
@@ -565,7 +565,7 @@
         pieces = lax.all_to_all(pieces, "dp", split_axis=0, concat_axis=0, tiled=True)
         return jnp.sum(pieces.astype(jnp.float32), axis=0).astype(jnp.bfloat16)
 
-    def lag_sum(pieces):
+    def lag_block(pieces):
         def block(index):
             return lax.dynamic_index_in_dim(pieces, index, 0, keepdims=False)
 
@@ -573,7 +573,9 @@
         for hop in (1, 2, 3):
             leaving = block((context_index + hop) % 4)
             total += lax.ppermute(leaving, "ctx", rotation(hop)).astype(jnp.float32)
-        total = total.astype(jnp.bfloat16)
+        return total.astype(jnp.bfloat16)
+
+    def lag_rows(total):
         spread = jnp.broadcast_to(total[None], (data_size, *total.shape))
         spread = lax.all_to_all(spread, "dp", split_axis=0, concat_axis=0, tiled=True)
         return jnp.transpose(spread, (1, 0, 2, 3)).reshape(total.shape[0], rows, LANES)
@@ -604,13 +606,16 @@
     )
     received = lax.ppermute(pending[0], "ctx", back_route)
     made = leave(near_start, skip_gain, flat, near_parts)
-    received, late, made = lax.optimization_barrier((received, lag_shares(pending[1]), made))
+    early = lag_block(jnp.concatenate(lag_parts, axis=1))
+    received, early, late, made, rest = lax.optimization_barrier(
+        (received, early, lag_shares(pending[1]), made, rest)
+    )
     received_parts.append(received)
-    lag = lag_sum(jnp.concatenate([*lag_parts, late], axis=1)).reshape(filters, local_len)
+    final = leave(rest, skip_gain, flat, other_parts, received_parts, made)
+    early, late, final = lax.optimization_barrier((lag_rows(early), lag_block(late), final))
+    outputs, grad_output_gate, grad_input_gate, grad_values = final
+    lag = jnp.concatenate([early, lag_rows(late)], axis=0).reshape(filters, local_len)
     grad_filter = lag.astype(jnp.float32) * envelope(filter_decay) * filter_scale
-    outputs, grad_output_gate, grad_input_gate, grad_values = leave(
-        1 - near_start, skip_gain, flat, other_parts, received_parts, made
-    )
     return (outputs, grad_input_gate, grad_output_gate, grad_values, grad_filter)
 
 

time: 348 us -> 345 us (level)
  waiting for transfers between devices: 80.8 us -> 99.1 us
  Pallas kernels: 160 us -> 146 us
  starting transfers between devices: 80.5 us -> 74.6 us
    ppermute x3, waiting for transfers between devices: 50.3 us -> 64.8 us  [block_shards(): arrivals = [lax.ppermute(own_parts[0], 'ctx', route) for route in routes]]
    ppermute x9 -> x6, starting transfers between devices: 34.3 us -> 22.2 us  [block_shards(): arrivals = [lax.ppermute(leaving, 'ctx', route) for route in routes]]
    ppermute x3 -> x6, waiting for transfers between devices: 11.7 us -> 3.72 us  [lag_block(): total += lax.ppermute(leaving, 'ctx', rotation(hop)).astype(jnp.float32)]
    ppermute x3 -> x6, starting transfers between devices: 4.75 us -> 12 us  [lag_block(): total += lax.ppermute(leaving, 'ctx', rotation(hop)).astype(jnp.float32)]
    pallas_call x2, Pallas kernels: 24.6 us -> 17.8 us  [enter(): pl.pallas_call(enter_kernel, grid_spec=pltpu.PrefetchScalarGridSpec(num_s...]
    all_to_all x1 -> x2, waiting for transfers between devices: 0.01 us -> 6.13 us  [lag_rows(): lax.all_to_all(spread, 'dp', split_axis=0, concat_axis=0, tiled=True)]
    pallas_call x2, Pallas kernels: 36.7 us -> 32.2 us  [leave(): pl.pallas_call(lambda *refs: leave_kernel(bool(received_parts), bool(made...]
    all_to_all x1 -> x2, starting transfers between devices: 3.84 us -> 7.97 us  [lag_rows(): lax.all_to_all(spread, 'dp', split_axis=0, concat_axis=0, tiled=True)]
  transfers between devices with their start and end apart: 28 -> 27, of which waited for: 8 -> 8; matrix products, arithmetic and copies ran while one was open for 0% -> 1% of each run, Pallas kernels for 46% -> 43%
where the time goes in v5:
time: 345 us; the launch traced here: 344 us
  Pallas kernels  146 us (42%)
  waiting for transfers between devices  99.1 us (29%)
  starting transfers between devices  74.6 us (22%)
  between operations  14.4 us (4%)
  other arithmetic  4.85 us (1%)
  local copies, waits for them, and re-layouts  4.67 us (1%)
    pallas_call x3, Pallas kernels, block_products(): pl.pallas_call(block_kernel, grid=(filters,), in_specs=[pl.BlockSpec(memo...  96.2 us
    ppermute x3, waiting for transfers between devices, block_shards(): arrivals = [lax.ppermute(own_parts[0], 'ctx', route) for route in routes]  64.8 us
    pallas_call x2, Pallas kernels, leave(): pl.pallas_call(lambda *refs: leave_kernel(bool(received_parts), bool(made...  32.2 us
    ppermute x6, starting transfers between devices, block_shards(): arrivals = [lax.ppermute(leaving, 'ctx', route) for route in routes]  22.2 us
    ppermute x6, waiting for transfers between devices, block_shards(): arrivals = [lax.ppermute(leaving, 'ctx', route) for route in routes]  20.7 us
    pallas_call x2, Pallas kernels, enter(): pl.pallas_call(enter_kernel, grid_spec=pltpu.PrefetchScalarGridSpec(num_s...  17.8 us
    ppermute x6, starting transfers between devices, lag_block(): total += lax.ppermute(leaving, 'ctx', rotation(hop)).astype(jnp.float32)  12 us
    all_to_all x3, starting transfers between devices, lag_shares(): lax.all_to_all(pieces, 'dp', split_axis=0, concat_axis=0, tiled=True)  11.4 us
  transfers between devices with their start and end apart: 27, of which 8 were waited for; matrix products, arithmetic and copies ran while one was open for 1% of the time, Pallas kernels for 43%

profile of v5, /device:TPU:0, one launch (start us, length us, event | category | flops | bytes accessed | tf_op | source)
XLA Modules:
  0.0 343.9 jit_solution(18185127197245769439)
XLA Ops:
  7.2 0.7 dynamic-slice_negate_fusion
  8.0 1.4 fusion.3
  9.4 5.1 %collective-permute-start = (bf16[1,2,256,128]{3,2,1,0:T(8,128)(2,1)S(1)}, bf16[1,2,256,128]{3,2,1,0:T(8,128)(2,1)S(1)}, u32[]{:S(2)}, u32[]{:S(2)}) collective-permute-start(bf16[1,2,256,128]{3,2,1,0:T(8,128)(2,1)S(1)} %copy.38), channel_id=1, source_target_pairs={{0,3},{1,0},{2,1},{3,2},{4,7},{5,4},{6,5},{7,6},{8,11},{9,8},{10,9... | collective-permute-start | bytes 393224 | tf_op jit(solution)/shard_map/ppermute | solution.py:556
  14.5 1.0 collective-permute-start.2
  15.5 8.9 %shard_map.164 = (bf16[4,7,256,128]{3,2,1,0:T(8,128)(2,1)}, bf16[4,5,256,128]{3,2,1,0:T(8,128)(2,1)}, bf16[4,4,256,128]{3,2,1,0:T(8,128)(2,1)}) custom-call(s32[1]{0:T(128)} %bitcast.1.first_ref.refs_0_, bf16[64,32768]{1,0:T(8,128)(2,1)} %refs_2_.3, bf16[64,32768]{1,0:T(8,128)(2,1)} %refs_3_.3, bf16[64,32768]{1,0:T(8,128)(2,1)} %refs_4_.3, ...), custom_call_target="tpu_custom_call" | custom-call | flops 4194304 | bytes 12582912 | tf_op jit(solution)/shard_map/pallas_call | solution.py:428
  24.5 1.3 collective-permute-done.1
  25.9 0.8 constant_dynamic-slice_fusion
  26.8 2.1 collective-permute-start.3
  28.9 6.4 %collective-permute-start.4 = (bf16[4,7,256,128]{3,2,1,0:T(8,128)(2,1)S(1)}, bf16[4,7,256,128]{3,2,1,0:T(8,128)(2,1)}, u32[]{:S(2)}, u32[]{:S(2)}) collective-permute-start(bf16[4,7,256,128]{3,2,1,0:T(8,128)(2,1)S(1)} %copy-done), channel_id=1, source_target_pairs={{0,2},{3,1},{4,6},{7,5},{8,10},{11,9},{12,14},{15,13},{16,18},{19,... | collective-permute-start | bytes 5505032 | tf_op jit(solution)/shard_map/ppermute | solution.py:560
  35.3 2.5 collective-permute-start.5
  37.8 8.9 %shard_map.165.other_own_ref = bf16[4,16,256,128]{3,2,1,0:T(8,128)(2,1)} custom-call(s32[1]{0:T(128)S(6)} %sub.7.first_ref.refs_0_, bf16[64,32768]{1,0:T(8,128)(2,1)} %refs_2_.3, bf16[64,32768]{1,0:T(8,128)(2,1)} %refs_3_.3, bf16[64,32768]{1,0:T(8,128)(2,1)} %refs_4_.3, bf16[64,32768]{1,0:T(8,128)(2,1)} %refs_5_.3), custom_call_target="tpu_custom_call" | custom-call | flops 4194304 | bytes 12582912 | tf_op jit(solution)/shard_map/pallas_call | solution.py:428
  46.7 27.7 %collective-permute-done.4.other_far_ref = bf16[4,7,256,128]{3,2,1,0:T(8,128)(2,1)} collective-permute-done((bf16[4,7,256,128]{3,2,1,0:T(8,128)(2,1)S(1)}, bf16[4,7,256,128]{3,2,1,0:T(8,128)(2,1)}, u32[]{:S(2)}, u32[]{:S(2)}) %collective-permute-start.4) | collective-permute-done | bytes 1835040 | tf_op jit(solution)/shard_map/ppermute | solution.py:560
  74.5 37.1 %collective-permute-done.5.far_ref = bf16[4,7,256,128]{3,2,1,0:T(8,128)(2,1)} collective-permute-done((bf16[4,7,256,128]{3,2,1,0:T(8,128)(2,1)S(1)}, bf16[4,7,256,128]{3,2,1,0:T(8,128)(2,1)}, u32[]{:S(2)}, u32[]{:S(2)}) %collective-permute-start.5) | collective-permute-done | bytes 1835040 | tf_op jit(solution)/shard_map/ppermute | solution.py:560
  111.5 0.7 collective-permute-start.6
  112.3 8.2 %collective-permute-start.7 = (bf16[4,5,256,128]{3,2,1,0:T(8,128)(2,1)S(1)}, bf16[4,5,256,128]{3,2,1,0:T(8,128)(2,1)}, u32[]{:S(2)}, u32[]{:S(2)}) collective-permute-start(bf16[4,5,256,128]{3,2,1,0:T(8,128)(2,1)S(1)} %copy-done.2), channel_id=1, source_target_pairs={{0,2},{3,1},{4,6},{7,5},{8,10},{11,9},{12,14},{15,13},{16,18},{19,... | collective-permute-start | bytes 3932168 | tf_op jit(solution)/shard_map/ppermute | solution.py:594
  120.4 2.4 collective-permute-start.8
  122.8 41.2 %shard_map.166 = (bf16[4,7,256,128]{3,2,1,0:T(8,128)(2,1)}, bf16[4,7,256,128]{3,2,1,0:T(8,128)(2,1)}, bf16[4,7,256,128]{3,2,1,0:T(8,128)(2,1)}, bf16[8,4,7,32,128]{4,3,2,1,0:T(8,128)(2,1)}) custom-call(f32[1]{0:T(128)} %bitcast.side_ref, bf16[4,7,256,128]{3,2,1,0:T(8,128)(2,1)} %get-tuple-element.90.own_ref, ...), custom_call_target="tpu_custom_call" | custom-call | flops 1 | bytes 1 | tf_op jit(solution)/shard_map/pallas_call | solution.py:379
  164.0 9.4 %collective-permute-done.8.far_ref = bf16[4,5,256,128]{3,2,1,0:T(8,128)(2,1)} collective-permute-done((bf16[4,5,256,128]{3,2,1,0:T(8,128)(2,1)S(1)}, bf16[4,5,256,128]{3,2,1,0:T(8,128)(2,1)}, u32[]{:S(2)}, u32[]{:S(2)}) %collective-permute-start.8) | collective-permute-done | bytes 1310752 | tf_op jit(solution)/shard_map/ppermute | solution.py:594
  173.4 1.3 collective-permute-start.12
  174.6 3.7 %all-to-all-start = ((bf16[8,4,7,32,128]{4,3,2,1,0:T(8,128)(2,1)}), bf16[8,4,7,32,128]{4,3,2,1,0:T(8,128)(2,1)S(1)}, u32[]{:S(2)}, u32[]{:S(2)}) async-start(bf16[8,4,7,32,128]{4,3,2,1,0:T(8,128)(2,1)} %get-tuple-element.108), calls=%async_computation | async-start | bytes 3670016 | tf_op jit(solution)/shard_map/all_to_all | solution.py:565
  178.4 7.0 %collective-permute-start.10 = (bf16[4,4,256,128]{3,2,1,0:T(8,128)(2,1)}, bf16[4,4,256,128]{3,2,1,0:T(8,128)(2,1)S(1)}, u32[]{:S(2)}, u32[]{:S(2)}) collective-permute-start(bf16[4,4,256,128]{3,2,1,0:T(8,128)(2,1)} %get-tuple-element.111.own_ref), channel_id=1, source_target_pairs={{0,2},{3,1},{4,6},{7,5},{8,10},{11,9},{12,14},{15,13},{16,18},{19,... | collective-permute-start | bytes 3145736 | tf_op jit(solution)/shard_map/ppermute | solution.py:594
  185.4 2.3 collective-permute-start.11
  187.7 1.6 collective-permute-start.9
  189.3 30.2 %shard_map.167 = (bf16[4,5,256,128]{3,2,1,0:T(8,128)(2,1)}, bf16[4,5,256,128]{3,2,1,0:T(8,128)(2,1)}, bf16[4,5,256,128]{3,2,1,0:T(8,128)(2,1)}, bf16[8,4,5,32,128]{4,3,2,1,0:T(8,128)(2,1)}) custom-call(f32[1]{0:T(128)} %bitcast.side_ref, bf16[4,5,256,128]{3,2,1,0:T(8,128)(2,1)} %get-tuple-element.100.own_ref, ...), custom_call_target="tpu_custom_call" | custom-call | flops 1 | bytes 1 | tf_op jit(solution)/shard_map/pallas_call | solution.py:379
  219.6 0.3 reduce_sum.36
  219.9 11.3 %collective-permute-done.11.far_ref = bf16[4,4,256,128]{3,2,1,0:T(8,128)(2,1)} collective-permute-done((bf16[4,4,256,128]{3,2,1,0:T(8,128)(2,1)}, bf16[4,4,256,128]{3,2,1,0:T(8,128)(2,1)}, u32[]{:S(2)}, u32[]{:S(2)}) %collective-permute-start.11) | collective-permute-done | bytes 1048608 | tf_op jit(solution)/shard_map/ppermute | solution.py:594
  231.2 1.3 collective-permute-start.13
  232.5 3.9 %all-to-all-start.1 = ((bf16[8,4,5,32,128]{4,3,2,1,0:T(8,128)(2,1)}), bf16[8,4,5,32,128]{4,3,2,1,0:T(8,128)(2,1)S(1)}, u32[]{:S(2)}, u32[]{:S(2)}) async-start(bf16[8,4,5,32,128]{4,3,2,1,0:T(8,128)(2,1)} %get-tuple-element.121), calls=%async_computation.1 | async-start | bytes 2621440 | tf_op jit(solution)/shard_map/all_to_all | solution.py:565
  236.4 24.8 %shard_map.168 = (bf16[4,4,256,128]{3,2,1,0:T(8,128)(2,1)}, bf16[4,4,256,128]{3,2,1,0:T(8,128)(2,1)}, bf16[4,4,256,128]{3,2,1,0:T(8,128)(2,1)}, bf16[8,4,4,32,128]{4,3,2,1,0:T(8,128)(2,1)}) custom-call(f32[1]{0:T(128)} %bitcast.side_ref, bf16[4,4,256,128]{3,2,1,0:T(8,128)(2,1)} %get-tuple-element.111.own_ref, ...), custom_call_target="tpu_custom_call" | custom-call | flops 1 | bytes 1 | tf_op jit(solution)/shard_map/pallas_call | solution.py:379
  261.4 2.5 collective-permute-done.13.refs_10_
  263.9 1.3 collective-permute-start.14
  265.2 3.8 %all-to-all-start.2 = ((bf16[8,4,4,32,128]{4,3,2,1,0:T(8,128)(2,1)}), bf16[8,4,4,32,128]{4,3,2,1,0:T(8,128)(2,1)S(1)}, u32[]{:S(2)}, u32[]{:S(2)}) async-start(bf16[8,4,4,32,128]{4,3,2,1,0:T(8,128)(2,1)} %get-tuple-element.128), calls=%async_computation.2 | async-start | bytes 2097152 | tf_op jit(solution)/shard_map/all_to_all | solution.py:565
  269.1 3.7 %collective-permute-start.15 = (bf16[12,32,128]{2,1,0:T(8,128)(2,1)S(1)}, bf16[12,32,128]{2,1,0:T(8,128)(2,1)S(1)}, u32[]{:S(2)}, u32[]{:S(2)}) collective-permute-start(bf16[12,32,128]{2,1,0:T(8,128)(2,1)S(1)} %get-tuple-element.159), channel_id=1, source_target_pairs={{0,1},{1,2},{2,3},{3,0},{4,5},{5,6},{6,7},{7,4},{8,9},{9,10},{10,1... | collective-permute-start | bytes 294920 | tf_op jit(solution)/shard_map/ppermute | solution.py:575
  272.7 1.2 collective-permute-start.16
  274.0 2.8 collective-permute-start.17
  276.8 0.7 copy.26.refs_1_
  277.5 15.1 %shard_map.169 = (bf16[64,32768]{1,0:T(8,128)(2,1)}, bf16[64,32768]{1,0:T(8,128)(2,1)}, bf16[64,32768]{1,0:T(8,128)(2,1)}, bf16[64,32768]{1,0:T(8,128)(2,1)}) custom-call(s32[1]{0:T(128)} %bitcast.1.first_ref.refs_0_, f32[64,1]{1,0:T(8,128)} %copy.26.refs_1_, bf16[64,32768]{1,0:T(8,128)(2,1)} %refs_2_.3, bf16[64,32768]{1,0:T(8,128)(2,1)} %refs_3_.3, ...), custom_call_target="tpu_custom_call" | custom-call | flops 16777216 | bytes 29360128 | tf_op jit(solution)/shard_map/pallas_call | solution.py:496
  292.6 3.7 %collective-permute-done.17 = bf16[12,32,128]{2,1,0:T(8,128)(2,1)S(1)} collective-permute-done((bf16[12,32,128]{2,1,0:T(8,128)(2,1)S(1)}, bf16[12,32,128]{2,1,0:T(8,128)(2,1)S(1)}, u32[]{:S(2)}, u32[]{:S(2)}) %collective-permute-start.17) | collective-permute-done | bytes 98336 | tf_op jit(solution)/shard_map/ppermute | solution.py:575
  296.6 1.0 broadcast_in_dim.7
  297.6 3.8 %all-to-all-start.3 = ((bf16[8,12,32,128]{3,2,1,0:T(8,128)(2,1)}), bf16[8,12,32,128]{3,2,1,0:T(8,128)(2,1)S(1)}, u32[]{:S(2)}, u32[]{:S(2)}) async-start(bf16[8,12,32,128]{3,2,1,0:T(8,128)(2,1)} %broadcast_in_dim.7), calls=%async_computation.3 | async-start | bytes 1572864 | tf_op jit(solution)/shard_map/all_to_all | solution.py:580
  301.5 3.7 %collective-permute-start.19 = (bf16[4,32,128]{2,1,0:T(8,128)(2,1)S(1)}, bf16[4,32,128]{2,1,0:T(8,128)(2,1)S(1)}, u32[]{:S(2)}, u32[]{:S(2)}) collective-permute-start(bf16[4,32,128]{2,1,0:T(8,128)(2,1)S(1)} %get-tuple-element.164), channel_id=1, source_target_pairs={{0,2},{1,3},{2,0},{3,1},{4,6},{5,7},{6,4},{7,5},{8,10},{9,11},{10,... | collective-permute-start | bytes 98312 | tf_op jit(solution)/shard_map/ppermute | solution.py:575
  305.2 0.4 collective-permute-start.20
  305.6 17.1 %shard_map.170 = (bf16[64,32768]{1,0:T(8,128)(2,1)}, bf16[64,32768]{1,0:T(8,128)(2,1)}, bf16[64,32768]{1,0:T(8,128)(2,1)}, bf16[64,32768]{1,0:T(8,128)(2,1)}) custom-call(s32[1]{0:T(128)S(6)} %sub.7.first_ref.refs_0_, f32[64,1]{1,0:T(8,128)} %copy.26.refs_1_, ...), custom_call_target="tpu_custom_call", output_to_operand_aliasing={{0}: (12, {}), {1}: (13, {}), {2}: (14, {}), {3}: (15, {})} | custom-call | flops 16777216 | bytes 29360128 | tf_op jit(solution)/shard_map/pallas_call | solution.py:496
  322.9 0.7 broadcast_in_dim.8
  323.7 4.2 %all-to-all-start.4 = ((bf16[8,4,32,128]{3,2,1,0:T(8,128)(2,1)}), bf16[8,4,32,128]{3,2,1,0:T(8,128)(2,1)S(1)}, u32[]{:S(2)}, u32[]{:S(2)}) async-start(bf16[8,4,32,128]{3,2,1,0:T(8,128)(2,1)} %broadcast_in_dim.8), calls=%async_computation.4 | async-start | bytes 524288 | tf_op jit(solution)/shard_map/all_to_all | solution.py:580
  328.0 0.7 copy.31
  328.7 6.1 %all-to-all-done.4 = bf16[8,4,32,128]{3,2,1,0:T(8,128)(2,1)S(1)} async-done(((bf16[8,4,32,128]{3,2,1,0:T(8,128)(2,1)}), bf16[8,4,32,128]{3,2,1,0:T(8,128)(2,1)S(1)}, u32[]{:S(2)}, u32[]{:S(2)}) %all-to-all-start.4) | async-done | bytes 262176 | tf_op jit(solution)/shard_map/all_to_all | solution.py:580
  335.1 2.0 multiply_multiply_fusion
  (59 shorter events, 1.3 us)
Async XLA Ops:
  7.2 115.6 %all-gather.2.cloned.1.call-start = ((), (), s32[]{:S(2)}) async-start(), calls=%async_computation.5 | async-start | bytes 4718592 | tf_op jit(solution)/shard_map/all_gather | solution.py:561
  9.4 15.0 %collective-permute-start = (bf16[1,2,256,128]{3,2,1,0:T(8,128)(2,1)S(1)}, bf16[1,2,256,128]{3,2,1,0:T(8,128)(2,1)S(1)}, u32[]{:S(2)}, u32[]{:S(2)}) collective-permute-start(bf16[1,2,256,128]{3,2,1,0:T(8,128)(2,1)S(1)} %copy.38), channel_id=1, source_target_pairs={{0,3},{1,0},{2,1},{3,2},{4,7},{5,4},{6,5},{7,6},{8,11},{9,8},{10,9... | collective-permute-start | bytes 393224 | tf_op jit(solution)/shard_map/ppermute | solution.py:556
  14.5 11.2 %collective-permute-start.1 = (bf16[1,2,256,128]{3,2,1,0:T(8,128)(2,1)S(1)}, bf16[1,2,256,128]{3,2,1,0:T(8,128)(2,1)S(1)}, u32[]{:S(2)}, u32[]{:S(2)}) collective-permute-start(bf16[1,2,256,128]{3,2,1,0:T(8,128)(2,1)S(1)} %copy.38), channel_id=1, source_target_pairs={{0,2},{1,3},{2,0},{3,1},{4,6},{5,7},{6,4},{7,5},{8,10},{9,11},{10,... | collective-permute-start | bytes 393224 | tf_op jit(solution)/shard_map/ppermute | solution.py:556
  14.5 11.2 %collective-permute-start.2 = (bf16[1,2,256,128]{3,2,1,0:T(8,128)(2,1)S(1)}, bf16[1,2,256,128]{3,2,1,0:T(8,128)(2,1)S(1)}, u32[]{:S(2)}, u32[]{:S(2)}) collective-permute-start(bf16[1,2,256,128]{3,2,1,0:T(8,128)(2,1)S(1)} %copy.38), channel_id=1, source_target_pairs={{0,1},{1,2},{2,3},{3,0},{4,5},{5,6},{6,7},{7,4},{8,9},{9,10},{10,1... | collective-permute-start | bytes 393224 | tf_op jit(solution)/shard_map/ppermute | solution.py:556
  24.4 2.3 copy-start
  26.8 84.7 %copy-start.2 = (bf16[4,5,256,128]{3,2,1,0:T(8,128)(2,1)S(1)}, bf16[4,5,256,128]{3,2,1,0:T(8,128)(2,1)}, u32[]{:S(2)}) copy-start(bf16[4,5,256,128]{3,2,1,0:T(8,128)(2,1)} %get-tuple-element.100.own_ref) | copy-start | bytes 3932164
  26.8 19.9 %collective-permute-start.3 = (bf16[4,7,256,128]{3,2,1,0:T(8,128)(2,1)S(1)}, bf16[4,7,256,128]{3,2,1,0:T(8,128)(2,1)}, u32[]{:S(2)}, u32[]{:S(2)}) collective-permute-start(bf16[4,7,256,128]{3,2,1,0:T(8,128)(2,1)S(1)} %copy-done), channel_id=1, source_target_pairs={{1,2},{2,1},{5,6},{6,5},{9,10},{10,9},{13,14},{14,13},{17,18},{18,... | collective-permute-start | bytes 5505032 | tf_op jit(solution)/shard_map/ppermute | solution.py:560
  28.9 45.6 %collective-permute-start.4 = (bf16[4,7,256,128]{3,2,1,0:T(8,128)(2,1)S(1)}, bf16[4,7,256,128]{3,2,1,0:T(8,128)(2,1)}, u32[]{:S(2)}, u32[]{:S(2)}) collective-permute-start(bf16[4,7,256,128]{3,2,1,0:T(8,128)(2,1)S(1)} %copy-done), channel_id=1, source_target_pairs={{0,2},{3,1},{4,6},{7,5},{8,10},{11,9},{12,14},{15,13},{16,18},{19,... | collective-permute-start | bytes 5505032 | tf_op jit(solution)/shard_map/ppermute | solution.py:560
  35.3 76.2 %collective-permute-start.5 = (bf16[4,7,256,128]{3,2,1,0:T(8,128)(2,1)S(1)}, bf16[4,7,256,128]{3,2,1,0:T(8,128)(2,1)}, u32[]{:S(2)}, u32[]{:S(2)}) collective-permute-start(bf16[4,7,256,128]{3,2,1,0:T(8,128)(2,1)S(1)} %copy-done), channel_id=1, source_target_pairs={{0,1},{3,2},{4,5},{7,6},{8,9},{11,10},{12,13},{15,14},{16,17},{19,... | collective-permute-start | bytes 5505032 | tf_op jit(solution)/shard_map/ppermute | solution.py:560
  111.5 52.4 %collective-permute-start.6 = (bf16[4,5,256,128]{3,2,1,0:T(8,128)(2,1)S(1)}, bf16[4,5,256,128]{3,2,1,0:T(8,128)(2,1)S(1)}, u32[]{:S(2)}, u32[]{:S(2)}) collective-permute-start(bf16[4,5,256,128]{3,2,1,0:T(8,128)(2,1)S(1)} %copy-done.2), channel_id=1, source_target_pairs={{1,2},{2,1},{5,6},{6,5},{9,10},{10,9},{13,14},{14,13},{17,18},{18,... | collective-permute-start | bytes 3932168 | tf_op jit(solution)/shard_map/ppermute | solution.py:594
  112.3 51.7 %collective-permute-start.7 = (bf16[4,5,256,128]{3,2,1,0:T(8,128)(2,1)S(1)}, bf16[4,5,256,128]{3,2,1,0:T(8,128)(2,1)}, u32[]{:S(2)}, u32[]{:S(2)}) collective-permute-start(bf16[4,5,256,128]{3,2,1,0:T(8,128)(2,1)S(1)} %copy-done.2), channel_id=1, source_target_pairs={{0,2},{3,1},{4,6},{7,5},{8,10},{11,9},{12,14},{15,13},{16,18},{19,... | collective-permute-start | bytes 3932168 | tf_op jit(solution)/shard_map/ppermute | solution.py:594
  120.4 52.9 %collective-permute-start.8 = (bf16[4,5,256,128]{3,2,1,0:T(8,128)(2,1)S(1)}, bf16[4,5,256,128]{3,2,1,0:T(8,128)(2,1)}, u32[]{:S(2)}, u32[]{:S(2)}) collective-permute-start(bf16[4,5,256,128]{3,2,1,0:T(8,128)(2,1)S(1)} %copy-done.2), channel_id=1, source_target_pairs={{0,1},{3,2},{4,5},{7,6},{8,9},{11,10},{12,13},{15,14},{16,17},{19,... | collective-permute-start | bytes 3932168 | tf_op jit(solution)/shard_map/ppermute | solution.py:594
  164.0 10.7 %copy-start.3 = (bf16[4,5,256,128]{3,2,1,0:T(8,128)(2,1)}, bf16[4,5,256,128]{3,2,1,0:T(8,128)(2,1)S(1)}, u32[]{:S(2)}) copy-start(bf16[4,5,256,128]{3,2,1,0:T(8,128)(2,1)S(1)} %collective-permute-done.6.other_next_ref) | copy-start | bytes 3932164
  173.4 57.9 %collective-permute-start.12 = (bf16[4,7,256,128]{3,2,1,0:T(8,128)(2,1)}, bf16[4,7,256,128]{3,2,1,0:T(8,128)(2,1)}, u32[]{:S(2)}, u32[]{:S(2)}) collective-permute-start(bf16[4,7,256,128]{3,2,1,0:T(8,128)(2,1)} %get-tuple-element.107), channel_id=1, source_target_pairs={{1,0},{2,3},{5,4},{6,7},{9,8},{10,11},{13,12},{14,15},{17,16},{18,... | collective-permute-start | bytes 5505032 | tf_op jit(solution)/shard_map/ppermute | solution.py:596
  174.6 44.9 %all-to-all-start = ((bf16[8,4,7,32,128]{4,3,2,1,0:T(8,128)(2,1)}), bf16[8,4,7,32,128]{4,3,2,1,0:T(8,128)(2,1)S(1)}, u32[]{:S(2)}, u32[]{:S(2)}) async-start(bf16[8,4,7,32,128]{4,3,2,1,0:T(8,128)(2,1)} %get-tuple-element.108), calls=%async_computation | async-start | bytes 3670016 | tf_op jit(solution)/shard_map/all_to_all | solution.py:565
  178.4 41.5 %collective-permute-start.10 = (bf16[4,4,256,128]{3,2,1,0:T(8,128)(2,1)}, bf16[4,4,256,128]{3,2,1,0:T(8,128)(2,1)S(1)}, u32[]{:S(2)}, u32[]{:S(2)}) collective-permute-start(bf16[4,4,256,128]{3,2,1,0:T(8,128)(2,1)} %get-tuple-element.111.own_ref), channel_id=1, source_target_pairs={{0,2},{3,1},{4,6},{7,5},{8,10},{11,9},{12,14},{15,13},{16,18},{19,... | collective-permute-start | bytes 3145736 | tf_op jit(solution)/shard_map/ppermute | solution.py:594
  185.4 45.8 %collective-permute-start.11 = (bf16[4,4,256,128]{3,2,1,0:T(8,128)(2,1)}, bf16[4,4,256,128]{3,2,1,0:T(8,128)(2,1)}, u32[]{:S(2)}, u32[]{:S(2)}) collective-permute-start(bf16[4,4,256,128]{3,2,1,0:T(8,128)(2,1)} %get-tuple-element.111.own_ref), channel_id=1, source_target_pairs={{0,1},{3,2},{4,5},{7,6},{8,9},{11,10},{12,13},{15,14},{16,17},{19,... | collective-permute-start | bytes 3145736 | tf_op jit(solution)/shard_map/ppermute | solution.py:594
  187.7 43.5 %collective-permute-start.9 = (bf16[4,4,256,128]{3,2,1,0:T(8,128)(2,1)}, bf16[4,4,256,128]{3,2,1,0:T(8,128)(2,1)}, u32[]{:S(2)}, u32[]{:S(2)}) collective-permute-start(bf16[4,4,256,128]{3,2,1,0:T(8,128)(2,1)} %get-tuple-element.111.own_ref), channel_id=1, source_target_pairs={{1,2},{2,1},{5,6},{6,5},{9,10},{10,9},{13,14},{14,13},{17,18},{18,... | collective-permute-start | bytes 3145736 | tf_op jit(solution)/shard_map/ppermute | solution.py:594
  219.9 12.6 %copy-start.4 = (bf16[4,4,256,128]{3,2,1,0:T(8,128)(2,1)}, bf16[4,4,256,128]{3,2,1,0:T(8,128)(2,1)S(1)}, u32[]{:S(2)}) copy-start(bf16[4,4,256,128]{3,2,1,0:T(8,128)(2,1)S(1)} %collective-permute-done.10.other_far_ref) | copy-start | bytes 3145732
  231.2 32.6 %collective-permute-start.13 = (bf16[4,5,256,128]{3,2,1,0:T(8,128)(2,1)}, bf16[4,5,256,128]{3,2,1,0:T(8,128)(2,1)S(1)}, u32[]{:S(2)}, u32[]{:S(2)}) collective-permute-start(bf16[4,5,256,128]{3,2,1,0:T(8,128)(2,1)} %get-tuple-element.119), channel_id=1, source_target_pairs={{1,0},{2,3},{5,4},{6,7},{9,8},{10,11},{13,12},{14,15},{17,16},{18,... | collective-permute-start | bytes 3932168 | tf_op jit(solution)/shard_map/ppermute | solution.py:596
  232.5 28.6 %all-to-all-start.1 = ((bf16[8,4,5,32,128]{4,3,2,1,0:T(8,128)(2,1)}), bf16[8,4,5,32,128]{4,3,2,1,0:T(8,128)(2,1)S(1)}, u32[]{:S(2)}, u32[]{:S(2)}) async-start(bf16[8,4,5,32,128]{4,3,2,1,0:T(8,128)(2,1)} %get-tuple-element.121), calls=%async_computation.1 | async-start | bytes 2621440 | tf_op jit(solution)/shard_map/all_to_all | solution.py:565
  261.3 15.5 %copy-start.5 = (f32[64]{0:T(128)S(1)}, f32[64]{0:T(128)}, u32[]{:S(2)}) copy-start(f32[64]{0:T(128)} %param.19) | copy-start | bytes 772
  263.9 28.8 %copy-start.1 = (bf16[4,5,256,128]{3,2,1,0:T(8,128)(2,1)}, bf16[4,5,256,128]{3,2,1,0:T(8,128)(2,1)S(1)}, u32[]{:S(2)}) copy-start(bf16[4,5,256,128]{3,2,1,0:T(8,128)(2,1)S(1)} %collective-permute-done.13.refs_10_) | copy-start | bytes 3932164
  263.9 32.7 %collective-permute-start.14 = (bf16[4,4,256,128]{3,2,1,0:T(8,128)(2,1)}, bf16[4,4,256,128]{3,2,1,0:T(8,128)(2,1)}, u32[]{:S(2)}, u32[]{:S(2)}) collective-permute-start(bf16[4,4,256,128]{3,2,1,0:T(8,128)(2,1)} %get-tuple-element.125), channel_id=1, source_target_pairs={{1,0},{2,3},{5,4},{6,7},{9,8},{10,11},{13,12},{14,15},{17,16},{18,... | collective-permute-start | bytes 3145736 | tf_op jit(solution)/shard_map/ppermute | solution.py:607
  265.2 31.3 %all-to-all-start.2 = ((bf16[8,4,4,32,128]{4,3,2,1,0:T(8,128)(2,1)}), bf16[8,4,4,32,128]{4,3,2,1,0:T(8,128)(2,1)S(1)}, u32[]{:S(2)}, u32[]{:S(2)}) async-start(bf16[8,4,4,32,128]{4,3,2,1,0:T(8,128)(2,1)} %get-tuple-element.128), calls=%async_computation.2 | async-start | bytes 2097152 | tf_op jit(solution)/shard_map/all_to_all | solution.py:565
  269.1 23.6 %collective-permute-start.15 = (bf16[12,32,128]{2,1,0:T(8,128)(2,1)S(1)}, bf16[12,32,128]{2,1,0:T(8,128)(2,1)S(1)}, u32[]{:S(2)}, u32[]{:S(2)}) collective-permute-start(bf16[12,32,128]{2,1,0:T(8,128)(2,1)S(1)} %get-tuple-element.159), channel_id=1, source_target_pairs={{0,1},{1,2},{2,3},{3,0},{4,5},{5,6},{6,7},{7,4},{8,9},{9,10},{10,1... | collective-permute-start | bytes 294920 | tf_op jit(solution)/shard_map/ppermute | solution.py:575
  272.7 19.9 %collective-permute-start.16 = (bf16[12,32,128]{2,1,0:T(8,128)(2,1)S(1)}, bf16[12,32,128]{2,1,0:T(8,128)(2,1)S(1)}, u32[]{:S(2)}, u32[]{:S(2)}) collective-permute-start(bf16[12,32,128]{2,1,0:T(8,128)(2,1)S(1)} %get-tuple-element.161), channel_id=1, source_target_pairs={{0,2},{1,3},{2,0},{3,1},{4,6},{5,7},{6,4},{7,5},{8,10},{9,11},{10,... | collective-permute-start | bytes 294920 | tf_op jit(solution)/shard_map/ppermute | solution.py:575
  274.0 22.4 %collective-permute-start.17 = (bf16[12,32,128]{2,1,0:T(8,128)(2,1)S(1)}, bf16[12,32,128]{2,1,0:T(8,128)(2,1)S(1)}, u32[]{:S(2)}, u32[]{:S(2)}) collective-permute-start(bf16[12,32,128]{2,1,0:T(8,128)(2,1)S(1)} %get-tuple-element.160), channel_id=1, source_target_pairs={{0,3},{1,0},{2,1},{3,2},{4,7},{5,4},{6,5},{7,6},{8,11},{9,8},{10,9... | collective-permute-start | bytes 294920 | tf_op jit(solution)/shard_map/ppermute | solution.py:575
  297.6 25.2 %all-to-all-start.3 = ((bf16[8,12,32,128]{3,2,1,0:T(8,128)(2,1)}), bf16[8,12,32,128]{3,2,1,0:T(8,128)(2,1)S(1)}, u32[]{:S(2)}, u32[]{:S(2)}) async-start(bf16[8,12,32,128]{3,2,1,0:T(8,128)(2,1)} %broadcast_in_dim.7), calls=%async_computation.3 | async-start | bytes 1572864 | tf_op jit(solution)/shard_map/all_to_all | solution.py:580
  301.4 21.4 %collective-permute-start.18 = (bf16[4,32,128]{2,1,0:T(8,128)(2,1)S(1)}, bf16[4,32,128]{2,1,0:T(8,128)(2,1)S(1)}, u32[]{:S(2)}, u32[]{:S(2)}) collective-permute-start(bf16[4,32,128]{2,1,0:T(8,128)(2,1)S(1)} %get-tuple-element.162), channel_id=1, source_target_pairs={{0,1},{1,2},{2,3},{3,0},{4,5},{5,6},{6,7},{7,4},{8,9},{9,10},{10,1... | collective-permute-start | bytes 98312 | tf_op jit(solution)/shard_map/ppermute | solution.py:575
  301.5 21.3 %collective-permute-start.19 = (bf16[4,32,128]{2,1,0:T(8,128)(2,1)S(1)}, bf16[4,32,128]{2,1,0:T(8,128)(2,1)S(1)}, u32[]{:S(2)}, u32[]{:S(2)}) collective-permute-start(bf16[4,32,128]{2,1,0:T(8,128)(2,1)S(1)} %get-tuple-element.164), channel_id=1, source_target_pairs={{0,2},{1,3},{2,0},{3,1},{4,6},{5,7},{6,4},{7,5},{8,10},{9,11},{10,... | collective-permute-start | bytes 98312 | tf_op jit(solution)/shard_map/ppermute | solution.py:575
  305.2 17.6 %collective-permute-start.20 = (bf16[4,32,128]{2,1,0:T(8,128)(2,1)S(1)}, bf16[4,32,128]{2,1,0:T(8,128)(2,1)S(1)}, u32[]{:S(2)}, u32[]{:S(2)}) collective-permute-start(bf16[4,32,128]{2,1,0:T(8,128)(2,1)S(1)} %get-tuple-element.163), channel_id=1, source_target_pairs={{0,3},{1,0},{2,1},{3,2},{4,7},{5,4},{6,5},{7,6},{8,11},{9,8},{10,9... | collective-permute-start | bytes 98312 | tf_op jit(solution)/shard_map/ppermute | solution.py:575
  322.8 5.1 %copy-start.6 = (f32[16]{0:T(128)S(1)}, f32[16]{0:T(128)}, u32[]{:S(2)}) copy-start(f32[16]{0:T(128)} %param.18) | copy-start | bytes 196
  323.7 11.1 %all-to-all-start.4 = ((bf16[8,4,32,128]{3,2,1,0:T(8,128)(2,1)}), bf16[8,4,32,128]{3,2,1,0:T(8,128)(2,1)S(1)}, u32[]{:S(2)}, u32[]{:S(2)}) async-start(bf16[8,4,32,128]{3,2,1,0:T(8,128)(2,1)} %broadcast_in_dim.8), calls=%async_computation.4 | async-start | bytes 524288 | tf_op jit(solution)/shard_map/all_to_all | solution.py:580
Sparse Core Ops, SparseCore 0:
  26.9 36.9 all-gather.1

commit v6 on v5

--- a/solution.py
+++ b/solution.py
@@ -484,24 +484,28 @@
         finish(cotangent_ref, out_gate_ref, (values_ref, gate_ref), out_refs[2:], (0, 1))
 
 
-def leave(first, skip_gain, flat, signal_parts, received_parts=(), made=()):
+def leave(first, skip_gain, flat, signal_parts, received_parts=(), made=(), span=(0, 1)):
     channels, local_len = flat[0].shape
     parts = (*signal_parts, *received_parts)
     block = (channels, EDGE_ROWS * LANES)
-    flat_block = pl.BlockSpec(block, lambda i, first: (0, i))
+    steps = local_len // (EDGE_ROWS * LANES * span[1])
+    offset = span[0] * steps
+    flat_block = pl.BlockSpec(block, lambda i, first: (0, i + offset))
     still_block = pl.BlockSpec(block, lambda i, first: (0, 0))
-    of_first = pl.BlockSpec(block, lambda i, first: (0, i * first[0]))
-    of_second = pl.BlockSpec(block, lambda i, first: (0, i * (1 - first[0])))
+    of_first = pl.BlockSpec(block, lambda i, first: (0, (i + offset) * first[0]))
+    of_second = pl.BlockSpec(block, lambda i, first: (0, (i + offset) * (1 - first[0])))
     before = 6 + len(parts)
     return pl.pallas_call(
         lambda *refs: leave_kernel(bool(received_parts), bool(made), *refs),
         grid_spec=pltpu.PrefetchScalarGridSpec(
             num_scalar_prefetch=1,
-            grid=(local_len // (EDGE_ROWS * LANES),),
+            grid=(steps,),
             in_specs=[pl.BlockSpec((channels, 1), lambda i, first: (0, 0))]
             + [flat_block] * 4
             + [
-                pl.BlockSpec((*part.shape[:2], EDGE_ROWS, LANES), lambda i, first: (0, 0, i, 0))
+                pl.BlockSpec(
+                    (*part.shape[:2], EDGE_ROWS, LANES), lambda i, first: (0, 0, i + offset, 0)
+                )
                 for part in parts
             ]
             + [still_block] * len(made),
@@ -511,8 +515,8 @@
         input_output_aliases={before + number: number for number in range(len(made))},
         compiler_params=pltpu.CompilerParams(vmem_limit_bytes=VMEM_BYTES),
         cost_estimate=pl.CostEstimate(
-            flops=8 * channels * local_len,
-            bytes_accessed=14 * channels * local_len,
+            flops=8 * channels * local_len // span[1],
+            bytes_accessed=14 * channels * local_len // span[1],
             transcendentals=0,
         ),
     )(first, skip_gain[:, None], *flat, *parts, *made)
@@ -606,15 +610,15 @@
     )
     received = lax.ppermute(pending[0], "ctx", back_route)
     made = leave(near_start, skip_gain, flat, near_parts)
-    early = lag_block(jnp.concatenate(lag_parts, axis=1))
-    received, early, late, made, rest = lax.optimization_barrier(
-        (received, early, lag_shares(pending[1]), made, rest)
+    received, late, made, rest = lax.optimization_barrier(
+        (received, lag_shares(pending[1]), made, rest)
     )
     received_parts.append(received)
-    final = leave(rest, skip_gain, flat, other_parts, received_parts, made)
-    early, late, final = lax.optimization_barrier((lag_rows(early), lag_block(late), final))
-    outputs, grad_output_gate, grad_input_gate, grad_values = final
-    lag = jnp.concatenate([early, lag_rows(late)], axis=0).reshape(filters, local_len)
+    sides = (rest, skip_gain, flat, other_parts, received_parts)
+    lag = lag_block(jnp.concatenate([*lag_parts, late], axis=1))
+    lag, made, sides = lax.optimization_barrier((lag, leave(*sides, made, (0, 2)), sides))
+    lag = lag_rows(lag).reshape(filters, local_len)
+    outputs, grad_output_gate, grad_input_gate, grad_values = leave(*sides, made, (1, 2))
     grad_filter = lag.astype(jnp.float32) * envelope(filter_decay) * filter_scale
     return (outputs, grad_input_gate, grad_output_gate, grad_values, grad_filter)
 
@@ -626,7 +630,7 @@
         by_blocks = (
             ctx == 4
             and local_len % (LANES * STRIP * dp) == 0
-            and local_len % (LANES * EDGE_ROWS) == 0
+            and local_len % (LANES * EDGE_ROWS * 2) == 0
             and channels % (2 * filters) == 0
             and filters % dp == 0
             and filters == sum(SHARES)

time: 345 us -> 340 us (0.986)
  starting transfers between devices: 74.6 us -> 63 us
    ppermute x6 -> x3, starting transfers between devices: 12 us -> 3.32 us  [lag_block(): total += lax.ppermute(leaving, 'ctx', rotation(hop)).astype(jnp.float32)]
    all_to_all x2 -> x1, starting transfers between devices: 7.97 us -> 3.85 us  [lag_rows(): lax.all_to_all(spread, 'dp', split_axis=0, concat_axis=0, tiled=True)]
    ppermute x1, waiting for transfers between devices: 0.01 us -> 4.12 us  [block_shards(): received = lax.ppermute(pending[0], 'ctx', back_route)]
    ppermute x6 -> x3, waiting for transfers between devices: 3.72 us -> 0.01 us  [lag_block(): total += lax.ppermute(leaving, 'ctx', rotation(hop)).astype(jnp.float32)]
    pallas_call x2 -> x3, Pallas kernels: 32.2 us -> 35.2 us  [leave(): pl.pallas_call(lambda *refs: leave_kernel(bool(received_parts), bool(made...]
  transfers between devices with their start and end apart: 27 -> 23, of which waited for: 8 -> 8; matrix products, arithmetic and copies ran while one was open for 1% -> 1% of each run, Pallas kernels for 43% -> 44%
where the time goes in v6:
time: 340 us; the launch traced here: 339 us
  Pallas kernels  149 us (44%)
  waiting for transfers between devices  97 us (29%)
  starting transfers between devices  63 us (19%)
  between operations  14.4 us (4%)
  other arithmetic  8.17 us (2%)
  local copies, waits for them, and re-layouts  7.18 us (2%)
    pallas_call x3, Pallas kernels, block_products(): pl.pallas_call(block_kernel, grid=(filters,), in_specs=[pl.BlockSpec(memo...  96.1 us
    ppermute x3, waiting for transfers between devices, block_shards(): arrivals = [lax.ppermute(own_parts[0], 'ctx', route) for route in routes]  64.9 us
    pallas_call x3, Pallas kernels, leave(): pl.pallas_call(lambda *refs: leave_kernel(bool(received_parts), bool(made...  35.2 us
    ppermute x6, starting transfers between devices, block_shards(): arrivals = [lax.ppermute(leaving, 'ctx', route) for route in routes]  23.7 us
    ppermute x6, waiting for transfers between devices, block_shards(): arrivals = [lax.ppermute(leaving, 'ctx', route) for route in routes]  20.5 us
    pallas_call x2, Pallas kernels, enter(): pl.pallas_call(enter_kernel, grid_spec=pltpu.PrefetchScalarGridSpec(num_s...  17.8 us
    all_to_all x3, starting transfers between devices, lag_shares(): lax.all_to_all(pieces, 'dp', split_axis=0, concat_axis=0, tiled=True)  11.2 us
    ppermute x3, starting transfers between devices, block_shards(): arrivals = [lax.ppermute(own_parts[0], 'ctx', route) for route in routes]  11 us
  transfers between devices with their start and end apart: 23, of which 8 were waited for; matrix products, arithmetic and copies ran while one was open for 1% of the time, Pallas kernels for 44%

profile of v6, /device:TPU:0, one launch (start us, length us, event | category | flops | bytes accessed | tf_op | source)
XLA Modules:
  0.0 338.7 jit_solution(15838558334292499000)
XLA Ops:
  7.2 0.7 dynamic-slice_negate_fusion
  8.0 1.4 fusion.4
  9.4 5.1 %collective-permute-start = (bf16[1,2,256,128]{3,2,1,0:T(8,128)(2,1)S(1)}, bf16[1,2,256,128]{3,2,1,0:T(8,128)(2,1)S(1)}, u32[]{:S(2)}, u32[]{:S(2)}) collective-permute-start(bf16[1,2,256,128]{3,2,1,0:T(8,128)(2,1)S(1)} %copy.42), channel_id=1, source_target_pairs={{0,3},{1,0},{2,1},{3,2},{4,7},{5,4},{6,5},{7,6},{8,11},{9,8},{10,9... | collective-permute-start | bytes 393224 | tf_op jit(solution)/shard_map/ppermute | solution.py:560
  14.5 1.0 collective-permute-start.2
  15.5 8.9 %shard_map.164 = (bf16[4,7,256,128]{3,2,1,0:T(8,128)(2,1)}, bf16[4,5,256,128]{3,2,1,0:T(8,128)(2,1)}, bf16[4,4,256,128]{3,2,1,0:T(8,128)(2,1)}) custom-call(s32[1]{0:T(128)} %bitcast.1.first_ref.refs_0_, bf16[64,32768]{1,0:T(8,128)(2,1)} %refs_2_.4, bf16[64,32768]{1,0:T(8,128)(2,1)} %refs_3_.4, bf16[64,32768]{1,0:T(8,128)(2,1)} %refs_4_.4, ...), custom_call_target="tpu_custom_call" | custom-call | flops 4194304 | bytes 12582912 | tf_op jit(solution)/shard_map/pallas_call | solution.py:428
  24.5 1.3 collective-permute-done.1
  25.9 0.8 constant_dynamic-slice_fusion
  26.8 2.0 collective-permute-start.3
  28.8 6.4 %collective-permute-start.4 = (bf16[4,7,256,128]{3,2,1,0:T(8,128)(2,1)S(1)}, bf16[4,7,256,128]{3,2,1,0:T(8,128)(2,1)}, u32[]{:S(2)}, u32[]{:S(2)}) collective-permute-start(bf16[4,7,256,128]{3,2,1,0:T(8,128)(2,1)S(1)} %copy-done.2), channel_id=1, source_target_pairs={{0,2},{3,1},{4,6},{7,5},{8,10},{11,9},{12,14},{15,13},{16,18},{19,... | collective-permute-start | bytes 5505032 | tf_op jit(solution)/shard_map/ppermute | solution.py:564
  35.2 2.5 collective-permute-start.5
  37.8 8.9 %shard_map.165.other_own_ref = bf16[4,16,256,128]{3,2,1,0:T(8,128)(2,1)} custom-call(s32[1]{0:T(128)S(6)} %sub.7.first_ref.refs_0_, bf16[64,32768]{1,0:T(8,128)(2,1)} %refs_2_.4, bf16[64,32768]{1,0:T(8,128)(2,1)} %refs_3_.4, bf16[64,32768]{1,0:T(8,128)(2,1)} %refs_4_.4, bf16[64,32768]{1,0:T(8,128)(2,1)} %refs_5_.4), custom_call_target="tpu_custom_call" | custom-call | flops 4194304 | bytes 12582912 | tf_op jit(solution)/shard_map/pallas_call | solution.py:428
  46.7 27.8 %collective-permute-done.4.other_far_ref = bf16[4,7,256,128]{3,2,1,0:T(8,128)(2,1)} collective-permute-done((bf16[4,7,256,128]{3,2,1,0:T(8,128)(2,1)S(1)}, bf16[4,7,256,128]{3,2,1,0:T(8,128)(2,1)}, u32[]{:S(2)}, u32[]{:S(2)}) %collective-permute-start.4) | collective-permute-done | bytes 1835040 | tf_op jit(solution)/shard_map/ppermute | solution.py:564
  74.5 37.0 %collective-permute-done.5.far_ref = bf16[4,7,256,128]{3,2,1,0:T(8,128)(2,1)} collective-permute-done((bf16[4,7,256,128]{3,2,1,0:T(8,128)(2,1)S(1)}, bf16[4,7,256,128]{3,2,1,0:T(8,128)(2,1)}, u32[]{:S(2)}, u32[]{:S(2)}) %collective-permute-start.5) | collective-permute-done | bytes 1835040 | tf_op jit(solution)/shard_map/ppermute | solution.py:564
  111.5 0.7 collective-permute-start.6
  112.3 8.2 %collective-permute-start.7 = (bf16[4,5,256,128]{3,2,1,0:T(8,128)(2,1)S(1)}, bf16[4,5,256,128]{3,2,1,0:T(8,128)(2,1)}, u32[]{:S(2)}, u32[]{:S(2)}) collective-permute-start(bf16[4,5,256,128]{3,2,1,0:T(8,128)(2,1)S(1)} %copy-done.3), channel_id=1, source_target_pairs={{0,2},{3,1},{4,6},{7,5},{8,10},{11,9},{12,14},{15,13},{16,18},{19,... | collective-permute-start | bytes 3932168 | tf_op jit(solution)/shard_map/ppermute | solution.py:598
  120.5 2.4 collective-permute-start.8
  122.8 41.2 %shard_map.166 = (bf16[4,7,256,128]{3,2,1,0:T(8,128)(2,1)}, bf16[4,7,256,128]{3,2,1,0:T(8,128)(2,1)}, bf16[4,7,256,128]{3,2,1,0:T(8,128)(2,1)}, bf16[8,4,7,32,128]{4,3,2,1,0:T(8,128)(2,1)}) custom-call(f32[1]{0:T(128)} %bitcast.side_ref, bf16[4,7,256,128]{3,2,1,0:T(8,128)(2,1)} %get-tuple-element.104.own_ref, ...), custom_call_target="tpu_custom_call" | custom-call | flops 1 | bytes 1 | tf_op jit(solution)/shard_map/pallas_call | solution.py:379
  164.0 9.3 %collective-permute-done.8.far_ref = bf16[4,5,256,128]{3,2,1,0:T(8,128)(2,1)} collective-permute-done((bf16[4,5,256,128]{3,2,1,0:T(8,128)(2,1)S(1)}, bf16[4,5,256,128]{3,2,1,0:T(8,128)(2,1)}, u32[]{:S(2)}, u32[]{:S(2)}) %collective-permute-start.8) | collective-permute-done | bytes 1310752 | tf_op jit(solution)/shard_map/ppermute | solution.py:598
  173.3 1.3 collective-permute-start.12
  174.6 3.7 %all-to-all-start = ((bf16[8,4,7,32,128]{4,3,2,1,0:T(8,128)(2,1)}), bf16[8,4,7,32,128]{4,3,2,1,0:T(8,128)(2,1)S(1)}, u32[]{:S(2)}, u32[]{:S(2)}) async-start(bf16[8,4,7,32,128]{4,3,2,1,0:T(8,128)(2,1)} %get-tuple-element.122), calls=%async_computation | async-start | bytes 3670016 | tf_op jit(solution)/shard_map/all_to_all | solution.py:569
  178.4 0.7 collective-permute-start.9
  179.1 9.4 %collective-permute-start.10 = (bf16[4,4,256,128]{3,2,1,0:T(8,128)(2,1)}, bf16[4,4,256,128]{3,2,1,0:T(8,128)(2,1)}, u32[]{:S(2)}, u32[]{:S(2)}) collective-permute-start(bf16[4,4,256,128]{3,2,1,0:T(8,128)(2,1)} %get-tuple-element.125.own_ref), channel_id=1, source_target_pairs={{0,2},{3,1},{4,6},{7,5},{8,10},{11,9},{12,14},{15,13},{16,18},{19,... | collective-permute-start | bytes 3145736 | tf_op jit(solution)/shard_map/ppermute | solution.py:598
  188.5 2.3 collective-permute-start.11
  190.8 30.2 %shard_map.167 = (bf16[4,5,256,128]{3,2,1,0:T(8,128)(2,1)}, bf16[4,5,256,128]{3,2,1,0:T(8,128)(2,1)}, bf16[4,5,256,128]{3,2,1,0:T(8,128)(2,1)}, bf16[8,4,5,32,128]{4,3,2,1,0:T(8,128)(2,1)}) custom-call(f32[1]{0:T(128)} %bitcast.side_ref, bf16[4,5,256,128]{3,2,1,0:T(8,128)(2,1)} %get-tuple-element.114.own_ref, ...), custom_call_target="tpu_custom_call" | custom-call | flops 1 | bytes 1 | tf_op jit(solution)/shard_map/pallas_call | solution.py:379
  221.0 1.0 reduce_sum.36
  222.0 11.2 %collective-permute-done.11.far_ref = bf16[4,4,256,128]{3,2,1,0:T(8,128)(2,1)} collective-permute-done((bf16[4,4,256,128]{3,2,1,0:T(8,128)(2,1)}, bf16[4,4,256,128]{3,2,1,0:T(8,128)(2,1)}, u32[]{:S(2)}, u32[]{:S(2)}) %collective-permute-start.11) | collective-permute-done | bytes 1048608 | tf_op jit(solution)/shard_map/ppermute | solution.py:598
  233.1 1.3 collective-permute-start.13
  234.4 3.9 %all-to-all-start.1 = ((bf16[8,4,5,32,128]{4,3,2,1,0:T(8,128)(2,1)}), bf16[8,4,5,32,128]{4,3,2,1,0:T(8,128)(2,1)S(1)}, u32[]{:S(2)}, u32[]{:S(2)}) async-start(bf16[8,4,5,32,128]{4,3,2,1,0:T(8,128)(2,1)} %get-tuple-element.135), calls=%async_computation.1 | async-start | bytes 2621440 | tf_op jit(solution)/shard_map/all_to_all | solution.py:569
  238.3 24.7 %shard_map.168 = (bf16[4,4,256,128]{3,2,1,0:T(8,128)(2,1)}, bf16[4,4,256,128]{3,2,1,0:T(8,128)(2,1)}, bf16[4,4,256,128]{3,2,1,0:T(8,128)(2,1)}, bf16[8,4,4,32,128]{4,3,2,1,0:T(8,128)(2,1)}) custom-call(f32[1]{0:T(128)} %bitcast.side_ref, bf16[4,4,256,128]{3,2,1,0:T(8,128)(2,1)} %get-tuple-element.125.own_ref, ...), custom_call_target="tpu_custom_call" | custom-call | flops 1 | bytes 1 | tf_op jit(solution)/shard_map/pallas_call | solution.py:379
  263.0 0.9 reduce_sum.37
  263.9 1.5 collective-permute-done.13.refs_10_
  265.4 1.3 collective-permute-start.14
  266.7 3.6 %all-to-all-start.2 = ((bf16[8,4,4,32,128]{4,3,2,1,0:T(8,128)(2,1)}), bf16[8,4,4,32,128]{4,3,2,1,0:T(8,128)(2,1)S(1)}, u32[]{:S(2)}, u32[]{:S(2)}) async-start(bf16[8,4,4,32,128]{4,3,2,1,0:T(8,128)(2,1)} %get-tuple-element.142), calls=%async_computation.2 | async-start | bytes 2097152 | tf_op jit(solution)/shard_map/all_to_all | solution.py:569
  270.4 0.7 copy.32.refs_1_
  271.1 15.1 %shard_map.169 = (bf16[64,32768]{1,0:T(8,128)(2,1)}, bf16[64,32768]{1,0:T(8,128)(2,1)}, bf16[64,32768]{1,0:T(8,128)(2,1)}, bf16[64,32768]{1,0:T(8,128)(2,1)}) custom-call(s32[1]{0:T(128)} %bitcast.1.first_ref.refs_0_, f32[64,1]{1,0:T(8,128)} %copy.32.refs_1_, bf16[64,32768]{1,0:T(8,128)(2,1)} %refs_2_.4, bf16[64,32768]{1,0:T(8,128)(2,1)} %refs_3_.4, ...), custom_call_target="tpu_custom_call" | custom-call | flops 16777216 | bytes 29360128 | tf_op jit(solution)/shard_map/pallas_call | solution.py:498
  286.2 0.8 constant_dynamic-update-slice_fusion.9
  287.0 0.7 constant_dynamic-update-slice_fusion.8
  287.8 4.1 %collective-permute-done.14.refs_11_ = bf16[4,4,256,128]{3,2,1,0:T(8,128)(2,1)S(1)} collective-permute-done((bf16[4,4,256,128]{3,2,1,0:T(8,128)(2,1)}, bf16[4,4,256,128]{3,2,1,0:T(8,128)(2,1)S(1)}, u32[]{:S(2)}, u32[]{:S(2)}) %collective-permute-start.14) | collective-permute-done | bytes 1048608 | tf_op jit(solution)/shard_map/ppermute | solution.py:611
  292.0 0.7 constant_dynamic-update-slice_fusion.7
  292.7 1.1 dynamic-slice_bitcast_fusion.2
  293.7 2.7 collective-permute-start.17
  297.1 10.0 %shard_map.170 = (bf16[64,32768]{1,0:T(8,128)(2,1)}, bf16[64,32768]{1,0:T(8,128)(2,1)}, bf16[64,32768]{1,0:T(8,128)(2,1)}, bf16[64,32768]{1,0:T(8,128)(2,1)}) custom-call(s32[1]{0:T(128)S(6)} %sub.7.first_ref.refs_0_, f32[64,1]{1,0:T(8,128)} %copy.32.refs_1_, ...), custom_call_target="tpu_custom_call", output_to_operand_aliasing={{0}: (12, {}), {1}: (13, {}), {2}: (14, {}), {3}: (15, {})} | custom-call | flops 8388608 | bytes 14680064 | tf_op jit(solution)/shard_map/pallas_call | solution.py:498
  307.1 1.0 fusion.3
  308.1 1.2 broadcast_in_dim.8
  309.4 3.8 %all-to-all-start.3 = ((bf16[8,16,32,128]{3,2,1,0:T(8,128)(2,1)}), bf16[8,16,32,128]{3,2,1,0:T(8,128)(2,1)S(1)}, u32[]{:S(2)}, u32[]{:S(2)}) async-start(bf16[8,16,32,128]{3,2,1,0:T(8,128)(2,1)} %broadcast_in_dim.8), calls=%async_computation.3 | async-start | bytes 2097152 | tf_op jit(solution)/shard_map/all_to_all | solution.py:584
  313.9 10.0 %shard_map.171 = (bf16[64,32768]{1,0:T(8,128)(2,1)}, bf16[64,32768]{1,0:T(8,128)(2,1)}, bf16[64,32768]{1,0:T(8,128)(2,1)}, bf16[64,32768]{1,0:T(8,128)(2,1)}) custom-call(s32[1]{0:T(128)S(6)} %sub.7.first_ref.refs_0_, f32[64,1]{1,0:T(8,128)} %copy.34.refs_1_, ...), custom_call_target="tpu_custom_call", output_to_operand_aliasing={{0}: (12, {}), {1}: (13, {}), {2}: (14, {}), {3}: (15, {})} | custom-call | flops 8388608 | bytes 14680064 | tf_op jit(solution)/shard_map/pallas_call | solution.py:498
  324.0 4.7 %all-to-all-done.3 = bf16[8,16,32,128]{3,2,1,0:T(8,128)(2,1)S(1)} async-done(((bf16[8,16,32,128]{3,2,1,0:T(8,128)(2,1)}), bf16[8,16,32,128]{3,2,1,0:T(8,128)(2,1)S(1)}, u32[]{:S(2)}, u32[]{:S(2)}) %all-to-all-start.3) | async-done | bytes 1048608 | tf_op jit(solution)/shard_map/all_to_all | solution.py:584
  329.2 2.7 fusion
  (54 shorter events, 2.3 us)
Async XLA Ops:
  7.2 115.7 %all-gather.2.cloned.1.call-start = ((), (), s32[]{:S(2)}) async-start(), calls=%async_computation.4 | async-start | bytes 4718592 | tf_op jit(solution)/shard_map/all_gather | solution.py:565
  9.4 15.0 %collective-permute-start = (bf16[1,2,256,128]{3,2,1,0:T(8,128)(2,1)S(1)}, bf16[1,2,256,128]{3,2,1,0:T(8,128)(2,1)S(1)}, u32[]{:S(2)}, u32[]{:S(2)}) collective-permute-start(bf16[1,2,256,128]{3,2,1,0:T(8,128)(2,1)S(1)} %copy.42), channel_id=1, source_target_pairs={{0,3},{1,0},{2,1},{3,2},{4,7},{5,4},{6,5},{7,6},{8,11},{9,8},{10,9... | collective-permute-start | bytes 393224 | tf_op jit(solution)/shard_map/ppermute | solution.py:560
  14.5 11.2 %collective-permute-start.1 = (bf16[1,2,256,128]{3,2,1,0:T(8,128)(2,1)S(1)}, bf16[1,2,256,128]{3,2,1,0:T(8,128)(2,1)S(1)}, u32[]{:S(2)}, u32[]{:S(2)}) collective-permute-start(bf16[1,2,256,128]{3,2,1,0:T(8,128)(2,1)S(1)} %copy.42), channel_id=1, source_target_pairs={{0,2},{1,3},{2,0},{3,1},{4,6},{5,7},{6,4},{7,5},{8,10},{9,11},{10,... | collective-permute-start | bytes 393224 | tf_op jit(solution)/shard_map/ppermute | solution.py:560
  14.5 11.2 %collective-permute-start.2 = (bf16[1,2,256,128]{3,2,1,0:T(8,128)(2,1)S(1)}, bf16[1,2,256,128]{3,2,1,0:T(8,128)(2,1)S(1)}, u32[]{:S(2)}, u32[]{:S(2)}) collective-permute-start(bf16[1,2,256,128]{3,2,1,0:T(8,128)(2,1)S(1)} %copy.42), channel_id=1, source_target_pairs={{0,1},{1,2},{2,3},{3,0},{4,5},{5,6},{6,7},{7,4},{8,9},{9,10},{10,1... | collective-permute-start | bytes 393224 | tf_op jit(solution)/shard_map/ppermute | solution.py:560
  24.4 2.3 copy-start.2
  26.8 84.7 %copy-start.3 = (bf16[4,5,256,128]{3,2,1,0:T(8,128)(2,1)S(1)}, bf16[4,5,256,128]{3,2,1,0:T(8,128)(2,1)}, u32[]{:S(2)}) copy-start(bf16[4,5,256,128]{3,2,1,0:T(8,128)(2,1)} %get-tuple-element.114.own_ref) | copy-start | bytes 3932164
  26.8 19.9 %collective-permute-start.3 = (bf16[4,7,256,128]{3,2,1,0:T(8,128)(2,1)S(1)}, bf16[4,7,256,128]{3,2,1,0:T(8,128)(2,1)}, u32[]{:S(2)}, u32[]{:S(2)}) collective-permute-start(bf16[4,7,256,128]{3,2,1,0:T(8,128)(2,1)S(1)} %copy-done.2), channel_id=1, source_target_pairs={{1,2},{2,1},{5,6},{6,5},{9,10},{10,9},{13,14},{14,13},{17,18},{18,... | collective-permute-start | bytes 5505032 | tf_op jit(solution)/shard_map/ppermute | solution.py:564
  28.8 45.7 %collective-permute-start.4 = (bf16[4,7,256,128]{3,2,1,0:T(8,128)(2,1)S(1)}, bf16[4,7,256,128]{3,2,1,0:T(8,128)(2,1)}, u32[]{:S(2)}, u32[]{:S(2)}) collective-permute-start(bf16[4,7,256,128]{3,2,1,0:T(8,128)(2,1)S(1)} %copy-done.2), channel_id=1, source_target_pairs={{0,2},{3,1},{4,6},{7,5},{8,10},{11,9},{12,14},{15,13},{16,18},{19,... | collective-permute-start | bytes 5505032 | tf_op jit(solution)/shard_map/ppermute | solution.py:564
  35.2 76.3 %collective-permute-start.5 = (bf16[4,7,256,128]{3,2,1,0:T(8,128)(2,1)S(1)}, bf16[4,7,256,128]{3,2,1,0:T(8,128)(2,1)}, u32[]{:S(2)}, u32[]{:S(2)}) collective-permute-start(bf16[4,7,256,128]{3,2,1,0:T(8,128)(2,1)S(1)} %copy-done.2), channel_id=1, source_target_pairs={{0,1},{3,2},{4,5},{7,6},{8,9},{11,10},{12,13},{15,14},{16,17},{19,... | collective-permute-start | bytes 5505032 | tf_op jit(solution)/shard_map/ppermute | solution.py:564
  111.5 52.5 %collective-permute-start.6 = (bf16[4,5,256,128]{3,2,1,0:T(8,128)(2,1)S(1)}, bf16[4,5,256,128]{3,2,1,0:T(8,128)(2,1)S(1)}, u32[]{:S(2)}, u32[]{:S(2)}) collective-permute-start(bf16[4,5,256,128]{3,2,1,0:T(8,128)(2,1)S(1)} %copy-done.3), channel_id=1, source_target_pairs={{1,2},{2,1},{5,6},{6,5},{9,10},{10,9},{13,14},{14,13},{17,18},{18,... | collective-permute-start | bytes 3932168 | tf_op jit(solution)/shard_map/ppermute | solution.py:598
  112.3 51.8 %collective-permute-start.7 = (bf16[4,5,256,128]{3,2,1,0:T(8,128)(2,1)S(1)}, bf16[4,5,256,128]{3,2,1,0:T(8,128)(2,1)}, u32[]{:S(2)}, u32[]{:S(2)}) collective-permute-start(bf16[4,5,256,128]{3,2,1,0:T(8,128)(2,1)S(1)} %copy-done.3), channel_id=1, source_target_pairs={{0,2},{3,1},{4,6},{7,5},{8,10},{11,9},{12,14},{15,13},{16,18},{19,... | collective-permute-start | bytes 3932168 | tf_op jit(solution)/shard_map/ppermute | solution.py:598
  120.5 52.9 %collective-permute-start.8 = (bf16[4,5,256,128]{3,2,1,0:T(8,128)(2,1)S(1)}, bf16[4,5,256,128]{3,2,1,0:T(8,128)(2,1)}, u32[]{:S(2)}, u32[]{:S(2)}) collective-permute-start(bf16[4,5,256,128]{3,2,1,0:T(8,128)(2,1)S(1)} %copy-done.3), channel_id=1, source_target_pairs={{0,1},{3,2},{4,5},{7,6},{8,9},{11,10},{12,13},{15,14},{16,17},{19,... | collective-permute-start | bytes 3932168 | tf_op jit(solution)/shard_map/ppermute | solution.py:598
  164.0 10.6 %copy-start.4 = (bf16[4,5,256,128]{3,2,1,0:T(8,128)(2,1)}, bf16[4,5,256,128]{3,2,1,0:T(8,128)(2,1)S(1)}, u32[]{:S(2)}) copy-start(bf16[4,5,256,128]{3,2,1,0:T(8,128)(2,1)S(1)} %collective-permute-done.6.other_next_ref) | copy-start | bytes 3932164
  173.3 59.8 %collective-permute-start.12 = (bf16[4,7,256,128]{3,2,1,0:T(8,128)(2,1)}, bf16[4,7,256,128]{3,2,1,0:T(8,128)(2,1)}, u32[]{:S(2)}, u32[]{:S(2)}) collective-permute-start(bf16[4,7,256,128]{3,2,1,0:T(8,128)(2,1)} %get-tuple-element.121), channel_id=1, source_target_pairs={{1,0},{2,3},{5,4},{6,7},{9,8},{10,11},{13,12},{14,15},{17,16},{18,... | collective-permute-start | bytes 5505032 | tf_op jit(solution)/shard_map/ppermute | solution.py:600
  174.6 46.3 %all-to-all-start = ((bf16[8,4,7,32,128]{4,3,2,1,0:T(8,128)(2,1)}), bf16[8,4,7,32,128]{4,3,2,1,0:T(8,128)(2,1)S(1)}, u32[]{:S(2)}, u32[]{:S(2)}) async-start(bf16[8,4,7,32,128]{4,3,2,1,0:T(8,128)(2,1)} %get-tuple-element.122), calls=%async_computation | async-start | bytes 3670016 | tf_op jit(solution)/shard_map/all_to_all | solution.py:569
  178.4 43.6 %collective-permute-start.9 = (bf16[4,4,256,128]{3,2,1,0:T(8,128)(2,1)}, bf16[4,4,256,128]{3,2,1,0:T(8,128)(2,1)S(1)}, u32[]{:S(2)}, u32[]{:S(2)}) collective-permute-start(bf16[4,4,256,128]{3,2,1,0:T(8,128)(2,1)} %get-tuple-element.125.own_ref), channel_id=1, source_target_pairs={{1,2},{2,1},{5,6},{6,5},{9,10},{10,9},{13,14},{14,13},{17,18},{18,... | collective-permute-start | bytes 3145736 | tf_op jit(solution)/shard_map/ppermute | solution.py:598
  179.1 42.9 %collective-permute-start.10 = (bf16[4,4,256,128]{3,2,1,0:T(8,128)(2,1)}, bf16[4,4,256,128]{3,2,1,0:T(8,128)(2,1)}, u32[]{:S(2)}, u32[]{:S(2)}) collective-permute-start(bf16[4,4,256,128]{3,2,1,0:T(8,128)(2,1)} %get-tuple-element.125.own_ref), channel_id=1, source_target_pairs={{0,2},{3,1},{4,6},{7,5},{8,10},{11,9},{12,14},{15,13},{16,18},{19,... | collective-permute-start | bytes 3145736 | tf_op jit(solution)/shard_map/ppermute | solution.py:598
  188.5 44.6 %collective-permute-start.11 = (bf16[4,4,256,128]{3,2,1,0:T(8,128)(2,1)}, bf16[4,4,256,128]{3,2,1,0:T(8,128)(2,1)}, u32[]{:S(2)}, u32[]{:S(2)}) collective-permute-start(bf16[4,4,256,128]{3,2,1,0:T(8,128)(2,1)} %get-tuple-element.125.own_ref), channel_id=1, source_target_pairs={{0,1},{3,2},{4,5},{7,6},{8,9},{11,10},{12,13},{15,14},{16,17},{19,... | collective-permute-start | bytes 3145736 | tf_op jit(solution)/shard_map/ppermute | solution.py:598
  222.0 12.5 %copy-start.5 = (bf16[4,4,256,128]{3,2,1,0:T(8,128)(2,1)}, bf16[4,4,256,128]{3,2,1,0:T(8,128)(2,1)S(1)}, u32[]{:S(2)}) copy-start(bf16[4,4,256,128]{3,2,1,0:T(8,128)(2,1)S(1)} %collective-permute-done.9.other_next_ref) | copy-start | bytes 3145732
  233.1 32.3 %collective-permute-start.13 = (bf16[4,5,256,128]{3,2,1,0:T(8,128)(2,1)}, bf16[4,5,256,128]{3,2,1,0:T(8,128)(2,1)S(1)}, u32[]{:S(2)}, u32[]{:S(2)}) collective-permute-start(bf16[4,5,256,128]{3,2,1,0:T(8,128)(2,1)} %get-tuple-element.133), channel_id=1, source_target_pairs={{1,0},{2,3},{5,4},{6,7},{9,8},{10,11},{13,12},{14,15},{17,16},{18,... | collective-permute-start | bytes 3932168 | tf_op jit(solution)/shard_map/ppermute | solution.py:600
  234.4 28.6 %all-to-all-start.1 = ((bf16[8,4,5,32,128]{4,3,2,1,0:T(8,128)(2,1)}), bf16[8,4,5,32,128]{4,3,2,1,0:T(8,128)(2,1)S(1)}, u32[]{:S(2)}, u32[]{:S(2)}) async-start(bf16[8,4,5,32,128]{4,3,2,1,0:T(8,128)(2,1)} %get-tuple-element.135), calls=%async_computation.1 | async-start | bytes 2621440 | tf_op jit(solution)/shard_map/all_to_all | solution.py:569
  263.0 7.3 %copy-start.8 = (f32[64]{0:T(128)S(1)}, f32[64]{0:T(128)}, u32[]{:S(2)}) copy-start(f32[64]{0:T(128)} %param.19) | copy-start | bytes 772
  265.4 20.8 %copy-start = (bf16[4,5,256,128]{3,2,1,0:T(8,128)(2,1)}, bf16[4,5,256,128]{3,2,1,0:T(8,128)(2,1)S(1)}, u32[]{:S(2)}) copy-start(bf16[4,5,256,128]{3,2,1,0:T(8,128)(2,1)S(1)} %collective-permute-done.13.refs_10_) | copy-start | bytes 3932164
  265.4 26.5 %collective-permute-start.14 = (bf16[4,4,256,128]{3,2,1,0:T(8,128)(2,1)}, bf16[4,4,256,128]{3,2,1,0:T(8,128)(2,1)S(1)}, u32[]{:S(2)}, u32[]{:S(2)}) collective-permute-start(bf16[4,4,256,128]{3,2,1,0:T(8,128)(2,1)} %get-tuple-element.141), channel_id=1, source_target_pairs={{1,0},{2,3},{5,4},{6,7},{9,8},{10,11},{13,12},{14,15},{17,16},{18,... | collective-permute-start | bytes 3145736 | tf_op jit(solution)/shard_map/ppermute | solution.py:611
  266.7 20.9 %all-to-all-start.2 = ((bf16[8,4,4,32,128]{4,3,2,1,0:T(8,128)(2,1)}), bf16[8,4,4,32,128]{4,3,2,1,0:T(8,128)(2,1)S(1)}, u32[]{:S(2)}, u32[]{:S(2)}) async-start(bf16[8,4,4,32,128]{4,3,2,1,0:T(8,128)(2,1)} %get-tuple-element.142), calls=%async_computation.2 | async-start | bytes 2097152 | tf_op jit(solution)/shard_map/all_to_all | solution.py:569
  271.1 15.1 %copy-start.6 = (bf16[4,7,32,128]{3,2,1,0:T(8,128)(2,1)S(1)}, bf16[4,7,32,128]{3,2,1,0:T(8,128)(2,1)}, u32[]{:S(2)}) copy-start(bf16[4,7,32,128]{3,2,1,0:T(8,128)(2,1)} %reduce_sum.36) | copy-start | bytes 688132
  271.1 15.9 %copy-start.7 = (bf16[4,5,32,128]{3,2,1,0:T(8,128)(2,1)S(1)}, bf16[4,5,32,128]{3,2,1,0:T(8,128)(2,1)}, u32[]{:S(2)}) copy-start(bf16[4,5,32,128]{3,2,1,0:T(8,128)(2,1)} %reduce_sum.37) | copy-start | bytes 491524
  292.0 5.1 %copy-start.1 = (bf16[4,4,256,128]{3,2,1,0:T(8,128)(2,1)}, bf16[4,4,256,128]{3,2,1,0:T(8,128)(2,1)S(1)}, u32[]{:S(2)}) copy-start(bf16[4,4,256,128]{3,2,1,0:T(8,128)(2,1)S(1)} %collective-permute-done.14.refs_11_) | copy-start | bytes 3145732
  293.7 13.4 %collective-permute-start.17 = (bf16[16,32,128]{2,1,0:T(8,128)(2,1)S(1)}, bf16[16,32,128]{2,1,0:T(8,128)(2,1)S(1)}, u32[]{:S(2)}, u32[]{:S(2)}) collective-permute-start(bf16[16,32,128]{2,1,0:T(8,128)(2,1)S(1)} %get-tuple-element.188), channel_id=1, source_target_pairs={{0,3},{1,0},{2,1},{3,2},{4,7},{5,4},{6,5},{7,6},{8,11},{9,8},{10,9... | collective-permute-start | bytes 393224 | tf_op jit(solution)/shard_map/ppermute | solution.py:579
  296.4 10.7 %collective-permute-start.16 = (bf16[16,32,128]{2,1,0:T(8,128)(2,1)S(1)}, bf16[16,32,128]{2,1,0:T(8,128)(2,1)S(1)}, u32[]{:S(2)}, u32[]{:S(2)}) collective-permute-start(bf16[16,32,128]{2,1,0:T(8,128)(2,1)S(1)} %get-tuple-element.189), channel_id=1, source_target_pairs={{0,2},{1,3},{2,0},{3,1},{4,6},{5,7},{6,4},{7,5},{8,10},{9,11},{10,... | collective-permute-start | bytes 393224 | tf_op jit(solution)/shard_map/ppermute | solution.py:579
  296.4 10.7 %collective-permute-start.15 = (bf16[16,32,128]{2,1,0:T(8,128)(2,1)S(1)}, bf16[16,32,128]{2,1,0:T(8,128)(2,1)S(1)}, u32[]{:S(2)}, u32[]{:S(2)}) collective-permute-start(bf16[16,32,128]{2,1,0:T(8,128)(2,1)S(1)} %get-tuple-element.187), channel_id=1, source_target_pairs={{0,1},{1,2},{2,3},{3,0},{4,5},{5,6},{6,7},{7,4},{8,9},{9,10},{10,1... | collective-permute-start | bytes 393224 | tf_op jit(solution)/shard_map/ppermute | solution.py:579
  307.1 6.1 %copy-start.9 = (f32[16]{0:T(128)S(1)}, f32[16]{0:T(128)}, u32[]{:S(2)}) copy-start(f32[16]{0:T(128)} %param.18) | copy-start | bytes 196
  309.4 19.3 %all-to-all-start.3 = ((bf16[8,16,32,128]{3,2,1,0:T(8,128)(2,1)}), bf16[8,16,32,128]{3,2,1,0:T(8,128)(2,1)S(1)}, u32[]{:S(2)}, u32[]{:S(2)}) async-start(bf16[8,16,32,128]{3,2,1,0:T(8,128)(2,1)} %broadcast_in_dim.8), calls=%async_computation.3 | async-start | bytes 2097152 | tf_op jit(solution)/shard_map/all_to_all | solution.py:584
Sparse Core Ops, SparseCore 0:
  26.9 36.9 all-gather.1

commit v7 on v6

--- a/solution.py
+++ b/solution.py
@@ -194,7 +194,7 @@
 LANES = 128
 SHARES = (7, 5, 4)
 STRIP = 16
-EDGE_ROWS = 32
+EDGE_ROWS = 64
 VMEM_BYTES = 60 * 2**20
 
 

time: 340 us -> 341 us (level)
  no operation moved by 1% of the time
where the time goes in v7:
time: 341 us; the launch traced here: 340 us
  Pallas kernels  149 us (44%)
  waiting for transfers between devices  98.9 us (29%)
  starting transfers between devices  62.3 us (18%)
  between operations  14.4 us (4%)
  other arithmetic  8.17 us (2%)
  local copies, waits for them, and re-layouts  7.18 us (2%)
    pallas_call x3, Pallas kernels, block_products(): pl.pallas_call(block_kernel, grid=(filters,), in_specs=[pl.BlockSpec(memo...  96.1 us
    ppermute x3, waiting for transfers between devices, block_shards(): arrivals = [lax.ppermute(own_parts[0], 'ctx', route) for route in routes]  66.5 us
    pallas_call x3, Pallas kernels, leave(): pl.pallas_call(lambda *refs: leave_kernel(bool(received_parts), bool(made...  37.5 us
    ppermute x6, starting transfers between devices, block_shards(): arrivals = [lax.ppermute(leaving, 'ctx', route) for route in routes]  23.7 us
    ppermute x6, waiting for transfers between devices, block_shards(): arrivals = [lax.ppermute(leaving, 'ctx', route) for route in routes]  20.9 us
    pallas_call x2, Pallas kernels, enter(): pl.pallas_call(enter_kernel, grid_spec=pltpu.PrefetchScalarGridSpec(num_s...  15.7 us
    all_to_all x3, starting transfers between devices, lag_shares(): lax.all_to_all(pieces, 'dp', split_axis=0, concat_axis=0, tiled=True)  11.4 us
    ppermute x3, starting transfers between devices, block_shards(): arrivals = [lax.ppermute(own_parts[0], 'ctx', route) for route in routes]  10.3 us
  transfers between devices with their start and end apart: 23, of which 8 were waited for; matrix products, arithmetic and copies ran while one was open for 1% of the time, Pallas kernels for 44%

profile of v7, /device:TPU:0, one launch (start us, length us, event | category | flops | bytes accessed | tf_op | source)
XLA Modules:
  0.0 340.1 jit_solution(18264181487870990263)
XLA Ops:
  7.2 0.7 dynamic-slice_negate_fusion
  8.0 1.4 fusion.4
  9.4 5.1 %collective-permute-start = (bf16[1,2,256,128]{3,2,1,0:T(8,128)(2,1)S(1)}, bf16[1,2,256,128]{3,2,1,0:T(8,128)(2,1)S(1)}, u32[]{:S(2)}, u32[]{:S(2)}) collective-permute-start(bf16[1,2,256,128]{3,2,1,0:T(8,128)(2,1)S(1)} %copy.42), channel_id=1, source_target_pairs={{0,3},{1,0},{2,1},{3,2},{4,7},{5,4},{6,5},{7,6},{8,11},{9,8},{10,9... | collective-permute-start | bytes 393224 | tf_op jit(solution)/shard_map/ppermute | solution.py:560
  14.5 1.0 collective-permute-start.2
  15.5 7.9 %shard_map.164 = (bf16[4,7,256,128]{3,2,1,0:T(8,128)(2,1)}, bf16[4,5,256,128]{3,2,1,0:T(8,128)(2,1)}, bf16[4,4,256,128]{3,2,1,0:T(8,128)(2,1)}) custom-call(s32[1]{0:T(128)} %bitcast.1.first_ref.refs_0_, bf16[64,32768]{1,0:T(8,128)(2,1)} %refs_2_.4, bf16[64,32768]{1,0:T(8,128)(2,1)} %refs_3_.4, bf16[64,32768]{1,0:T(8,128)(2,1)} %refs_4_.4, ...), custom_call_target="tpu_custom_call" | custom-call | flops 4194304 | bytes 12582912 | tf_op jit(solution)/shard_map/pallas_call | solution.py:428
  23.4 2.3 collective-permute-done.1
  25.9 0.8 constant_dynamic-slice_fusion
  26.8 2.0 collective-permute-start.3
  28.8 5.8 %collective-permute-start.4 = (bf16[4,7,256,128]{3,2,1,0:T(8,128)(2,1)S(1)}, bf16[4,7,256,128]{3,2,1,0:T(8,128)(2,1)}, u32[]{:S(2)}, u32[]{:S(2)}) collective-permute-start(bf16[4,7,256,128]{3,2,1,0:T(8,128)(2,1)S(1)} %copy-done.2), channel_id=1, source_target_pairs={{0,2},{3,1},{4,6},{7,5},{8,10},{11,9},{12,14},{15,13},{16,18},{19,... | collective-permute-start | bytes 5505032 | tf_op jit(solution)/shard_map/ppermute | solution.py:564
  34.6 2.5 collective-permute-start.5
  37.1 7.8 %shard_map.165.other_own_ref = bf16[4,16,256,128]{3,2,1,0:T(8,128)(2,1)} custom-call(s32[1]{0:T(128)S(6)} %sub.7.first_ref.refs_0_, bf16[64,32768]{1,0:T(8,128)(2,1)} %refs_2_.4, bf16[64,32768]{1,0:T(8,128)(2,1)} %refs_3_.4, bf16[64,32768]{1,0:T(8,128)(2,1)} %refs_4_.4, bf16[64,32768]{1,0:T(8,128)(2,1)} %refs_5_.4), custom_call_target="tpu_custom_call" | custom-call | flops 4194304 | bytes 12582912 | tf_op jit(solution)/shard_map/pallas_call | solution.py:428
  44.9 28.9 %collective-permute-done.4.other_far_ref = bf16[4,7,256,128]{3,2,1,0:T(8,128)(2,1)} collective-permute-done((bf16[4,7,256,128]{3,2,1,0:T(8,128)(2,1)S(1)}, bf16[4,7,256,128]{3,2,1,0:T(8,128)(2,1)}, u32[]{:S(2)}, u32[]{:S(2)}) %collective-permute-start.4) | collective-permute-done | bytes 1835040 | tf_op jit(solution)/shard_map/ppermute | solution.py:564
  73.8 37.6 %collective-permute-done.5.far_ref = bf16[4,7,256,128]{3,2,1,0:T(8,128)(2,1)} collective-permute-done((bf16[4,7,256,128]{3,2,1,0:T(8,128)(2,1)S(1)}, bf16[4,7,256,128]{3,2,1,0:T(8,128)(2,1)}, u32[]{:S(2)}, u32[]{:S(2)}) %collective-permute-start.5) | collective-permute-done | bytes 1835040 | tf_op jit(solution)/shard_map/ppermute | solution.py:564
  111.4 0.7 collective-permute-start.6
  112.1 8.2 %collective-permute-start.7 = (bf16[4,5,256,128]{3,2,1,0:T(8,128)(2,1)S(1)}, bf16[4,5,256,128]{3,2,1,0:T(8,128)(2,1)}, u32[]{:S(2)}, u32[]{:S(2)}) collective-permute-start(bf16[4,5,256,128]{3,2,1,0:T(8,128)(2,1)S(1)} %copy-done.3), channel_id=1, source_target_pairs={{0,2},{3,1},{4,6},{7,5},{8,10},{11,9},{12,14},{15,13},{16,18},{19,... | collective-permute-start | bytes 3932168 | tf_op jit(solution)/shard_map/ppermute | solution.py:598
  120.3 2.4 collective-permute-start.8
  122.7 41.2 %shard_map.166 = (bf16[4,7,256,128]{3,2,1,0:T(8,128)(2,1)}, bf16[4,7,256,128]{3,2,1,0:T(8,128)(2,1)}, bf16[4,7,256,128]{3,2,1,0:T(8,128)(2,1)}, bf16[8,4,7,32,128]{4,3,2,1,0:T(8,128)(2,1)}) custom-call(f32[1]{0:T(128)} %bitcast.side_ref, bf16[4,7,256,128]{3,2,1,0:T(8,128)(2,1)} %get-tuple-element.104.own_ref, ...), custom_call_target="tpu_custom_call" | custom-call | flops 1 | bytes 1 | tf_op jit(solution)/shard_map/pallas_call | solution.py:379
  163.9 9.7 %collective-permute-done.8.far_ref = bf16[4,5,256,128]{3,2,1,0:T(8,128)(2,1)} collective-permute-done((bf16[4,5,256,128]{3,2,1,0:T(8,128)(2,1)S(1)}, bf16[4,5,256,128]{3,2,1,0:T(8,128)(2,1)}, u32[]{:S(2)}, u32[]{:S(2)}) %collective-permute-start.8) | collective-permute-done | bytes 1310752 | tf_op jit(solution)/shard_map/ppermute | solution.py:598
  173.6 1.3 collective-permute-start.12
  174.9 3.7 %all-to-all-start = ((bf16[8,4,7,32,128]{4,3,2,1,0:T(8,128)(2,1)}), bf16[8,4,7,32,128]{4,3,2,1,0:T(8,128)(2,1)S(1)}, u32[]{:S(2)}, u32[]{:S(2)}) async-start(bf16[8,4,7,32,128]{4,3,2,1,0:T(8,128)(2,1)} %get-tuple-element.122), calls=%async_computation | async-start | bytes 3670016 | tf_op jit(solution)/shard_map/all_to_all | solution.py:569
  178.7 0.7 collective-permute-start.9
  179.4 9.4 %collective-permute-start.10 = (bf16[4,4,256,128]{3,2,1,0:T(8,128)(2,1)}, bf16[4,4,256,128]{3,2,1,0:T(8,128)(2,1)}, u32[]{:S(2)}, u32[]{:S(2)}) collective-permute-start(bf16[4,4,256,128]{3,2,1,0:T(8,128)(2,1)} %get-tuple-element.125.own_ref), channel_id=1, source_target_pairs={{0,2},{3,1},{4,6},{7,5},{8,10},{11,9},{12,14},{15,13},{16,18},{19,... | collective-permute-start | bytes 3145736 | tf_op jit(solution)/shard_map/ppermute | solution.py:598
  188.8 2.3 collective-permute-start.11
  191.0 30.2 %shard_map.167 = (bf16[4,5,256,128]{3,2,1,0:T(8,128)(2,1)}, bf16[4,5,256,128]{3,2,1,0:T(8,128)(2,1)}, bf16[4,5,256,128]{3,2,1,0:T(8,128)(2,1)}, bf16[8,4,5,32,128]{4,3,2,1,0:T(8,128)(2,1)}) custom-call(f32[1]{0:T(128)} %bitcast.side_ref, bf16[4,5,256,128]{3,2,1,0:T(8,128)(2,1)} %get-tuple-element.114.own_ref, ...), custom_call_target="tpu_custom_call" | custom-call | flops 1 | bytes 1 | tf_op jit(solution)/shard_map/pallas_call | solution.py:379
  221.3 1.0 reduce_sum.36
  222.3 11.1 %collective-permute-done.11.far_ref = bf16[4,4,256,128]{3,2,1,0:T(8,128)(2,1)} collective-permute-done((bf16[4,4,256,128]{3,2,1,0:T(8,128)(2,1)}, bf16[4,4,256,128]{3,2,1,0:T(8,128)(2,1)}, u32[]{:S(2)}, u32[]{:S(2)}) %collective-permute-start.11) | collective-permute-done | bytes 1048608 | tf_op jit(solution)/shard_map/ppermute | solution.py:598
  233.4 1.3 collective-permute-start.13
  234.7 3.9 %all-to-all-start.1 = ((bf16[8,4,5,32,128]{4,3,2,1,0:T(8,128)(2,1)}), bf16[8,4,5,32,128]{4,3,2,1,0:T(8,128)(2,1)S(1)}, u32[]{:S(2)}, u32[]{:S(2)}) async-start(bf16[8,4,5,32,128]{4,3,2,1,0:T(8,128)(2,1)} %get-tuple-element.135), calls=%async_computation.1 | async-start | bytes 2621440 | tf_op jit(solution)/shard_map/all_to_all | solution.py:569
  238.6 24.7 %shard_map.168 = (bf16[4,4,256,128]{3,2,1,0:T(8,128)(2,1)}, bf16[4,4,256,128]{3,2,1,0:T(8,128)(2,1)}, bf16[4,4,256,128]{3,2,1,0:T(8,128)(2,1)}, bf16[8,4,4,32,128]{4,3,2,1,0:T(8,128)(2,1)}) custom-call(f32[1]{0:T(128)} %bitcast.side_ref, bf16[4,4,256,128]{3,2,1,0:T(8,128)(2,1)} %get-tuple-element.125.own_ref, ...), custom_call_target="tpu_custom_call" | custom-call | flops 1 | bytes 1 | tf_op jit(solution)/shard_map/pallas_call | solution.py:379
  263.3 0.9 reduce_sum.37
  264.2 1.5 collective-permute-done.13.refs_10_
  265.7 1.3 collective-permute-start.14
  267.0 3.8 %all-to-all-start.2 = ((bf16[8,4,4,32,128]{4,3,2,1,0:T(8,128)(2,1)}), bf16[8,4,4,32,128]{4,3,2,1,0:T(8,128)(2,1)S(1)}, u32[]{:S(2)}, u32[]{:S(2)}) async-start(bf16[8,4,4,32,128]{4,3,2,1,0:T(8,128)(2,1)} %get-tuple-element.142), calls=%async_computation.2 | async-start | bytes 2097152 | tf_op jit(solution)/shard_map/all_to_all | solution.py:569
  270.9 0.7 copy.32.refs_1_
  271.6 14.7 %shard_map.169 = (bf16[64,32768]{1,0:T(8,128)(2,1)}, bf16[64,32768]{1,0:T(8,128)(2,1)}, bf16[64,32768]{1,0:T(8,128)(2,1)}, bf16[64,32768]{1,0:T(8,128)(2,1)}) custom-call(s32[1]{0:T(128)} %bitcast.1.first_ref.refs_0_, f32[64,1]{1,0:T(8,128)} %copy.32.refs_1_, bf16[64,32768]{1,0:T(8,128)(2,1)} %refs_2_.4, bf16[64,32768]{1,0:T(8,128)(2,1)} %refs_3_.4, ...), custom_call_target="tpu_custom_call" | custom-call | flops 16777216 | bytes 29360128 | tf_op jit(solution)/shard_map/pallas_call | solution.py:498
  286.3 0.8 constant_dynamic-update-slice_fusion.9
  287.1 0.7 constant_dynamic-update-slice_fusion.8
  287.9 4.3 %collective-permute-done.14.refs_11_ = bf16[4,4,256,128]{3,2,1,0:T(8,128)(2,1)S(1)} collective-permute-done((bf16[4,4,256,128]{3,2,1,0:T(8,128)(2,1)}, bf16[4,4,256,128]{3,2,1,0:T(8,128)(2,1)S(1)}, u32[]{:S(2)}, u32[]{:S(2)}) %collective-permute-start.14) | collective-permute-done | bytes 1048608 | tf_op jit(solution)/shard_map/ppermute | solution.py:611
  292.2 0.7 constant_dynamic-update-slice_fusion.7
  293.0 1.1 dynamic-slice_bitcast_fusion.2
  294.0 2.4 collective-permute-start.17
  297.1 11.4 %shard_map.170 = (bf16[64,32768]{1,0:T(8,128)(2,1)}, bf16[64,32768]{1,0:T(8,128)(2,1)}, bf16[64,32768]{1,0:T(8,128)(2,1)}, bf16[64,32768]{1,0:T(8,128)(2,1)}) custom-call(s32[1]{0:T(128)S(6)} %sub.7.first_ref.refs_0_, f32[64,1]{1,0:T(8,128)} %copy.32.refs_1_, ...), custom_call_target="tpu_custom_call", output_to_operand_aliasing={{0}: (12, {}), {1}: (13, {}), {2}: (14, {}), {3}: (15, {})} | custom-call | flops 8388608 | bytes 14680064 | tf_op jit(solution)/shard_map/pallas_call | solution.py:498
  308.5 1.0 fusion.3
  309.5 1.2 broadcast_in_dim.8
  310.7 3.9 %all-to-all-start.3 = ((bf16[8,16,32,128]{3,2,1,0:T(8,128)(2,1)}), bf16[8,16,32,128]{3,2,1,0:T(8,128)(2,1)S(1)}, u32[]{:S(2)}, u32[]{:S(2)}) async-start(bf16[8,16,32,128]{3,2,1,0:T(8,128)(2,1)} %broadcast_in_dim.8), calls=%async_computation.3 | async-start | bytes 2097152 | tf_op jit(solution)/shard_map/all_to_all | solution.py:584
  315.3 11.4 %shard_map.171 = (bf16[64,32768]{1,0:T(8,128)(2,1)}, bf16[64,32768]{1,0:T(8,128)(2,1)}, bf16[64,32768]{1,0:T(8,128)(2,1)}, bf16[64,32768]{1,0:T(8,128)(2,1)}) custom-call(s32[1]{0:T(128)S(6)} %sub.7.first_ref.refs_0_, f32[64,1]{1,0:T(8,128)} %copy.34.refs_1_, ...), custom_call_target="tpu_custom_call", output_to_operand_aliasing={{0}: (12, {}), {1}: (13, {}), {2}: (14, {}), {3}: (15, {})} | custom-call | flops 8388608 | bytes 14680064 | tf_op jit(solution)/shard_map/pallas_call | solution.py:498
  326.6 3.3 all-to-all-done.3
  330.5 2.7 fusion
  (54 shorter events, 2.3 us)
Async XLA Ops:
  7.2 115.5 %all-gather.2.cloned.1.call-start = ((), (), s32[]{:S(2)}) async-start(), calls=%async_computation.4 | async-start | bytes 4718592 | tf_op jit(solution)/shard_map/all_gather | solution.py:565
  9.4 14.0 %collective-permute-start = (bf16[1,2,256,128]{3,2,1,0:T(8,128)(2,1)S(1)}, bf16[1,2,256,128]{3,2,1,0:T(8,128)(2,1)S(1)}, u32[]{:S(2)}, u32[]{:S(2)}) collective-permute-start(bf16[1,2,256,128]{3,2,1,0:T(8,128)(2,1)S(1)} %copy.42), channel_id=1, source_target_pairs={{0,3},{1,0},{2,1},{3,2},{4,7},{5,4},{6,5},{7,6},{8,11},{9,8},{10,9... | collective-permute-start | bytes 393224 | tf_op jit(solution)/shard_map/ppermute | solution.py:560
  14.5 11.2 %collective-permute-start.1 = (bf16[1,2,256,128]{3,2,1,0:T(8,128)(2,1)S(1)}, bf16[1,2,256,128]{3,2,1,0:T(8,128)(2,1)S(1)}, u32[]{:S(2)}, u32[]{:S(2)}) collective-permute-start(bf16[1,2,256,128]{3,2,1,0:T(8,128)(2,1)S(1)} %copy.42), channel_id=1, source_target_pairs={{0,2},{1,3},{2,0},{3,1},{4,6},{5,7},{6,4},{7,5},{8,10},{9,11},{10,... | collective-permute-start | bytes 393224 | tf_op jit(solution)/shard_map/ppermute | solution.py:560
  14.5 11.2 %collective-permute-start.2 = (bf16[1,2,256,128]{3,2,1,0:T(8,128)(2,1)S(1)}, bf16[1,2,256,128]{3,2,1,0:T(8,128)(2,1)S(1)}, u32[]{:S(2)}, u32[]{:S(2)}) collective-permute-start(bf16[1,2,256,128]{3,2,1,0:T(8,128)(2,1)S(1)} %copy.42), channel_id=1, source_target_pairs={{0,1},{1,2},{2,3},{3,0},{4,5},{5,6},{6,7},{7,4},{8,9},{9,10},{10,1... | collective-permute-start | bytes 393224 | tf_op jit(solution)/shard_map/ppermute | solution.py:560
  23.4 3.4 copy-start.2
  26.8 84.6 %copy-start.3 = (bf16[4,5,256,128]{3,2,1,0:T(8,128)(2,1)S(1)}, bf16[4,5,256,128]{3,2,1,0:T(8,128)(2,1)}, u32[]{:S(2)}) copy-start(bf16[4,5,256,128]{3,2,1,0:T(8,128)(2,1)} %get-tuple-element.114.own_ref) | copy-start | bytes 3932164
  26.8 18.1 %collective-permute-start.3 = (bf16[4,7,256,128]{3,2,1,0:T(8,128)(2,1)S(1)}, bf16[4,7,256,128]{3,2,1,0:T(8,128)(2,1)}, u32[]{:S(2)}, u32[]{:S(2)}) collective-permute-start(bf16[4,7,256,128]{3,2,1,0:T(8,128)(2,1)S(1)} %copy-done.2), channel_id=1, source_target_pairs={{1,2},{2,1},{5,6},{6,5},{9,10},{10,9},{13,14},{14,13},{17,18},{18,... | collective-permute-start | bytes 5505032 | tf_op jit(solution)/shard_map/ppermute | solution.py:564
  28.8 45.0 %collective-permute-start.4 = (bf16[4,7,256,128]{3,2,1,0:T(8,128)(2,1)S(1)}, bf16[4,7,256,128]{3,2,1,0:T(8,128)(2,1)}, u32[]{:S(2)}, u32[]{:S(2)}) collective-permute-start(bf16[4,7,256,128]{3,2,1,0:T(8,128)(2,1)S(1)} %copy-done.2), channel_id=1, source_target_pairs={{0,2},{3,1},{4,6},{7,5},{8,10},{11,9},{12,14},{15,13},{16,18},{19,... | collective-permute-start | bytes 5505032 | tf_op jit(solution)/shard_map/ppermute | solution.py:564
  34.6 76.8 %collective-permute-start.5 = (bf16[4,7,256,128]{3,2,1,0:T(8,128)(2,1)S(1)}, bf16[4,7,256,128]{3,2,1,0:T(8,128)(2,1)}, u32[]{:S(2)}, u32[]{:S(2)}) collective-permute-start(bf16[4,7,256,128]{3,2,1,0:T(8,128)(2,1)S(1)} %copy-done.2), channel_id=1, source_target_pairs={{0,1},{3,2},{4,5},{7,6},{8,9},{11,10},{12,13},{15,14},{16,17},{19,... | collective-permute-start | bytes 5505032 | tf_op jit(solution)/shard_map/ppermute | solution.py:564
  111.4 52.5 %collective-permute-start.6 = (bf16[4,5,256,128]{3,2,1,0:T(8,128)(2,1)S(1)}, bf16[4,5,256,128]{3,2,1,0:T(8,128)(2,1)S(1)}, u32[]{:S(2)}, u32[]{:S(2)}) collective-permute-start(bf16[4,5,256,128]{3,2,1,0:T(8,128)(2,1)S(1)} %copy-done.3), channel_id=1, source_target_pairs={{1,2},{2,1},{5,6},{6,5},{9,10},{10,9},{13,14},{14,13},{17,18},{18,... | collective-permute-start | bytes 3932168 | tf_op jit(solution)/shard_map/ppermute | solution.py:598
  112.1 51.8 %collective-permute-start.7 = (bf16[4,5,256,128]{3,2,1,0:T(8,128)(2,1)S(1)}, bf16[4,5,256,128]{3,2,1,0:T(8,128)(2,1)}, u32[]{:S(2)}, u32[]{:S(2)}) collective-permute-start(bf16[4,5,256,128]{3,2,1,0:T(8,128)(2,1)S(1)} %copy-done.3), channel_id=1, source_target_pairs={{0,2},{3,1},{4,6},{7,5},{8,10},{11,9},{12,14},{15,13},{16,18},{19,... | collective-permute-start | bytes 3932168 | tf_op jit(solution)/shard_map/ppermute | solution.py:598
  120.3 53.3 %collective-permute-start.8 = (bf16[4,5,256,128]{3,2,1,0:T(8,128)(2,1)S(1)}, bf16[4,5,256,128]{3,2,1,0:T(8,128)(2,1)}, u32[]{:S(2)}, u32[]{:S(2)}) collective-permute-start(bf16[4,5,256,128]{3,2,1,0:T(8,128)(2,1)S(1)} %copy-done.3), channel_id=1, source_target_pairs={{0,1},{3,2},{4,5},{7,6},{8,9},{11,10},{12,13},{15,14},{16,17},{19,... | collective-permute-start | bytes 3932168 | tf_op jit(solution)/shard_map/ppermute | solution.py:598
  163.9 11.1 %copy-start.4 = (bf16[4,5,256,128]{3,2,1,0:T(8,128)(2,1)}, bf16[4,5,256,128]{3,2,1,0:T(8,128)(2,1)S(1)}, u32[]{:S(2)}) copy-start(bf16[4,5,256,128]{3,2,1,0:T(8,128)(2,1)S(1)} %collective-permute-done.6.other_next_ref) | copy-start | bytes 3932164
  173.6 59.8 %collective-permute-start.12 = (bf16[4,7,256,128]{3,2,1,0:T(8,128)(2,1)}, bf16[4,7,256,128]{3,2,1,0:T(8,128)(2,1)}, u32[]{:S(2)}, u32[]{:S(2)}) collective-permute-start(bf16[4,7,256,128]{3,2,1,0:T(8,128)(2,1)} %get-tuple-element.121), channel_id=1, source_target_pairs={{1,0},{2,3},{5,4},{6,7},{9,8},{10,11},{13,12},{14,15},{17,16},{18,... | collective-permute-start | bytes 5505032 | tf_op jit(solution)/shard_map/ppermute | solution.py:600
  174.9 46.3 %all-to-all-start = ((bf16[8,4,7,32,128]{4,3,2,1,0:T(8,128)(2,1)}), bf16[8,4,7,32,128]{4,3,2,1,0:T(8,128)(2,1)S(1)}, u32[]{:S(2)}, u32[]{:S(2)}) async-start(bf16[8,4,7,32,128]{4,3,2,1,0:T(8,128)(2,1)} %get-tuple-element.122), calls=%async_computation | async-start | bytes 3670016 | tf_op jit(solution)/shard_map/all_to_all | solution.py:569
  178.7 43.6 %collective-permute-start.9 = (bf16[4,4,256,128]{3,2,1,0:T(8,128)(2,1)}, bf16[4,4,256,128]{3,2,1,0:T(8,128)(2,1)S(1)}, u32[]{:S(2)}, u32[]{:S(2)}) collective-permute-start(bf16[4,4,256,128]{3,2,1,0:T(8,128)(2,1)} %get-tuple-element.125.own_ref), channel_id=1, source_target_pairs={{1,2},{2,1},{5,6},{6,5},{9,10},{10,9},{13,14},{14,13},{17,18},{18,... | collective-permute-start | bytes 3145736 | tf_op jit(solution)/shard_map/ppermute | solution.py:598
  179.4 42.9 %collective-permute-start.10 = (bf16[4,4,256,128]{3,2,1,0:T(8,128)(2,1)}, bf16[4,4,256,128]{3,2,1,0:T(8,128)(2,1)}, u32[]{:S(2)}, u32[]{:S(2)}) collective-permute-start(bf16[4,4,256,128]{3,2,1,0:T(8,128)(2,1)} %get-tuple-element.125.own_ref), channel_id=1, source_target_pairs={{0,2},{3,1},{4,6},{7,5},{8,10},{11,9},{12,14},{15,13},{16,18},{19,... | collective-permute-start | bytes 3145736 | tf_op jit(solution)/shard_map/ppermute | solution.py:598
  188.8 44.6 %collective-permute-start.11 = (bf16[4,4,256,128]{3,2,1,0:T(8,128)(2,1)}, bf16[4,4,256,128]{3,2,1,0:T(8,128)(2,1)}, u32[]{:S(2)}, u32[]{:S(2)}) collective-permute-start(bf16[4,4,256,128]{3,2,1,0:T(8,128)(2,1)} %get-tuple-element.125.own_ref), channel_id=1, source_target_pairs={{0,1},{3,2},{4,5},{7,6},{8,9},{11,10},{12,13},{15,14},{16,17},{19,... | collective-permute-start | bytes 3145736 | tf_op jit(solution)/shard_map/ppermute | solution.py:598
  222.3 12.4 %copy-start.5 = (bf16[4,4,256,128]{3,2,1,0:T(8,128)(2,1)}, bf16[4,4,256,128]{3,2,1,0:T(8,128)(2,1)S(1)}, u32[]{:S(2)}) copy-start(bf16[4,4,256,128]{3,2,1,0:T(8,128)(2,1)S(1)} %collective-permute-done.9.other_next_ref) | copy-start | bytes 3145732
  233.4 32.3 %collective-permute-start.13 = (bf16[4,5,256,128]{3,2,1,0:T(8,128)(2,1)}, bf16[4,5,256,128]{3,2,1,0:T(8,128)(2,1)S(1)}, u32[]{:S(2)}, u32[]{:S(2)}) collective-permute-start(bf16[4,5,256,128]{3,2,1,0:T(8,128)(2,1)} %get-tuple-element.133), channel_id=1, source_target_pairs={{1,0},{2,3},{5,4},{6,7},{9,8},{10,11},{13,12},{14,15},{17,16},{18,... | collective-permute-start | bytes 3932168 | tf_op jit(solution)/shard_map/ppermute | solution.py:600
  234.7 28.6 %all-to-all-start.1 = ((bf16[8,4,5,32,128]{4,3,2,1,0:T(8,128)(2,1)}), bf16[8,4,5,32,128]{4,3,2,1,0:T(8,128)(2,1)S(1)}, u32[]{:S(2)}, u32[]{:S(2)}) async-start(bf16[8,4,5,32,128]{4,3,2,1,0:T(8,128)(2,1)} %get-tuple-element.135), calls=%async_computation.1 | async-start | bytes 2621440 | tf_op jit(solution)/shard_map/all_to_all | solution.py:569
  263.3 7.5 %copy-start.8 = (f32[64]{0:T(128)S(1)}, f32[64]{0:T(128)}, u32[]{:S(2)}) copy-start(f32[64]{0:T(128)} %param.19) | copy-start | bytes 772
  265.7 20.6 %copy-start = (bf16[4,5,256,128]{3,2,1,0:T(8,128)(2,1)}, bf16[4,5,256,128]{3,2,1,0:T(8,128)(2,1)S(1)}, u32[]{:S(2)}) copy-start(bf16[4,5,256,128]{3,2,1,0:T(8,128)(2,1)S(1)} %collective-permute-done.13.refs_10_) | copy-start | bytes 3932164
  265.7 26.5 %collective-permute-start.14 = (bf16[4,4,256,128]{3,2,1,0:T(8,128)(2,1)}, bf16[4,4,256,128]{3,2,1,0:T(8,128)(2,1)S(1)}, u32[]{:S(2)}, u32[]{:S(2)}) collective-permute-start(bf16[4,4,256,128]{3,2,1,0:T(8,128)(2,1)} %get-tuple-element.141), channel_id=1, source_target_pairs={{1,0},{2,3},{5,4},{6,7},{9,8},{10,11},{13,12},{14,15},{17,16},{18,... | collective-permute-start | bytes 3145736 | tf_op jit(solution)/shard_map/ppermute | solution.py:611
  267.0 20.8 %all-to-all-start.2 = ((bf16[8,4,4,32,128]{4,3,2,1,0:T(8,128)(2,1)}), bf16[8,4,4,32,128]{4,3,2,1,0:T(8,128)(2,1)S(1)}, u32[]{:S(2)}, u32[]{:S(2)}) async-start(bf16[8,4,4,32,128]{4,3,2,1,0:T(8,128)(2,1)} %get-tuple-element.142), calls=%async_computation.2 | async-start | bytes 2097152 | tf_op jit(solution)/shard_map/all_to_all | solution.py:569
  271.6 14.7 %copy-start.6 = (bf16[4,7,32,128]{3,2,1,0:T(8,128)(2,1)S(1)}, bf16[4,7,32,128]{3,2,1,0:T(8,128)(2,1)}, u32[]{:S(2)}) copy-start(bf16[4,7,32,128]{3,2,1,0:T(8,128)(2,1)} %reduce_sum.36) | copy-start | bytes 688132
  271.6 15.5 %copy-start.7 = (bf16[4,5,32,128]{3,2,1,0:T(8,128)(2,1)S(1)}, bf16[4,5,32,128]{3,2,1,0:T(8,128)(2,1)}, u32[]{:S(2)}) copy-start(bf16[4,5,32,128]{3,2,1,0:T(8,128)(2,1)} %reduce_sum.37) | copy-start | bytes 491524
  292.2 4.8 %copy-start.1 = (bf16[4,4,256,128]{3,2,1,0:T(8,128)(2,1)}, bf16[4,4,256,128]{3,2,1,0:T(8,128)(2,1)S(1)}, u32[]{:S(2)}) copy-start(bf16[4,4,256,128]{3,2,1,0:T(8,128)(2,1)S(1)} %collective-permute-done.14.refs_11_) | copy-start | bytes 3145732
  294.0 14.4 %collective-permute-start.17 = (bf16[16,32,128]{2,1,0:T(8,128)(2,1)S(1)}, bf16[16,32,128]{2,1,0:T(8,128)(2,1)S(1)}, u32[]{:S(2)}, u32[]{:S(2)}) collective-permute-start(bf16[16,32,128]{2,1,0:T(8,128)(2,1)S(1)} %get-tuple-element.188), channel_id=1, source_target_pairs={{0,3},{1,0},{2,1},{3,2},{4,7},{5,4},{6,5},{7,6},{8,11},{9,8},{10,9... | collective-permute-start | bytes 393224 | tf_op jit(solution)/shard_map/ppermute | solution.py:579
  296.4 12.0 %collective-permute-start.16 = (bf16[16,32,128]{2,1,0:T(8,128)(2,1)S(1)}, bf16[16,32,128]{2,1,0:T(8,128)(2,1)S(1)}, u32[]{:S(2)}, u32[]{:S(2)}) collective-permute-start(bf16[16,32,128]{2,1,0:T(8,128)(2,1)S(1)} %get-tuple-element.189), channel_id=1, source_target_pairs={{0,2},{1,3},{2,0},{3,1},{4,6},{5,7},{6,4},{7,5},{8,10},{9,11},{10,... | collective-permute-start | bytes 393224 | tf_op jit(solution)/shard_map/ppermute | solution.py:579
  296.4 12.0 %collective-permute-start.15 = (bf16[16,32,128]{2,1,0:T(8,128)(2,1)S(1)}, bf16[16,32,128]{2,1,0:T(8,128)(2,1)S(1)}, u32[]{:S(2)}, u32[]{:S(2)}) collective-permute-start(bf16[16,32,128]{2,1,0:T(8,128)(2,1)S(1)} %get-tuple-element.187), channel_id=1, source_target_pairs={{0,1},{1,2},{2,3},{3,0},{4,5},{5,6},{6,7},{7,4},{8,9},{9,10},{10,1... | collective-permute-start | bytes 393224 | tf_op jit(solution)/shard_map/ppermute | solution.py:579
  308.4 6.1 %copy-start.9 = (f32[16]{0:T(128)S(1)}, f32[16]{0:T(128)}, u32[]{:S(2)}) copy-start(f32[16]{0:T(128)} %param.18) | copy-start | bytes 196
  310.7 19.3 %all-to-all-start.3 = ((bf16[8,16,32,128]{3,2,1,0:T(8,128)(2,1)}), bf16[8,16,32,128]{3,2,1,0:T(8,128)(2,1)S(1)}, u32[]{:S(2)}, u32[]{:S(2)}) async-start(bf16[8,16,32,128]{3,2,1,0:T(8,128)(2,1)} %broadcast_in_dim.8), calls=%async_computation.3 | async-start | bytes 2097152 | tf_op jit(solution)/shard_map/all_to_all | solution.py:584
Sparse Core Ops, SparseCore 0:
  26.9 36.9 all-gather.1
